TPU v7x, 32 devices: a whole 2x2x4 slice. The times are simulated.
32 devices in a mesh: row: 8 (over z, x), col: 4 (over y, core).
Axes of the slice: x: 2, y: 2, z: 4, core: 2. Of those that a mesh axis runs over, the one named last changes fastest.
Arguments:
- rhs: float32 [32, 64, 128], P(('row', 'col')), may hold values from -16 to 16
- item_factors: bfloat16 [256, 64, 128], P('col'), may hold values from -0.125 to 0.125
- slot_users: int32 [8, 4, 96], P('row', 'col'), may hold values from 0 to 3, as said below
- slot_items: int32 [8, 4, 96], P('row', 'col'), may hold values from 0 to 63
- slot_counts: int32 [8, 4], P('row', 'col'), may hold values from 12 to 96, as said below
- mask_words: int32 [8, 4, 96, 16, 128], P('row', 'col'), may hold values from 0 to 255
- self_tiles: int32 [32, 128, 128], P(('row', 'col')), may hold values from 0 to 3, as said below
- next_tiles: int32 [32, 128, 128], P(('row', 'col')), may hold values from 0 to 3, as said below
Outputs:
- solution: float32 [32, 64, 128], P(('row', 'col'))
- residual: float32 [32, 64, 128], P(('row', 'col'))
Inputs may be any that keep to these rules, and one draw needn't show every extreme that they name: `slot_users`: on each grid cell the 96 slots name distinct pairs of user block and item block. Some grid cells use all 96 slots; slots at positions slot_counts or later are ignored. `self_tiles`: most weights are zero. `next_tiles`: most weights are zero.
All inputs are finite; a program needn't handle non-finite values.
Results may differ from a plain program's by a relative error of at most 0.018.
Values may be sent and summed in bfloat16 or wider, within the bound.
No kernel may reach another device: no remote copies, remote signals or barrier semaphores. Data moves between devices by JAX's collectives and lax.ppermute only.
A program may use at most 64 MiB of HBM per device.

v0:
```python
import jax
import jax.numpy as jnp
from jax import lax
from jax.sharding import PartitionSpec as P

ITERS = 2


graph_weight = 0.01
ridge_weight = 0.5


def group_size():
    return 16


def unpack_masks(words):
    shifts = jnp.arange(8, dtype=jnp.int32)
    bits = jnp.right_shift(words[:, :, None, :], shifts[None, None, :, None]) & 1
    return bits.reshape(words.shape[0], words.shape[1] * 8, words.shape[2]).astype(jnp.float32)


def masked_tiles(row_dir, item_factors, users, items, words, valid):
    scores = jnp.einsum(
        "sdi,sdu->siu", item_factors[items], row_dir[users], preferred_element_type=jnp.float32
    )
    return (scores * unpack_masks(words) * valid[:, None, None]).astype(jnp.bfloat16)


def second_half(tiles, item_factors, items):
    return jnp.einsum(
        "siu,sdi->sdu", tiles, item_factors[items], preferred_element_type=jnp.float32
    )


def own_slots(partial_value, row_dir, item_factors, users, items, words, limit):
    group = group_size()
    trips = (limit + group - 1) // group

    def turn(index, acc):
        start = index * group
        part_users = lax.dynamic_slice_in_dim(users, start, group)
        part_items = lax.dynamic_slice_in_dim(items, start, group)
        part_words = lax.dynamic_slice_in_dim(words, start, group)
        valid = (start + jnp.arange(group, dtype=jnp.int32) < limit).astype(jnp.float32)
        tiles = masked_tiles(row_dir, item_factors, part_users, part_items, part_words, valid)
        return acc.at[part_users].add(second_half(tiles, item_factors, part_items))

    return lax.fori_loop(0, trips, turn, partial_value)


def graph_terms(partial_value, row_dir, self_tiles, next_tiles, first_local):
    row_blocks = row_dir.shape[0]
    local = first_local + jnp.arange(self_tiles.shape[0], dtype=jnp.int32)
    after = jnp.minimum(local + 1, row_blocks - 1)
    keep = (local < row_blocks - 1).astype(jnp.int32)
    own = row_dir[local]
    following = row_dir[after]
    sym_weights = self_tiles + jnp.swapaxes(self_tiles, 1, 2)
    edge_weights = next_tiles * keep[:, None, None]
    degree = jnp.sum(sym_weights, axis=2).astype(jnp.float32) + jnp.sum(
        edge_weights, axis=2
    ).astype(jnp.float32)
    column_degree = jnp.sum(edge_weights, axis=1).astype(jnp.float32)
    sym = sym_weights.astype(jnp.bfloat16)
    edges = edge_weights.astype(jnp.bfloat16)
    here = degree[:, None, :] * own.astype(jnp.float32) - jnp.einsum(
        "buv,bdv->bdu", sym, own, preferred_element_type=jnp.float32
    )
    here = here - jnp.einsum("buv,bdv->bdu", edges, following, preferred_element_type=jnp.float32)
    there = column_degree[:, None, :] * following.astype(jnp.float32) - jnp.einsum(
        "buv,bdu->bdv", edges, own, preferred_element_type=jnp.float32
    )
    partial_value = partial_value.at[local].add(graph_weight * here)
    return partial_value.at[after].add(graph_weight * there)


def per_device(
    rhs, item_factors, slot_users, slot_items, slot_counts, mask_words, self_tiles, next_tiles
):
    users = slot_users[0, 0]
    items = slot_items[0, 0]
    words = mask_words[0, 0]
    count = slot_counts[0, 0]
    count_dev = self_tiles.shape[0]
    first_local = lax.axis_index("col") * count_dev

    def share(vector):
        return lax.dynamic_slice_in_dim(vector, first_local, count_dev, 0)

    start = lax.all_gather(rhs, "col", axis=0, tiled=True)
    solution = jnp.zeros_like(start)
    residual = start
    direction = start
    mine = share(residual)
    norm_now = lax.psum(jnp.sum(mine * mine), ("row", "col"))
    for iteration in range(ITERS):
        row_dir = direction.astype(jnp.bfloat16)
        partial_value = jnp.zeros(row_dir.shape, jnp.float32)
        partial_value = own_slots(partial_value, row_dir, item_factors, users, items, words, count)
        apply_partial_value = graph_terms(
            partial_value, row_dir, self_tiles, next_tiles, first_local
        )
        image = lax.psum(apply_partial_value, "col") + ridge_weight * direction
        image_share = share(image)
        curve, cross, square = lax.psum(
            (
                jnp.sum(share(direction) * image_share),
                jnp.sum(share(residual) * image_share),
                jnp.sum(image_share * image_share),
            ),
            ("row", "col"),
        )
        alpha = norm_now / curve
        solution = solution + alpha * direction
        residual = residual - alpha * image
        norm_next = norm_now - 2.0 * alpha * cross + alpha * alpha * square
        direction = residual + norm_next / norm_now * direction
        norm_now = norm_next
    return (share(solution), share(residual))


def solution(mesh):
    return jax.shard_map(
        per_device,
        mesh=mesh,
        in_specs=(
            P(("row", "col"), None, None),
            P("col", None, None),
            P("row", "col", None),
            P("row", "col", None),
            P("row", "col"),
            P("row", "col", None, None, None),
            P(("row", "col"), None, None),
            P(("row", "col"), None, None),
        ),
        out_specs=(P(("row", "col"), None, None), P(("row", "col"), None, None)),
        check_vma=False,
    )
```

profile of v0, /device:TPU:0, one launch (start us, length us, event | category | flops | bytes accessed | tf_op | source)
XLA Modules:
  0.0 255.3 jit_solution(7115297098338548619)
XLA Ops:
  7.2 0.0 all-reduce.4.cloned.1.call-start
  7.9 1.0 copy.12
  8.9 0.1 multiply_reduce_fusion
  9.1 0.6 copy-done.7
  9.7 6.5 %all_gather.3 = f32[4,64,128]{2,1,0:T(8,128)S(1)} all-gather(f32[1,64,128]{2,1,0:T(8,128)S(1)} %copy-done.7), channel_id=1, replica_groups=mesh['row'=8,'col'=4] {'col'}, dimensions={0}, use_global_device_ids=true | all-gather | bytes 163840 | tf_op jit(solution)/shard_map/all_gather | solution.py:91
  16.2 0.6 copy-done.5
  16.9 0.0 copy-done.6
  16.9 12.3 %while.28 = (s32[]{:T(128)}, f32[4,64,128]{2,1,0:T(8,128)S(1)}, s32[]{:T(128)}, s32[96]{0:T(128)S(1)}, s32[96]{0:T(128)S(1)}, /*index=5*/bf16[64,64,128]{2,1,0:T...) while((s32[]{:T(128)}, f32[4,64,128]{2,1,0:T(8,128)S(1)}, ...), condition=%wide.region_4.5_spmd, body=%wide.region_2.4_spmd.sunk | while | flops 68815000 | bytes 4074363 | solution.py:49
  16.9 0.6 compare_convert_fusion.4
  17.5 0.1 compare_select_fusion.6
  17.6 0.1 shift_right_arithmetic.86
  17.7 0.9 constant_dynamic-slice_fusion.4
  18.6 0.6 gather_fusion.1
  19.3 1.8 gather_fusion
  21.1 0.6 fusion.87
  21.6 1.4 scatter_fusion
  23.0 0.7 compare_convert_fusion.4
  23.7 0.1 compare_select_fusion.6
  23.8 0.1 shift_right_arithmetic.86
  23.9 0.9 constant_dynamic-slice_fusion.4
  24.8 0.6 gather_fusion.1
  25.4 1.8 gather_fusion
  27.2 0.6 fusion.87
  27.8 1.4 scatter_fusion
  29.2 0.6 copy-done.8
  29.8 0.7 and_reduce_fusion
  30.6 0.1 convolution_subtract_fusion.5
  30.7 0.7 fusion.32
  31.4 0.8 fusion.35
  32.2 0.7 copy-done.1
  32.8 0.0 all-reduce.4.cloned.1.call-update
  32.9 0.0 all-reduce.6.cloned.1.call-start
  32.9 56.8 %all-reduce.4.cloned.1.call-done = f32[4,64,128]{2,1,0:T(8,128)} async-done(((f32[4,64,128]{2,1,0:T(8,128)}), f32[4,64,128]{2,1,0:T(8,128)}) %all-reduce.4.cloned.1.call-update) | async-done | bytes 131088 | tf_op jit(solution)/shard_map/psum | solution.py:104
  89.7 1.0 multiply_add_fusion.2
  90.7 0.7 multiply_reduce_fusion.3
  91.4 39.6 %all-reduce = (f32[]{:T(128)}, f32[]{:T(128)}, f32[]{:T(128)}) all-reduce(f32[]{:T(128)} %get-tuple-element.194, f32[]{:T(128)} %get-tuple-element.193, f32[]{:T(128)} %get-tuple-element.192), channel_id=1, replica_groups=mesh['row'=8,'col'=4] {'row','col'}, use_global_device_ids=true, to_apply=%region_1.0 | all-reduce | flops 3 | bytes 24 | tf_op jit(solution)/shard_map/psum | solution.py:96
  134.9 0.1 convolution_subtract_fusion.2
  135.1 12.3 %while.29 = (s32[]{:T(128)}, f32[4,64,128]{2,1,0:T(8,128)S(1)}, s32[]{:T(128)}, s32[96]{0:T(128)S(1)}, s32[96]{0:T(128)S(1)}, /*index=5*/bf16[64,64,128]{2,1,0:T...) while((s32[]{:T(128)}, f32[4,64,128]{2,1,0:T(8,128)S(1)}, ...), condition=%wide.region_17.18_spmd, body=%wide.region_15.17_spmd.sunk | while | flops 68815000 | bytes 4074363 | solution.py:49
  135.1 0.7 compare_convert_fusion.5
  135.8 0.1 compare_select_fusion.7
  135.9 0.1 shift_right_arithmetic.91
  136.0 0.9 constant_dynamic-slice_fusion.5
  136.9 0.6 gather_fusion.3
  137.5 1.8 gather_fusion.2
  139.4 0.6 fusion.91
  139.9 1.4 scatter_fusion.1
  141.3 0.7 compare_convert_fusion.5
  142.0 0.1 compare_select_fusion.7
  142.1 0.1 shift_right_arithmetic.91
  142.1 0.9 constant_dynamic-slice_fusion.5
  143.1 0.6 gather_fusion.3
  143.7 1.8 gather_fusion.2
  145.5 0.6 fusion.91
  146.1 1.4 scatter_fusion.1
  147.4 0.7 fusion.38
  148.1 0.8 fusion.41
  148.9 0.7 copy-done
  149.6 0.0 all-reduce.6.cloned.1.call-update
  149.6 55.9 %all-reduce.6.cloned.1.call-done = f32[4,64,128]{2,1,0:T(8,128)} async-done(((f32[4,64,128]{2,1,0:T(8,128)}), f32[4,64,128]{2,1,0:T(8,128)}) %all-reduce.6.cloned.1.call-update) | async-done | bytes 131088 | tf_op jit(solution)/shard_map/psum | solution.py:104
  205.5 0.9 multiply_add_fusion
  206.4 0.6 multiply_reduce_fusion.2
  207.0 39.5 %psum.50 = f32[]{:T(128)} all-reduce(f32[]{:T(128)} %multiply_reduce_fusion.2), channel_id=1, replica_groups=mesh['row'=8,'col'=4] {'row','col'}, use_global_device_ids=true, to_apply=%region_20.21 | all-reduce | flops 1 | bytes 8 | tf_op jit(solution)/shard_map/psum | solution.py:106
  247.2 0.6 multiply_add_fusion.3
  247.9 0.6 dynamic-slice_subtract_fusion
  (30 shorter events, 0.2 us)
Async XLA Ops:
  7.2 82.6 %all-reduce.4.cloned.1.call-start = ((), (), s32[]{:S(2)}) async-start(), calls=%async_computation | async-start | bytes 262144 | tf_op jit(solution)/shard_map/psum | solution.py:104
  7.9 1.0 copy-start.3
  7.9 1.0 copy-start.4
  8.9 0.8 copy-start.7
  16.2 0.7 copy-start.5
  16.2 0.7 copy-start.6
  29.2 0.7 copy-start.8
  32.2 0.7 copy-start.1
  32.9 172.6 %all-reduce.6.cloned.1.call-start = ((), (), s32[]{:S(2)}) async-start(), calls=%async_computation.1 | async-start | bytes 262144 | tf_op jit(solution)/shard_map/psum | solution.py:104
  89.7 45.2 %copy-start.2 = (f32[4,64,128]{2,1,0:T(8,128)S(1)}, f32[4,64,128]{2,1,0:T(8,128)}, u32[]{:S(2)}) copy-start(f32[4,64,128]{2,1,0:T(8,128)} %all-reduce.4.cloned.1.call-done) | copy-start | bytes 393220
  148.9 0.7 copy-start
Sparse Core Ops, SparseCore 0:
  33.0 56.6 all-reduce.3
  149.7 55.7 all-reduce.5
where the time goes:
time: 257 us; the launch traced here: 255 us
  waiting for transfers between devices  113 us (44%)
  blocking collectives  85.6 us (33%)
  between operations  19.4 us (8%)
  local copies, waits for them, and re-layouts  18 us (7%)
  other arithmetic  13.7 us (5%)
  matrix products  5.47 us (2%)
    psum x2, waiting for transfers between devices, per_device(): image = lax.psum(apply_partial_value, 'col') + ridge_weight * direction  113 us
    psum x1, blocking collectives, per_device(): norm_now = lax.psum(jnp.sum(mine * mine), ('row', 'col'))  39.6 us
    psum x1, blocking collectives, per_device(): lax.psum((jnp.sum(share(direction) * image_share), jnp.sum(share(residual...  39.5 us
    gather x4, local copies, waits for them, and re-layouts, second_half(): item_factors[items]  7.29 us
    all_gather x1, blocking collectives, per_device(): start = lax.all_gather(rhs, 'col', axis=0, tiled=True)  6.49 us
    scatter-add x4, other arithmetic, turn(): return acc.at[part_users].add(second_half(tiles, item_factors, part_items))  5.4 us
  transfers between devices with their start and end apart: 2, of which 2 were waited for; matrix products, arithmetic and copies ran while one was open for 0% of the time, Pallas kernels for 0%

commit v1 on v0

v1 whole, which is shorter than its diff:
```python
import functools

import jax
import jax.numpy as jnp
from jax import lax
from jax.experimental import pallas as pl
from jax.experimental.pallas import tpu as pltpu
from jax.sharding import PartitionSpec as P

graph_weight = 0.01
ridge_weight = 0.5
unroll = 16
f32 = jnp.float32
bf16 = jnp.bfloat16

VMEM = pl.BlockSpec(memory_space=pltpu.VMEM)
SMEM = pl.BlockSpec(memory_space=pltpu.SMEM)


def dot(a, b, dims):
    return lax.dot_general(a, b, ((dims[:1], dims[1:]), ((), ())), preferred_element_type=f32)


def add_data(cell, shared, acc):
    users, items, count_ref, factors, words = cell
    count = count_ref[0, 0]
    group = unroll if users.shape[0] % unroll == 0 else 1
    bit = jnp.left_shift(1, lax.broadcasted_iota(jnp.int32, (8, words.shape[2]), 0))

    def turn(index, carry):
        start = index * group
        for step in range(group):
            slot = start + step
            user, item = users[slot], items[slot]
            left = factors[item]
            scores = dot(left, shared[user], (0, 0))
            used = jnp.where(slot < count, bit, 0)
            mask = (words[slot][:, None, :] & used[None]) != 0
            tile = jnp.where(mask.reshape(scores.shape), scores, 0.0).astype(bf16)
            acc[user] += dot(left, tile, (1, 0))
        return carry

    lax.fori_loop(0, (count + group - 1) // group, turn, 0)


def add_graph(tiles, shared, acc, first):
    self_tiles, next_tiles = tiles
    row_blocks = shared.shape[0]
    for j in range(self_tiles.shape[0]):
        local = first + j
        after = jnp.minimum(local + 1, row_blocks - 1)
        keep = (local < row_blocks - 1).astype(f32)
        own, following = shared[local], shared[after]
        weights = self_tiles[j].astype(f32)
        sym = weights + weights.T
        edges = next_tiles[j].astype(f32) * keep
        sym_b, edges_b = sym.astype(bf16), edges.astype(bf16)
        ones = jnp.ones((8, sym.shape[0]), bf16)
        degree = jnp.sum(sym, axis=0, keepdims=True) + dot(ones, edges_b, (1, 1))[:1]
        column_degree = jnp.sum(edges, axis=0, keepdims=True)
        here = degree * own.astype(f32) - dot(own, sym_b, (1, 0)) - dot(following, edges_b, (1, 1))
        there = column_degree * following.astype(f32) - dot(own, edges_b, (1, 0))
        acc[local] += graph_weight * here
        acc[after] += graph_weight * there


def total(value):
    return jnp.sum(jnp.sum(value, axis=tuple(range(value.ndim - 2))), keepdims=True)


def first_kernel(parts, *refs):
    users, items, count, factors, words, self_tiles, next_tiles = refs[:7]
    pieces = refs[7 : 7 + parts]
    acc, shared = refs[7 + parts :]
    me = lax.axis_index("col")
    share = pieces[0].shape[0]
    for offset in range(parts):
        block = (me ^ offset) * share
        shared[pl.ds(block, share)] = pieces[offset][...].astype(bf16)
    acc[...] = jnp.zeros_like(acc)
    add_graph((self_tiles, next_tiles), shared, acc, me * share)
    add_data((users, items, count, factors, words), shared, acc)


def second_kernel(parts, height, *refs):
    users, items, count, factors, words, self_tiles, next_tiles = refs[:7]
    pieces = refs[7 : 7 + parts]
    left, right = refs[7 + parts : 9 + parts]
    outs = refs[9 + parts : 9 + 2 * parts]
    scalars, own_z, own_w, shared, acc, start, image, move = refs[9 + 2 * parts :]
    me, row = lax.axis_index("col"), lax.axis_index("row")
    share = pieces[0].shape[0]
    for offset in range(parts):
        block = (me ^ offset) * share
        start[pl.ds(block, share)] = pieces[offset][...]
    rhs = start[...]
    w = left[...] + right[...] + ridge_weight * rhs
    a, b = total(rhs * rhs), total(rhs * w)
    step = jnp.where(b > 0.0, a / jnp.where(b > 0.0, b, 1.0), 1.0)
    step = jnp.where(step > 0.0, step, 1.0)
    z = rhs - step * w
    image[...] = w
    move[...] = z
    shared[...] = z.astype(bf16)
    rz, zz, zw = total(rhs * z), total(z * z), total(z * w)
    acc[...] = jnp.zeros_like(acc)
    add_graph((self_tiles, next_tiles), shared, acc, me * share)
    add_data((users, items, count, factors, words), shared, acc)
    partial_value = acc[...]
    zh, rh = total(partial_value * move[...]), total(partial_value * start[...])
    part = 1.0 / parts
    values = (
        a * part,
        b * part,
        step * part,
        rz * part,
        zz * part,
        zw * part,
        zh + ridge_weight * part * zz,
        rh + ridge_weight * part * rz,
    )
    lane = lax.broadcasted_iota(jnp.int32, (height, 128), 1)
    sublane = lax.broadcasted_iota(jnp.int32, (height, 128), 0)
    packed = jnp.zeros((height, 128), f32)
    for index, value in enumerate(values):
        packed = jnp.where(lane == index, value, packed)
    scalars[...] = jnp.where(sublane == row, packed, 0.0)
    for offset in range(parts):
        outs[offset][...] = acc[pl.ds((me ^ offset) * share, share)]
    own_z[...] = move[pl.ds(me * share, share)]
    own_w[...] = image[pl.ds(me * share, share)]


def last_kernel(parts, scalar_parts, *refs):
    own_r, own_z, own_w = refs[:3]
    images = refs[3 : 3 + parts]
    scalars = refs[3 + parts : 3 + parts + scalar_parts]
    solution_ref, residual_ref = refs[3 + parts + scalar_parts :]
    table = scalars[0][...]
    for ref in scalars[1:]:
        table = table + ref[...]
    row = lax.axis_index("row")
    height = table.shape[0]
    a, b, step, rz, zz, zw, zh, rh = (table[:, k : k + 1] for k in range(8))

    def whole(value):
        return jnp.sum(value, axis=0, keepdims=True)

    norm = whole(a)
    alpha = norm / whole(b)
    rho = alpha / jnp.where(step > 0.0, step, 1.0)
    rest = 1.0 - rho
    norm_next = whole(rest * rest * a + 2.0 * rest * rho * rz + rho * rho * zz)
    beta = norm_next / norm
    p = rest + beta
    curve = whole(p * p * b + p * rho * (zw + rh) + rho * rho * zh)
    alpha_next = norm_next / curve
    sublane = lax.broadcasted_iota(jnp.int32, (height, 1), 0)
    mine = jnp.where(sublane == row, rho, 0.0)
    rho = whole(mine)
    rest = 1.0 - rho
    p = rest + beta
    r, z, w = own_r[...], own_z[...], own_w[...]
    hz = ridge_weight * z
    for ref in images:
        hz = hz + ref[...]
    solution_ref[...] = (alpha + alpha_next * p) * r + (alpha_next * rho) * z
    residual_ref[...] = rest * r + rho * z - alpha_next * (p * w + rho * hz)


def exchange(value, axes, size, offset):
    return lax.ppermute(value, axes, [(i, i ^ offset) for i in range(size)])


def bit_groups(size):
    bits = [1 << k for k in range(size.bit_length() - 1)]
    groups = [bits[:1]] + [bits[k : k + 2] for k in range(1, len(bits), 2)]
    return [group for group in groups if group]


def spans(group):
    offsets = [0]
    for bit in group:
        offsets = offsets + [offset ^ bit for offset in offsets]
    return offsets[1:]


def per_device(
    rows, cols, rhs, item_factors, slot_users, slot_items, slot_counts, mask_words, self_tiles, next_tiles
):
    share, rank, width = rhs.shape
    row_shape = (cols * share, rank, width)
    cell = (
        slot_users[0, 0],
        slot_items[0, 0],
        slot_counts,
        item_factors,
        mask_words[0, 0],
        self_tiles,
        next_tiles,
    )
    cell_specs = [SMEM] * 3 + [VMEM] * 4
    params = pltpu.CompilerParams(vmem_limit_bytes=40 * 1024 * 1024)
    pieces = [rhs] + [exchange(rhs, "col", cols, offset) for offset in range(1, cols)]

    value = pl.pallas_call(
        functools.partial(first_kernel, cols),
        out_shape=jax.ShapeDtypeStruct(row_shape, f32),
        in_specs=cell_specs + [VMEM] * cols,
        out_specs=VMEM,
        scratch_shapes=[pltpu.VMEM(row_shape, bf16)],
        compiler_params=params,
        name="first_apply",
    )(*cell, *pieces)
    bits = [1 << k for k in range(cols.bit_length() - 1)]
    other = jnp.zeros_like(value) if not bits else None
    for index, bit in enumerate(bits):
        other = exchange(value, "col", cols, bit)
        if index + 1 < len(bits):
            value = value + other

    height = -(-rows // 8) * 8
    piece = jax.ShapeDtypeStruct(rhs.shape, f32)
    outs = pl.pallas_call(
        functools.partial(second_kernel, cols, height),
        out_shape=[piece] * cols + [jax.ShapeDtypeStruct((height, 128), f32), piece, piece],
        in_specs=cell_specs + [VMEM] * (cols + 2),
        out_specs=[VMEM] * (cols + 3),
        scratch_shapes=[pltpu.VMEM(row_shape, bf16)] + [pltpu.VMEM(row_shape, f32)] * 4,
        compiler_params=params,
        name="second_apply",
    )(*cell, *pieces, value, other)
    table, own_z, own_w = outs[cols:]
    images = [outs[0]] + [exchange(outs[offset], "col", cols, offset) for offset in range(1, cols)]
    groups = bit_groups(rows * cols)
    tables = [table]
    for group in groups:
        table = functools.reduce(jnp.add, tables)
        tables = [table] + [exchange(table, ("row", "col"), rows * cols, o) for o in spans(group)]

    return pl.pallas_call(
        functools.partial(last_kernel, cols, len(tables)),
        out_shape=[piece, piece],
        in_specs=[VMEM] * (3 + cols + len(tables)),
        out_specs=[VMEM] * 2,
        compiler_params=params,
        name="last_update",
    )(rhs, own_z, own_w, *images, *tables)


def solution(mesh):
    rows, cols = mesh.shape["row"], mesh.shape["col"]
    return jax.shard_map(
        functools.partial(per_device, rows, cols),
        mesh=mesh,
        in_specs=(
            P(("row", "col"), None, None),
            P("col", None, None),
            P("row", "col", None),
            P("row", "col", None),
            P("row", "col"),
            P("row", "col", None, None, None),
            P(("row", "col"), None, None),
            P(("row", "col"), None, None),
        ),
        out_specs=(P(("row", "col"), None, None), P(("row", "col"), None, None)),
        check_vma=False,
    )
```

time: 257 us -> 45.4 us (0.18)
  waiting for transfers between devices: 113 us -> 15.5 us
  blocking collectives: 85.6 us -> 0 us
  starting transfers between devices: 0.08 us -> 18.7 us
  between operations: 19.4 us -> 1.32 us
  other arithmetic: 13.7 us -> 0.03 us
  local copies, waits for them, and re-layouts: 18 us -> 5.46 us
  matrix products: 5.47 us -> 0 us
  Pallas kernels: 0 us -> 3.9 us
    psum x2 -> x0, waiting for transfers between devices: 113 us -> none  [per_device(): image = lax.psum(apply_partial_value, 'col') + ridge_weight * direction]
    psum x2 -> x0, blocking collectives: 79.1 us -> none  [the longest x1 39.6 us: per_device(): norm_now = lax.psum(jnp.sum(mine * mine), ('row', 'col'))]
    ppermute x0 -> x15, starting transfers between devices: none -> 18.7 us  [exchange(): return lax.ppermute(value, axes, [(i, i ^ offset) for i in range(size)])]
    ppermute x0 -> x15, waiting for transfers between devices: none -> 15.5 us  [exchange(): return lax.ppermute(value, axes, [(i, i ^ offset) for i in range(size)])]
    gather x8 -> x0, local copies, waits for them, and re-layouts: 9.68 us -> none  [the longest x4 7.29 us: second_half(): item_factors[items]]
    all_gather x1 -> x0, blocking collectives: 6.49 us -> none  [per_device(): start = lax.all_gather(rhs, 'col', axis=0, tiled=True)]
    dot_general x10 -> x0, matrix products: 5.47 us -> none  [the longest x4 2.26 us: second_half(): jnp.einsum('siu,sdi->sdu', tiles, item_factors[items], preferred_element_...]
    scatter-add x4 -> x0, other arithmetic: 5.4 us -> none  [turn(): return acc.at[part_users].add(second_half(tiles, item_factors, part_items))]
  transfers between devices with their start and end apart: 2 -> 15, of which waited for: 2 -> 9; matrix products, arithmetic and copies ran while one was open for 0% -> 0% of each run, Pallas kernels for 0% -> 0%
where the time goes in v1:
time: 45.4 us; the launch traced here: 45 us
  starting transfers between devices  18.7 us (41%)
  waiting for transfers between devices  15.5 us (34%)
  local copies, waits for them, and re-layouts  5.46 us (12%)
  Pallas kernels  3.9 us (9%)
  between operations  1.32 us (3%)
    ppermute x15, starting transfers between devices, exchange(): return lax.ppermute(value, axes, [(i, i ^ offset) for i in range(size)])  18.7 us
    ppermute x15, waiting for transfers between devices, exchange(): return lax.ppermute(value, axes, [(i, i ^ offset) for i in range(size)])  15.5 us
    unnamed x14, local copies, waits for them, and re-layouts  5.46 us
    pallas_call x1, Pallas kernels, per_device(): pl.pallas_call(functools.partial(second_kernel, cols, height), out_shape=...  1.66 us
    pallas_call x1, Pallas kernels, per_device(): pl.pallas_call(functools.partial(first_kernel, cols), out_shape=jax.Shape...  1.39 us
  transfers between devices with their start and end apart: 15, of which 9 were waited for; matrix products, arithmetic and copies ran while one was open for 0% of the time, Pallas kernels for 0%

profile of v1, /device:TPU:0, one launch (start us, length us, event | category | flops | bytes accessed | tf_op | source)
XLA Modules:
  0.0 45.0 jit_solution(169784841963441512)
XLA Ops:
  0.6 2.5 %collective-permute-start.2 = (f32[1,64,128]{2,1,0:T(8,128)}, f32[1,64,128]{2,1,0:T(8,128)S(1)}, u32[]{:S(2)}, u32[]{:S(2)}) collective-permute-start(f32[1,64,128]{2,1,0:T(8,128)} %refs_0_.1), channel_id=1, source_target_pairs={{0,3},{1,2},{2,1},{3,0},{4,7},{5,6},{6,5},{7,4},{8,11},{9,10},{10,... | collective-permute-start | bytes 98312 | tf_op jit(solution)/shard_map/ppermute | solution.py:172
  3.1 0.6 %collective-permute-start.1 = (f32[1,64,128]{2,1,0:T(8,128)}, f32[1,64,128]{2,1,0:T(8,128)S(1)}, u32[]{:S(2)}, u32[]{:S(2)}) collective-permute-start(f32[1,64,128]{2,1,0:T(8,128)} %refs_0_.1), channel_id=1, source_target_pairs={{0,2},{1,3},{2,0},{3,1},{4,6},{5,7},{6,4},{7,5},{8,10},{9,11},{10,... | collective-permute-start | bytes 98312 | tf_op jit(solution)/shard_map/ppermute | solution.py:172
  3.7 0.0 collective-permute-start
  4.4 0.8 %collective-permute-done.2.refs_10_ = f32[1,64,128]{2,1,0:T(8,128)S(1)} collective-permute-done((f32[1,64,128]{2,1,0:T(8,128)}, f32[1,64,128]{2,1,0:T(8,128)S(1)}, u32[]{:S(2)}, u32[]{:S(2)}) %collective-permute-start.2) | collective-permute-done | bytes 32800 | tf_op jit(solution)/shard_map/ppermute | solution.py:172
  5.2 2.1 %collective-permute-done.1.refs_9_ = f32[1,64,128]{2,1,0:T(8,128)S(1)} collective-permute-done((f32[1,64,128]{2,1,0:T(8,128)}, f32[1,64,128]{2,1,0:T(8,128)S(1)}, u32[]{:S(2)}, u32[]{:S(2)}) %collective-permute-start.1) | collective-permute-done | bytes 32800 | tf_op jit(solution)/shard_map/ppermute | solution.py:172
  7.3 0.0 collective-permute-done.refs_8_
  7.3 0.0 copy-start.5
  7.3 0.0 copy-start.6
  7.3 0.7 %copy-done.5 = s32[1,1,96]{2,1,0:T(1,128)S(1)} copy-done((s32[1,1,96]{2,1,0:T(1,128)S(1)}, s32[1,1,96]{2,1,0:T(1,128)}, u32[]{:S(2)}) %copy-start.5) | copy-done | bytes 408
  7.9 0.0 copy-done.6
  8.0 0.0 copy-start
  8.0 1.2 %copy-done = bf16[64,64,128]{2,1,0:T(8,128)(2,1)S(1)} copy-done((bf16[64,64,128]{2,1,0:T(8,128)(2,1)S(1)}, bf16[64,64,128]{2,1,0:T(8,128)(2,1)}, u32[]{:S(2)}) %copy-start) | copy-done | bytes 1048600
  9.2 0.0 copy-start.1
  9.2 1.1 %copy-done.1 = s32[1,1,96,16,128]{4,3,2,1,0:T(8,128)S(1)} copy-done((s32[1,1,96,16,128]{4,3,2,1,0:T(8,128)S(1)}, s32[1,1,96,16,128]{4,3,2,1,0:T(8,128)}, u32[]{:S(2)}) %copy-start.1) | copy-done | bytes 786456
  10.3 0.0 copy-start.2
  10.3 0.8 %copy-done.2 = f32[1,64,128]{2,1,0:T(8,128)S(1)} copy-done((f32[1,64,128]{2,1,0:T(8,128)S(1)}, f32[1,64,128]{2,1,0:T(8,128)}, u32[]{:S(2)}) %copy-start.2) | copy-done | bytes 32792
  11.1 0.0 copy-start.3
  11.1 0.8 %copy-done.3 = s32[1,128,128]{2,1,0:T(8,128)S(1)} copy-done((s32[1,128,128]{2,1,0:T(8,128)S(1)}, s32[1,128,128]{2,1,0:T(8,128)}, u32[]{:S(2)}) %copy-start.3) | copy-done | bytes 65560
  11.9 0.0 copy-start.4
  11.9 0.8 %copy-done.4 = s32[1,128,128]{2,1,0:T(8,128)S(1)} copy-done((s32[1,128,128]{2,1,0:T(8,128)S(1)}, s32[1,128,128]{2,1,0:T(8,128)}, u32[]{:S(2)}) %copy-start.4) | copy-done | bytes 65560
  12.8 1.4 %first_apply.1 = f32[4,64,128]{2,1,0:T(8,128)S(1)} custom-call(s32[96]{0:T(128)S(1)} %bitcast.5, s32[96]{0:T(128)S(1)} %bitcast.7, s32[1,1]{1,0:T(1,128)S(6)} %copy.10.refs_2_, bf16[64,64,128]{2,1,0:T(8,128)(2,1)S(1)} %copy-done, s32[96,16,128]{2,1,0:T(8,128)S(1)} %bitcast.3, s32[1,128,128]{2,1,0:T(8,128)S(1)} %copy-done.3, s32[1,128,128]{2,1,0:T(8,128)S(1)} %copy-done.4, ...), custom_call_target="tpu_custom_call" | custom-call | tf_op jit(solution)/shard_map/first_apply/pallas_call | solution.py:206
  14.1 2.8 %collective-permute-start.3 = (f32[4,64,128]{2,1,0:T(8,128)S(1)}, f32[4,64,128]{2,1,0:T(8,128)S(1)}, u32[]{:S(2)}, u32[]{:S(2)}) collective-permute-start(f32[4,64,128]{2,1,0:T(8,128)S(1)} %first_apply.1), channel_id=1, source_target_pairs={{0,1},{1,0},{2,3},{3,2},{4,5},{5,4},{6,7},{7,6},{8,9},{9,8},{10,11... | collective-permute-start | bytes 393224 | tf_op jit(solution)/shard_map/ppermute | solution.py:172
  16.9 1.0 %collective-permute-done.3 = f32[4,64,128]{2,1,0:T(8,128)S(1)} collective-permute-done((f32[4,64,128]{2,1,0:T(8,128)S(1)}, f32[4,64,128]{2,1,0:T(8,128)S(1)}, u32[]{:S(2)}, u32[]{:S(2)}) %collective-permute-start.3) | collective-permute-done | bytes 131104 | tf_op jit(solution)/shard_map/ppermute | solution.py:172
  17.9 1.3 %collective-permute-start.4 = (f32[4,64,128]{2,1,0:T(8,128)S(1)}, f32[4,64,128]{2,1,0:T(8,128)S(1)}, u32[]{:S(2)}, u32[]{:S(2)}) collective-permute-start(f32[4,64,128]{2,1,0:T(8,128)S(1)} %add.15.refs_11_), channel_id=1, source_target_pairs={{0,2},{1,3},{2,0},{3,1},{4,6},{5,7},{6,4},{7,5},{8,10},{9,11},{10,... | collective-permute-start | bytes 393224 | tf_op jit(solution)/shard_map/ppermute | solution.py:172
  19.3 4.5 %collective-permute-done.4.refs_12_ = f32[4,64,128]{2,1,0:T(8,128)S(1)} collective-permute-done((f32[4,64,128]{2,1,0:T(8,128)S(1)}, f32[4,64,128]{2,1,0:T(8,128)S(1)}, u32[]{:S(2)}, u32[]{:S(2)}) %collective-permute-start.4) | collective-permute-done | bytes 131104 | tf_op jit(solution)/shard_map/ppermute | solution.py:172
  23.8 1.7 %second_apply.1 = (f32[1,64,128]{2,1,0:T(8,128)S(1)}, f32[1,64,128]{2,1,0:T(8,128)S(1)}, f32[1,64,128]{2,1,0:T(8,128)S(1)}, f32[1,64,128]{2,1,0:T(8,128)S(1)}, f...) custom-call(s32[96]{0:T(128)S(1)} %bitcast.6, s32[96]{0:T(128)S(1)} %bitcast.8, ...), custom_call_target="tpu_custom_call" | custom-call | tf_op jit(solution)/shard_map/second_apply/pallas_call | solution.py:224
  25.4 2.5 %collective-permute-start.8 = (f32[8,128]{1,0:T(8,128)S(1)}, f32[8,128]{1,0:T(8,128)S(1)}, u32[]{:S(2)}, u32[]{:S(2)}) collective-permute-start(f32[8,128]{1,0:T(8,128)S(1)} %get-tuple-element.15), channel_id=1, source_target_pairs={{0,1},{1,0},{2,3},{3,2},{4,5},{5,4},{6,7},{7,6},{8,9},{9,8},{10,11... | collective-permute-start | bytes 12296 | tf_op jit(solution)/shard_map/ppermute | solution.py:172
  27.9 0.8 %collective-permute-done.8 = f32[8,128]{1,0:T(8,128)S(1)} collective-permute-done((f32[8,128]{1,0:T(8,128)S(1)}, f32[8,128]{1,0:T(8,128)S(1)}, u32[]{:S(2)}, u32[]{:S(2)}) %collective-permute-start.8) | collective-permute-done | bytes 4128 | tf_op jit(solution)/shard_map/ppermute | solution.py:172
  28.7 0.0 collective-permute-start.11
  28.8 2.7 %collective-permute-start.10 = (f32[8,128]{1,0:T(8,128)S(1)}, f32[8,128]{1,0:T(8,128)S(1)}, u32[]{:S(2)}, u32[]{:S(2)}) collective-permute-start(f32[8,128]{1,0:T(8,128)S(1)} %add.16), channel_id=1, source_target_pairs={{0,4},{1,5},{2,6},{3,7},{4,0},{5,1},{6,2},{7,3},{8,12},{9,13},{10,... | collective-permute-start | bytes 12296 | tf_op jit(solution)/shard_map/ppermute | solution.py:172
  31.5 0.8 %collective-permute-start.9 = (f32[8,128]{1,0:T(8,128)S(1)}, f32[8,128]{1,0:T(8,128)S(1)}, u32[]{:S(2)}, u32[]{:S(2)}) collective-permute-start(f32[8,128]{1,0:T(8,128)S(1)} %add.16), channel_id=1, source_target_pairs={{0,2},{1,3},{2,0},{3,1},{4,6},{5,7},{6,4},{7,5},{8,10},{9,11},{10,... | collective-permute-start | bytes 12296 | tf_op jit(solution)/shard_map/ppermute | solution.py:172
  32.2 0.0 collective-permute-start.5
  32.2 1.3 %collective-permute-start.6 = (f32[1,64,128]{2,1,0:T(8,128)S(1)}, f32[1,64,128]{2,1,0:T(8,128)S(1)}, u32[]{:S(2)}, u32[]{:S(2)}) collective-permute-start(f32[1,64,128]{2,1,0:T(8,128)S(1)} %get-tuple-element.13), channel_id=1, source_target_pairs={{0,2},{1,3},{2,0},{3,1},{4,6},{5,7},{6,4},{7,5},{8,10},{9,11},{10,... | collective-permute-start | bytes 98312 | tf_op jit(solution)/shard_map/ppermute | solution.py:172
  33.5 0.0 collective-permute-done.11
  33.5 0.6 %collective-permute-start.7 = (f32[1,64,128]{2,1,0:T(8,128)S(1)}, f32[1,64,128]{2,1,0:T(8,128)S(1)}, u32[]{:S(2)}, u32[]{:S(2)}) collective-permute-start(f32[1,64,128]{2,1,0:T(8,128)S(1)} %get-tuple-element.14), channel_id=1, source_target_pairs={{0,3},{1,2},{2,1},{3,0},{4,7},{5,6},{6,5},{7,4},{8,11},{9,10},{10,... | collective-permute-start | bytes 98312 | tf_op jit(solution)/shard_map/ppermute | solution.py:172
  34.1 0.0 collective-permute-done.10
  34.1 1.0 %collective-permute-done.9 = f32[8,128]{1,0:T(8,128)S(1)} collective-permute-done((f32[8,128]{1,0:T(8,128)S(1)}, f32[8,128]{1,0:T(8,128)S(1)}, u32[]{:S(2)}, u32[]{:S(2)}) %collective-permute-start.9) | collective-permute-done | bytes 4128 | tf_op jit(solution)/shard_map/ppermute | solution.py:172
  35.1 3.6 %collective-permute-start.14 = (f32[8,128]{1,0:T(8,128)S(1)}, f32[8,128]{1,0:T(8,128)S(1)}, u32[]{:S(2)}, u32[]{:S(2)}) collective-permute-start(f32[8,128]{1,0:T(8,128)S(1)} %add_add_fusion.refs_7_), channel_id=1, source_target_pairs={{0,24},{1,25},{2,26},{3,27},{4,28},{5,29},{6,30},{7,31},{8,16},{9,... | collective-permute-start | bytes 12296 | tf_op jit(solution)/shard_map/ppermute | solution.py:172
  38.7 0.0 collective-permute-start.13
  38.7 1.8 %collective-permute-done.14.refs_10_ = f32[8,128]{1,0:T(8,128)S(1)} collective-permute-done((f32[8,128]{1,0:T(8,128)S(1)}, f32[8,128]{1,0:T(8,128)S(1)}, u32[]{:S(2)}, u32[]{:S(2)}) %collective-permute-start.14) | collective-permute-done | bytes 4128 | tf_op jit(solution)/shard_map/ppermute | solution.py:172
  40.5 0.0 collective-permute-start.12
  40.5 2.7 %collective-permute-done.13.refs_9_ = f32[8,128]{1,0:T(8,128)S(1)} collective-permute-done((f32[8,128]{1,0:T(8,128)S(1)}, f32[8,128]{1,0:T(8,128)S(1)}, u32[]{:S(2)}, u32[]{:S(2)}) %collective-permute-start.13) | collective-permute-done | bytes 4128 | tf_op jit(solution)/shard_map/ppermute | solution.py:172
  43.2 0.9 %collective-permute-done.12.refs_8_ = f32[8,128]{1,0:T(8,128)S(1)} collective-permute-done((f32[8,128]{1,0:T(8,128)S(1)}, f32[8,128]{1,0:T(8,128)S(1)}, u32[]{:S(2)}, u32[]{:S(2)}) %collective-permute-start.12) | collective-permute-done | bytes 4128 | tf_op jit(solution)/shard_map/ppermute | solution.py:172
  44.1 0.0 collective-permute-done.5.refs_4_
  44.1 0.0 collective-permute-done.6.refs_5_
  44.1 0.0 collective-permute-done.7.refs_6_
  44.1 0.9 %last_update.1 = (f32[1,64,128]{2,1,0:T(8,128)}, f32[1,64,128]{2,1,0:T(8,128)}) custom-call(f32[1,64,128]{2,1,0:T(8,128)S(1)} %copy-done.2, f32[1,64,128]{2,1,0:T(8,128)S(1)} %get-tuple-element.9.refs_1_, f32[1,64,128]{2,1,0:T(8,128)S(1)} %get-tuple-element.10.refs_2_, f32[1,64,128]{2,1,0:T(8,128)S(1)} %get-tuple-element.11.refs_3_, ...), custom_call_target="tpu_custom_call" | custom-call | tf_op jit(solution)/shard_map/last_update/pallas_call | solution.py:241
  (3 shorter events, 0.0 us)
Async XLA Ops:
  0.6 4.6 %collective-permute-start.2 = (f32[1,64,128]{2,1,0:T(8,128)}, f32[1,64,128]{2,1,0:T(8,128)S(1)}, u32[]{:S(2)}, u32[]{:S(2)}) collective-permute-start(f32[1,64,128]{2,1,0:T(8,128)} %refs_0_.1), channel_id=1, source_target_pairs={{0,3},{1,2},{2,1},{3,0},{4,7},{5,6},{6,5},{7,4},{8,11},{9,10},{10,... | collective-permute-start | bytes 98312 | tf_op jit(solution)/shard_map/ppermute | solution.py:172
  3.1 4.2 %collective-permute-start.1 = (f32[1,64,128]{2,1,0:T(8,128)}, f32[1,64,128]{2,1,0:T(8,128)S(1)}, u32[]{:S(2)}, u32[]{:S(2)}) collective-permute-start(f32[1,64,128]{2,1,0:T(8,128)} %refs_0_.1), channel_id=1, source_target_pairs={{0,2},{1,3},{2,0},{3,1},{4,6},{5,7},{6,4},{7,5},{8,10},{9,11},{10,... | collective-permute-start | bytes 98312 | tf_op jit(solution)/shard_map/ppermute | solution.py:172
  3.7 3.5 %collective-permute-start = (f32[1,64,128]{2,1,0:T(8,128)}, f32[1,64,128]{2,1,0:T(8,128)S(1)}, u32[]{:S(2)}, u32[]{:S(2)}) collective-permute-start(f32[1,64,128]{2,1,0:T(8,128)} %refs_0_.1), channel_id=1, source_target_pairs={{0,1},{1,0},{2,3},{3,2},{4,5},{5,4},{6,7},{7,6},{8,9},{9,8},{10,11... | collective-permute-start | bytes 98312 | tf_op jit(solution)/shard_map/ppermute | solution.py:172
  7.3 0.7 %copy-start.5 = (s32[1,1,96]{2,1,0:T(1,128)S(1)}, s32[1,1,96]{2,1,0:T(1,128)}, u32[]{:S(2)}) copy-start(s32[1,1,96]{2,1,0:T(1,128)} %param.10) | copy-start | bytes 1156
  7.3 0.7 %copy-start.6 = (s32[1,1,96]{2,1,0:T(1,128)S(1)}, s32[1,1,96]{2,1,0:T(1,128)}, u32[]{:S(2)}) copy-start(s32[1,1,96]{2,1,0:T(1,128)} %param.11) | copy-start | bytes 1156
  8.0 1.2 %copy-start = (bf16[64,64,128]{2,1,0:T(8,128)(2,1)S(1)}, bf16[64,64,128]{2,1,0:T(8,128)(2,1)}, u32[]{:S(2)}) copy-start(bf16[64,64,128]{2,1,0:T(8,128)(2,1)} %refs_3_.3) | copy-start | bytes 3145732
  9.2 1.1 %copy-start.1 = (s32[1,1,96,16,128]{4,3,2,1,0:T(8,128)S(1)}, s32[1,1,96,16,128]{4,3,2,1,0:T(8,128)}, u32[]{:S(2)}) copy-start(s32[1,1,96,16,128]{4,3,2,1,0:T(8,128)} %param.13) | copy-start | bytes 2359300
  10.3 0.8 %copy-start.2 = (f32[1,64,128]{2,1,0:T(8,128)S(1)}, f32[1,64,128]{2,1,0:T(8,128)}, u32[]{:S(2)}) copy-start(f32[1,64,128]{2,1,0:T(8,128)} %refs_0_.1) | copy-start | bytes 98308
  11.1 0.8 %copy-start.3 = (s32[1,128,128]{2,1,0:T(8,128)S(1)}, s32[1,128,128]{2,1,0:T(8,128)}, u32[]{:S(2)}) copy-start(s32[1,128,128]{2,1,0:T(8,128)} %refs_5_.3) | copy-start | bytes 196612
  11.9 0.8 %copy-start.4 = (s32[1,128,128]{2,1,0:T(8,128)S(1)}, s32[1,128,128]{2,1,0:T(8,128)}, u32[]{:S(2)}) copy-start(s32[1,128,128]{2,1,0:T(8,128)} %refs_6_.3) | copy-start | bytes 196612
  14.1 3.8 %collective-permute-start.3 = (f32[4,64,128]{2,1,0:T(8,128)S(1)}, f32[4,64,128]{2,1,0:T(8,128)S(1)}, u32[]{:S(2)}, u32[]{:S(2)}) collective-permute-start(f32[4,64,128]{2,1,0:T(8,128)S(1)} %first_apply.1), channel_id=1, source_target_pairs={{0,1},{1,0},{2,3},{3,2},{4,5},{5,4},{6,7},{7,6},{8,9},{9,8},{10,11... | collective-permute-start | bytes 393224 | tf_op jit(solution)/shard_map/ppermute | solution.py:172
  17.9 5.8 %collective-permute-start.4 = (f32[4,64,128]{2,1,0:T(8,128)S(1)}, f32[4,64,128]{2,1,0:T(8,128)S(1)}, u32[]{:S(2)}, u32[]{:S(2)}) collective-permute-start(f32[4,64,128]{2,1,0:T(8,128)S(1)} %add.15.refs_11_), channel_id=1, source_target_pairs={{0,2},{1,3},{2,0},{3,1},{4,6},{5,7},{6,4},{7,5},{8,10},{9,11},{10,... | collective-permute-start | bytes 393224 | tf_op jit(solution)/shard_map/ppermute | solution.py:172
  25.4 3.3 %collective-permute-start.8 = (f32[8,128]{1,0:T(8,128)S(1)}, f32[8,128]{1,0:T(8,128)S(1)}, u32[]{:S(2)}, u32[]{:S(2)}) collective-permute-start(f32[8,128]{1,0:T(8,128)S(1)} %get-tuple-element.15), channel_id=1, source_target_pairs={{0,1},{1,0},{2,3},{3,2},{4,5},{5,4},{6,7},{7,6},{8,9},{9,8},{10,11... | collective-permute-start | bytes 12296 | tf_op jit(solution)/shard_map/ppermute | solution.py:172
  28.7 4.8 %collective-permute-start.11 = (f32[8,128]{1,0:T(8,128)S(1)}, f32[8,128]{1,0:T(8,128)S(1)}, u32[]{:S(2)}, u32[]{:S(2)}) collective-permute-start(f32[8,128]{1,0:T(8,128)S(1)} %add.16), channel_id=1, source_target_pairs={{0,6},{1,7},{2,4},{3,5},{4,2},{5,3},{6,0},{7,1},{8,14},{9,15},{10,... | collective-permute-start | bytes 12296 | tf_op jit(solution)/shard_map/ppermute | solution.py:172
  28.8 5.4 %collective-permute-start.10 = (f32[8,128]{1,0:T(8,128)S(1)}, f32[8,128]{1,0:T(8,128)S(1)}, u32[]{:S(2)}, u32[]{:S(2)}) collective-permute-start(f32[8,128]{1,0:T(8,128)S(1)} %add.16), channel_id=1, source_target_pairs={{0,4},{1,5},{2,6},{3,7},{4,0},{5,1},{6,2},{7,3},{8,12},{9,13},{10,... | collective-permute-start | bytes 12296 | tf_op jit(solution)/shard_map/ppermute | solution.py:172
  31.5 3.6 %collective-permute-start.9 = (f32[8,128]{1,0:T(8,128)S(1)}, f32[8,128]{1,0:T(8,128)S(1)}, u32[]{:S(2)}, u32[]{:S(2)}) collective-permute-start(f32[8,128]{1,0:T(8,128)S(1)} %add.16), channel_id=1, source_target_pairs={{0,2},{1,3},{2,0},{3,1},{4,6},{5,7},{6,4},{7,5},{8,10},{9,11},{10,... | collective-permute-start | bytes 12296 | tf_op jit(solution)/shard_map/ppermute | solution.py:172
  32.2 11.9 %collective-permute-start.5 = (f32[1,64,128]{2,1,0:T(8,128)S(1)}, f32[1,64,128]{2,1,0:T(8,128)S(1)}, u32[]{:S(2)}, u32[]{:S(2)}) collective-permute-start(f32[1,64,128]{2,1,0:T(8,128)S(1)} %get-tuple-element.12), channel_id=1, source_target_pairs={{0,1},{1,0},{2,3},{3,2},{4,5},{5,4},{6,7},{7,6},{8,9},{9,8},{10,11... | collective-permute-start | bytes 98312 | tf_op jit(solution)/shard_map/ppermute | solution.py:172
  32.2 11.9 %collective-permute-start.6 = (f32[1,64,128]{2,1,0:T(8,128)S(1)}, f32[1,64,128]{2,1,0:T(8,128)S(1)}, u32[]{:S(2)}, u32[]{:S(2)}) collective-permute-start(f32[1,64,128]{2,1,0:T(8,128)S(1)} %get-tuple-element.13), channel_id=1, source_target_pairs={{0,2},{1,3},{2,0},{3,1},{4,6},{5,7},{6,4},{7,5},{8,10},{9,11},{10,... | collective-permute-start | bytes 98312 | tf_op jit(solution)/shard_map/ppermute | solution.py:172
  33.5 10.6 %collective-permute-start.7 = (f32[1,64,128]{2,1,0:T(8,128)S(1)}, f32[1,64,128]{2,1,0:T(8,128)S(1)}, u32[]{:S(2)}, u32[]{:S(2)}) collective-permute-start(f32[1,64,128]{2,1,0:T(8,128)S(1)} %get-tuple-element.14), channel_id=1, source_target_pairs={{0,3},{1,2},{2,1},{3,0},{4,7},{5,6},{6,5},{7,4},{8,11},{9,10},{10,... | collective-permute-start | bytes 98312 | tf_op jit(solution)/shard_map/ppermute | solution.py:172
  35.1 5.4 %collective-permute-start.14 = (f32[8,128]{1,0:T(8,128)S(1)}, f32[8,128]{1,0:T(8,128)S(1)}, u32[]{:S(2)}, u32[]{:S(2)}) collective-permute-start(f32[8,128]{1,0:T(8,128)S(1)} %add_add_fusion.refs_7_), channel_id=1, source_target_pairs={{0,24},{1,25},{2,26},{3,27},{4,28},{5,29},{6,30},{7,31},{8,16},{9,... | collective-permute-start | bytes 12296 | tf_op jit(solution)/shard_map/ppermute | solution.py:172
  38.7 4.5 %collective-permute-start.13 = (f32[8,128]{1,0:T(8,128)S(1)}, f32[8,128]{1,0:T(8,128)S(1)}, u32[]{:S(2)}, u32[]{:S(2)}) collective-permute-start(f32[8,128]{1,0:T(8,128)S(1)} %add_add_fusion.refs_7_), channel_id=1, source_target_pairs={{0,16},{1,17},{2,18},{3,19},{4,20},{5,21},{6,22},{7,23},{8,24},{9,... | collective-permute-start | bytes 12296 | tf_op jit(solution)/shard_map/ppermute | solution.py:172
  40.5 3.6 %collective-permute-start.12 = (f32[8,128]{1,0:T(8,128)S(1)}, f32[8,128]{1,0:T(8,128)S(1)}, u32[]{:S(2)}, u32[]{:S(2)}) collective-permute-start(f32[8,128]{1,0:T(8,128)S(1)} %add_add_fusion.refs_7_), channel_id=1, source_target_pairs={{0,8},{1,9},{2,10},{3,11},{4,12},{5,13},{6,14},{7,15},{8,0},{9,1},... | collective-permute-start | bytes 12296 | tf_op jit(solution)/shard_map/ppermute | solution.py:172

commit v2 on v1

--- a/solution.py
+++ b/solution.py
@@ -14,6 +14,7 @@
 bf16 = jnp.bfloat16
 
 VMEM = pl.BlockSpec(memory_space=pltpu.VMEM)
+HBM = pl.BlockSpec(memory_space=pltpu.HBM)
 SMEM = pl.BlockSpec(memory_space=pltpu.SMEM)
 
 
@@ -43,58 +44,90 @@
     lax.fori_loop(0, (count + group - 1) // group, turn, 0)
 
 
-def add_graph(tiles, shared, acc, first):
-    self_tiles, next_tiles = tiles
+def add_graph(graph, shared, acc, first):
+    sym, edges, degrees = graph
     row_blocks = shared.shape[0]
-    for j in range(self_tiles.shape[0]):
+    for j in range(sym.shape[0]):
         local = first + j
         after = jnp.minimum(local + 1, row_blocks - 1)
-        keep = (local < row_blocks - 1).astype(f32)
         own, following = shared[local], shared[after]
-        weights = self_tiles[j].astype(f32)
-        sym = weights + weights.T
-        edges = next_tiles[j].astype(f32) * keep
-        sym_b, edges_b = sym.astype(bf16), edges.astype(bf16)
-        ones = jnp.ones((8, sym.shape[0]), bf16)
-        degree = jnp.sum(sym, axis=0, keepdims=True) + dot(ones, edges_b, (1, 1))[:1]
-        column_degree = jnp.sum(edges, axis=0, keepdims=True)
-        here = degree * own.astype(f32) - dot(own, sym_b, (1, 0)) - dot(following, edges_b, (1, 1))
-        there = column_degree * following.astype(f32) - dot(own, edges_b, (1, 0))
+        degree, column_degree = degrees[j, 0:1], degrees[j, 8:9]
+        here = degree * own.astype(f32) - dot(own, sym[j], (1, 0)) - dot(following, edges[j], (1, 1))
+        there = column_degree * following.astype(f32) - dot(own, edges[j], (1, 0))
         acc[local] += graph_weight * here
         acc[after] += graph_weight * there
 
 
+def prepare_kernel(cols, factors_in, words_in, self_in, next_in, factors, words, sym, edges, degrees, tiles, sems):
+    first = lax.axis_index("col") * self_in.shape[0]
+    copies = [
+        pltpu.make_async_copy(source, target, sems.at[k])
+        for k, (source, target) in enumerate(
+            ((self_in, tiles.at[0]), (next_in, tiles.at[1]), (factors_in, factors), (words_in, words))
+        )
+    ]
+    for copy in copies:
+        copy.start()
+    copies[0].wait()
+    copies[1].wait()
+    count = self_in.shape[0]
+    for j in range(count):
+        keep = (first + j < cols * count - 1).astype(f32)
+        weights = tiles[0, j].astype(f32)
+        both = weights + weights.T
+        edge = tiles[1, j].astype(f32) * keep
+        edges_b = edge.astype(bf16)
+        sym[j] = both.astype(bf16)
+        edges[j] = edges_b
+        ones = jnp.ones((8, both.shape[0]), bf16)
+        degrees[j, 0:8] = jnp.sum(both, axis=0, keepdims=True) + dot(ones, edges_b, (1, 1))
+        degrees[j, 8:16] = jnp.broadcast_to(jnp.sum(edge, axis=0, keepdims=True), (8, both.shape[1]))
+    copies[2].wait()
+    copies[3].wait()
+
+
 def total(value):
     return jnp.sum(jnp.sum(value, axis=tuple(range(value.ndim - 2))), keepdims=True)
 
 
 def first_kernel(parts, *refs):
-    users, items, count, factors, words, self_tiles, next_tiles = refs[:7]
-    pieces = refs[7 : 7 + parts]
-    acc, shared = refs[7 + parts :]
+    users, items, count, factors, words, sym, edges, degrees = refs[:8]
+    pieces = refs[8 : 8 + parts]
+    keep, send, shared, acc = refs[8 + parts :]
     me = lax.axis_index("col")
     share = pieces[0].shape[0]
     for offset in range(parts):
         block = (me ^ offset) * share
         shared[pl.ds(block, share)] = pieces[offset][...].astype(bf16)
     acc[...] = jnp.zeros_like(acc)
-    add_graph((self_tiles, next_tiles), shared, acc, me * share)
+    add_graph((sym, edges, degrees), shared, acc, me * share)
     add_data((users, items, count, factors, words), shared, acc)
+    split(acc, keep, send, me, share)
+
+
+def split(acc, keep, send, me, share):
+    odd = me & 1
+    for j in range(keep.shape[0] // share):
+        keep[pl.ds(j * share, share)] = acc[pl.ds((2 * j + odd) * share, share)]
+        send[pl.ds(j * share, share)] = acc[pl.ds((2 * j + (odd ^ 1)) * share, share)]
 
 
 def second_kernel(parts, height, *refs):
-    users, items, count, factors, words, self_tiles, next_tiles = refs[:7]
-    pieces = refs[7 : 7 + parts]
-    left, right = refs[7 + parts : 9 + parts]
-    outs = refs[9 + parts : 9 + 2 * parts]
-    scalars, own_z, own_w, shared, acc, start, image, move = refs[9 + 2 * parts :]
+    users, items, count, factors, words, sym, edges, degrees = refs[:8]
+    pieces = refs[8 : 8 + parts]
+    mine, theirs = refs[8 + parts : 10 + parts]
+    keep, send, scalars, own_z, own_w, shared, acc, start, image, move = refs[10 + parts :]
     me, row = lax.axis_index("col"), lax.axis_index("row")
     share = pieces[0].shape[0]
     for offset in range(parts):
         block = (me ^ offset) * share
         start[pl.ds(block, share)] = pieces[offset][...]
+    odd = me & 1
+    for j in range(parts // 2):
+        image[pl.ds((2 * j + odd) * share, share)] = mine[pl.ds(j * share, share)]
+        image[pl.ds((2 * j + (odd ^ 1)) * share, share)] = theirs[pl.ds(j * share, share)]
     rhs = start[...]
-    w = left[...] + right[...] + ridge_weight * rhs
+    w = image[...] + ridge_weight * rhs
     a, b = total(rhs * rhs), total(rhs * w)
     step = jnp.where(b > 0.0, a / jnp.where(b > 0.0, b, 1.0), 1.0)
     step = jnp.where(step > 0.0, step, 1.0)
@@ -104,7 +137,7 @@
     shared[...] = z.astype(bf16)
     rz, zz, zw = total(rhs * z), total(z * z), total(z * w)
     acc[...] = jnp.zeros_like(acc)
-    add_graph((self_tiles, next_tiles), shared, acc, me * share)
+    add_graph((sym, edges, degrees), shared, acc, me * share)
     add_data((users, items, count, factors, words), shared, acc)
     partial_value = acc[...]
     zh, rh = total(partial_value * move[...]), total(partial_value * start[...])
@@ -125,8 +158,9 @@
     for index, value in enumerate(values):
         packed = jnp.where(lane == index, value, packed)
     scalars[...] = jnp.where(sublane == row, packed, 0.0)
-    for offset in range(parts):
-        outs[offset][...] = acc[pl.ds((me ^ offset) * share, share)]
+    for j in range(parts // 2):
+        keep[pl.ds(j * share, share)] = acc[pl.ds((me ^ (2 * j)) * share, share)]
+        send[pl.ds(j * share, share)] = acc[pl.ds((me ^ (2 * j + 1)) * share, share)]
     own_z[...] = move[pl.ds(me * share, share)]
     own_w[...] = image[pl.ds(me * share, share)]
 
@@ -163,7 +197,7 @@
     r, z, w = own_r[...], own_z[...], own_w[...]
     hz = ridge_weight * z
     for ref in images:
-        hz = hz + ref[...]
+        hz = hz + ref[: z.shape[0]]
     solution_ref[...] = (alpha + alpha_next * p) * r + (alpha_next * rho) * z
     residual_ref[...] = rest * r + rho * z - alpha_next * (p * w + rho * hz)
 
@@ -190,58 +224,71 @@
 ):
     share, rank, width = rhs.shape
     row_shape = (cols * share, rank, width)
-    cell = (
-        slot_users[0, 0],
-        slot_items[0, 0],
-        slot_counts,
-        item_factors,
-        mask_words[0, 0],
-        self_tiles,
-        next_tiles,
-    )
-    cell_specs = [SMEM] * 3 + [VMEM] * 4
+    half = jax.ShapeDtypeStruct((cols * share // 2, rank, width), f32)
+    piece = jax.ShapeDtypeStruct(rhs.shape, f32)
     params = pltpu.CompilerParams(vmem_limit_bytes=40 * 1024 * 1024)
     pieces = [rhs] + [exchange(rhs, "col", cols, offset) for offset in range(1, cols)]
-
-    value = pl.pallas_call(
+    words = mask_words[0, 0]
+    tile_shape = self_tiles.shape
+
+    factors, words, sym, edges, degrees = pl.pallas_call(
+        functools.partial(prepare_kernel, cols),
+        out_shape=[
+            jax.ShapeDtypeStruct(item_factors.shape, bf16),
+            jax.ShapeDtypeStruct(words.shape, words.dtype),
+            jax.ShapeDtypeStruct(tile_shape, bf16),
+            jax.ShapeDtypeStruct(tile_shape, bf16),
+            jax.ShapeDtypeStruct((tile_shape[0], 16, tile_shape[2]), f32),
+        ],
+        in_specs=[HBM] * 4,
+        out_specs=[VMEM] * 5,
+        scratch_shapes=[pltpu.VMEM((2,) + tile_shape, jnp.int32), pltpu.SemaphoreType.DMA((4,))],
+        compiler_params=params,
+        cost_estimate=pl.CostEstimate(flops=10**6, bytes_accessed=4 * 10**6, transcendentals=0),
+        name="prepare",
+    )(*(pltpu.with_memory_space_constraint(x, pltpu.HBM) for x in (item_factors, words, self_tiles, next_tiles)))
+    cell = (slot_users[0, 0], slot_items[0, 0], slot_counts, factors, words, sym, edges, degrees)
+    cell_specs = [SMEM] * 3 + [VMEM] * 5
+
+    keep, send = pl.pallas_call(
         functools.partial(first_kernel, cols),
-        out_shape=jax.ShapeDtypeStruct(row_shape, f32),
+        out_shape=[half, half],
         in_specs=cell_specs + [VMEM] * cols,
-        out_specs=VMEM,
-        scratch_shapes=[pltpu.VMEM(row_shape, bf16)],
+        out_specs=[VMEM] * 2,
+        scratch_shapes=[pltpu.VMEM(row_shape, bf16), pltpu.VMEM(row_shape, f32)],
         compiler_params=params,
         name="first_apply",
     )(*cell, *pieces)
-    bits = [1 << k for k in range(cols.bit_length() - 1)]
-    other = jnp.zeros_like(value) if not bits else None
-    for index, bit in enumerate(bits):
-        other = exchange(value, "col", cols, bit)
-        if index + 1 < len(bits):
-            value = value + other
+    keep = keep + exchange(send, "col", cols, 1)
+    bits = [1 << k for k in range(1, cols.bit_length() - 1)]
+    for bit in bits:
+        keep = keep + exchange(keep, "col", cols, bit)
+    theirs = exchange(keep, "col", cols, 1)
 
     height = -(-rows // 8) * 8
-    piece = jax.ShapeDtypeStruct(rhs.shape, f32)
-    outs = pl.pallas_call(
+    keep, send, table, own_z, own_w = pl.pallas_call(
         functools.partial(second_kernel, cols, height),
-        out_shape=[piece] * cols + [jax.ShapeDtypeStruct((height, 128), f32), piece, piece],
+        out_shape=[half, half, jax.ShapeDtypeStruct((height, 128), f32), piece, piece],
         in_specs=cell_specs + [VMEM] * (cols + 2),
-        out_specs=[VMEM] * (cols + 3),
+        out_specs=[VMEM] * 5,
         scratch_shapes=[pltpu.VMEM(row_shape, bf16)] + [pltpu.VMEM(row_shape, f32)] * 4,
         compiler_params=params,
         name="second_apply",
-    )(*cell, *pieces, value, other)
-    table, own_z, own_w = outs[cols:]
-    images = [outs[0]] + [exchange(outs[offset], "col", cols, offset) for offset in range(1, cols)]
-    groups = bit_groups(rows * cols)
+    )(*cell, *pieces, keep, theirs)
+    pair = exchange(send, "col", cols, 1)
+    images = [keep, pair]
+    for j in range(1, cols // 2):
+        block = slice(j * share, (j + 1) * share)
+        images.append(exchange(keep[block] + pair[block], "col", cols, 2 * j))
     tables = [table]
-    for group in groups:
+    for group in bit_groups(rows * cols):
         table = functools.reduce(jnp.add, tables)
         tables = [table] + [exchange(table, ("row", "col"), rows * cols, o) for o in spans(group)]
 
     return pl.pallas_call(
-        functools.partial(last_kernel, cols, len(tables)),
+        functools.partial(last_kernel, len(images), len(tables)),
         out_shape=[piece, piece],
-        in_specs=[VMEM] * (3 + cols + len(tables)),
+        in_specs=[VMEM] * (3 + len(images) + len(tables)),
         out_specs=[VMEM] * 2,
         compiler_params=params,
         name="last_update",

time: 45.4 us -> 40 us (0.88); the launches traced: 45 us -> 40.1 us
  local copies, waits for them, and re-layouts: 5.46 us -> 0.67 us
  waiting for transfers between devices: 15.5 us -> 12.7 us
  Pallas kernels: 3.9 us -> 5.35 us
  starting transfers between devices: 18.7 us -> 20 us
    unnamed x14 -> x6, local copies, waits for them, and re-layouts: 5.46 us -> 0.67 us
    ppermute x15, waiting for transfers between devices: 15.5 us -> 12.7 us  [exchange(): return lax.ppermute(value, axes, [(i, i ^ offset) for i in range(size)])]
    pallas_call x2 -> x3, Pallas kernels: 2.24 us -> 3.72 us  [the longest x1 1.57 us: per_device(): pl.pallas_call(functools.partial(prepare_kernel, cols), out_shape=[jax.Sh...]
    ppermute x15, starting transfers between devices: 18.7 us -> 20 us  [exchange(): return lax.ppermute(value, axes, [(i, i ^ offset) for i in range(size)])]
  transfers between devices with their start and end apart: 15 -> 15, of which waited for: 9 -> 8; matrix products, arithmetic and copies ran while one was open for 0% -> 0% of each run, Pallas kernels for 0% -> 4%
where the time goes in v2:
time: 40 us; the launch traced here: 40.1 us
  starting transfers between devices  20 us (50%)
  waiting for transfers between devices  12.7 us (32%)
  Pallas kernels  5.35 us (13%)
  between operations  1.37 us (3%)
  local copies, waits for them, and re-layouts  0.67 us (2%)
    ppermute x15, starting transfers between devices, exchange(): return lax.ppermute(value, axes, [(i, i ^ offset) for i in range(size)])  20 us
    ppermute x15, waiting for transfers between devices, exchange(): return lax.ppermute(value, axes, [(i, i ^ offset) for i in range(size)])  12.7 us
    pallas_call x1, Pallas kernels, per_device(): pl.pallas_call(functools.partial(second_kernel, cols, height), out_shape=...  1.63 us
    pallas_call x1, Pallas kernels, per_device(): pl.pallas_call(functools.partial(prepare_kernel, cols), out_shape=[jax.Sh...  1.57 us
    pallas_call x1, Pallas kernels, per_device(): pl.pallas_call(functools.partial(first_kernel, cols), out_shape=[half, ha...  1.29 us
    pallas_call x1, Pallas kernels, per_device(): pl.pallas_call(functools.partial(last_kernel, len(images), len(tables)),...  0.86 us
  transfers between devices with their start and end apart: 15, of which 8 were waited for; matrix products, arithmetic and copies ran while one was open for 0% of the time, Pallas kernels for 4%

profile of v2, /device:TPU:0, one launch (start us, length us, event | category | flops | bytes accessed | tf_op | source)
XLA Modules:
  0.0 40.1 jit_solution(11782484166041328563)
XLA Ops:
  0.6 2.5 %collective-permute-start.2 = (f32[1,64,128]{2,1,0:T(8,128)}, f32[1,64,128]{2,1,0:T(8,128)S(1)}, u32[]{:S(2)}, u32[]{:S(2)}) collective-permute-start(f32[1,64,128]{2,1,0:T(8,128)} %refs_0_.1), channel_id=1, source_target_pairs={{0,3},{1,2},{2,1},{3,0},{4,7},{5,6},{6,5},{7,4},{8,11},{9,10},{10,... | collective-permute-start | bytes 98312 | tf_op jit(solution)/shard_map/ppermute | solution.py:206
  3.1 0.6 %collective-permute-start.1 = (f32[1,64,128]{2,1,0:T(8,128)}, f32[1,64,128]{2,1,0:T(8,128)S(1)}, u32[]{:S(2)}, u32[]{:S(2)}) collective-permute-start(f32[1,64,128]{2,1,0:T(8,128)} %refs_0_.1), channel_id=1, source_target_pairs={{0,2},{1,3},{2,0},{3,1},{4,6},{5,7},{6,4},{7,5},{8,10},{9,11},{10,... | collective-permute-start | bytes 98312 | tf_op jit(solution)/shard_map/ppermute | solution.py:206
  3.7 0.0 collective-permute-start
  4.4 0.0 copy-start
  4.4 1.6 %prepare.1 = (bf16[64,64,128]{2,1,0:T(8,128)(2,1)S(1)}, s32[96,16,128]{2,1,0:T(8,128)S(1)}, bf16[1,128,128]{2,1,0:T(8,128)(2,1)S(1)}, bf16[1,128,128]{2,1,0:T(8,128)(2,1)S(1)}, f32[1,16,128]{2,1,0:T(8,128)S(1)}) custom-call(bf16[64,64,128]{2,1,0:T(8,128)(2,1)} %factors_in.1, s32[96,16,128]{2,1,0:T(8,128)} %bitcast.7, s32[1,128,128]{2,1,0:T(8,128)} %self_in.1, ...), custom_call_target="tpu_custom_call" | custom-call | flops 1000000 | bytes 4000000 | tf_op jit(solution)/shard_map/prepare/pallas_call | solution.py:234
  6.0 0.0 collective-permute-done.2.refs_11_
  6.0 1.3 %collective-permute-done.1.refs_10_ = f32[1,64,128]{2,1,0:T(8,128)S(1)} collective-permute-done((f32[1,64,128]{2,1,0:T(8,128)}, f32[1,64,128]{2,1,0:T(8,128)S(1)}, u32[]{:S(2)}, u32[]{:S(2)}) %collective-permute-start.1) | collective-permute-done | bytes 32800 | tf_op jit(solution)/shard_map/ppermute | solution.py:206
  7.3 0.0 collective-permute-done.refs_9_
  7.3 0.0 copy-start.1
  7.3 0.0 copy-start.2
  7.3 0.0 copy-done
  7.3 0.6 %copy-done.1 = s32[1,1,96]{2,1,0:T(1,128)S(1)} copy-done((s32[1,1,96]{2,1,0:T(1,128)S(1)}, s32[1,1,96]{2,1,0:T(1,128)}, u32[]{:S(2)}) %copy-start.1) | copy-done | bytes 408
  7.9 0.0 copy-done.2
  8.0 1.3 %first_apply.1 = (f32[2,64,128]{2,1,0:T(8,128)S(1)}, f32[2,64,128]{2,1,0:T(8,128)S(1)}) custom-call(s32[96]{0:T(128)S(1)} %bitcast.3, s32[96]{0:T(128)S(1)} %bitcast.5, s32[1,1]{1,0:T(1,128)S(6)} %copy.10.refs_2_, bf16[64,64,128]{2,1,0:T(8,128)(2,1)S(1)} %get-tuple-element.14.refs_3_, s32[96,16,128]{2,1,0:T(8,128)S(1)} %get-tuple-element.15.refs_4_, ...), custom_call_target="tpu_custom_call" | custom-call | tf_op jit(solution)/shard_map/first_apply/pallas_call | solution.py:253
  9.3 0.1 collective-permute-start.3
  9.3 1.2 %collective-permute-done.3 = f32[2,64,128]{2,1,0:T(8,128)S(1)} collective-permute-done((f32[2,64,128]{2,1,0:T(8,128)S(1)}, f32[2,64,128]{2,1,0:T(8,128)S(1)}, u32[]{:S(2)}, u32[]{:S(2)}) %collective-permute-start.3) | collective-permute-done | bytes 65568 | tf_op jit(solution)/shard_map/ppermute | solution.py:206
  10.6 1.6 %collective-permute-start.4 = (f32[2,64,128]{2,1,0:T(8,128)S(1)}, f32[2,64,128]{2,1,0:T(8,128)S(1)}, u32[]{:S(2)}, u32[]{:S(2)}) collective-permute-start(f32[2,64,128]{2,1,0:T(8,128)S(1)} %add.21), channel_id=1, source_target_pairs={{0,2},{1,3},{2,0},{3,1},{4,6},{5,7},{6,4},{7,5},{8,10},{9,11},{10,... | collective-permute-start | bytes 196616 | tf_op jit(solution)/shard_map/ppermute | solution.py:206
  12.2 2.7 %collective-permute-done.4 = f32[2,64,128]{2,1,0:T(8,128)S(1)} collective-permute-done((f32[2,64,128]{2,1,0:T(8,128)S(1)}, f32[2,64,128]{2,1,0:T(8,128)S(1)}, u32[]{:S(2)}, u32[]{:S(2)}) %collective-permute-start.4) | collective-permute-done | bytes 65568 | tf_op jit(solution)/shard_map/ppermute | solution.py:206
  14.9 0.1 collective-permute-start.5
  15.0 1.2 %collective-permute-done.5.refs_13_ = f32[2,64,128]{2,1,0:T(8,128)S(1)} collective-permute-done((f32[2,64,128]{2,1,0:T(8,128)S(1)}, f32[2,64,128]{2,1,0:T(8,128)S(1)}, u32[]{:S(2)}, u32[]{:S(2)}) %collective-permute-start.5) | collective-permute-done | bytes 65568 | tf_op jit(solution)/shard_map/ppermute | solution.py:206
  16.3 1.6 %second_apply.1 = (f32[2,64,128]{2,1,0:T(8,128)S(1)}, f32[2,64,128]{2,1,0:T(8,128)S(1)}, f32[8,128]{1,0:T(8,128)S(1)}, f32[1,64,128]{2,1,0:T(8,128)S(1)}, f32[1,64,128]{2,1,0:T(8,128)S(1)}) custom-call(s32[96]{0:T(128)S(1)} %bitcast.4, s32[96]{0:T(128)S(1)} %bitcast.6, s32[1,1]{1,0:T(1,128)S(6)} %copy.10.refs_2_, ...), custom_call_target="tpu_custom_call" | custom-call | tf_op jit(solution)/shard_map/second_apply/pallas_call | solution.py:269
  17.9 0.2 collective-permute-start.6
  18.1 0.4 collective-permute-start.8
  18.5 0.8 %collective-permute-done.8 = f32[8,128]{1,0:T(8,128)S(1)} collective-permute-done((f32[8,128]{1,0:T(8,128)S(1)}, f32[8,128]{1,0:T(8,128)S(1)}, u32[]{:S(2)}, u32[]{:S(2)}) %collective-permute-start.8) | collective-permute-done | bytes 4128 | tf_op jit(solution)/shard_map/ppermute | solution.py:206
  19.3 4.0 %collective-permute-start.11 = (f32[8,128]{1,0:T(8,128)S(1)}, f32[8,128]{1,0:T(8,128)S(1)}, u32[]{:S(2)}, u32[]{:S(2)}) collective-permute-start(f32[8,128]{1,0:T(8,128)S(1)} %add.24), channel_id=1, source_target_pairs={{0,6},{1,7},{2,4},{3,5},{4,2},{5,3},{6,0},{7,1},{8,14},{9,15},{10,... | collective-permute-start | bytes 12296 | tf_op jit(solution)/shard_map/ppermute | solution.py:206
  23.3 0.0 collective-permute-start.10
  23.4 1.2 %collective-permute-start.9 = (f32[8,128]{1,0:T(8,128)S(1)}, f32[8,128]{1,0:T(8,128)S(1)}, u32[]{:S(2)}, u32[]{:S(2)}) collective-permute-start(f32[8,128]{1,0:T(8,128)S(1)} %add.24), channel_id=1, source_target_pairs={{0,2},{1,3},{2,0},{3,1},{4,6},{5,7},{6,4},{7,5},{8,10},{9,11},{10,... | collective-permute-start | bytes 12296 | tf_op jit(solution)/shard_map/ppermute | solution.py:206
  24.6 0.0 collective-permute-done.6.refs_4_
  24.6 0.9 %collective-permute-start.7 = (f32[1,64,128]{2,1,0:T(8,128)S(1)}, f32[1,64,128]{2,1,0:T(8,128)S(1)}, u32[]{:S(2)}, u32[]{:S(2)}) collective-permute-start(f32[1,64,128]{2,1,0:T(8,128)S(1)} %slice_add_fusion), channel_id=1, source_target_pairs={{0,2},{1,3},{2,0},{3,1},{4,6},{5,7},{6,4},{7,5},{8,10},{9,11},{10,... | collective-permute-start | bytes 98312 | tf_op jit(solution)/shard_map/ppermute | solution.py:206
  25.5 0.0 collective-permute-done.11
  25.5 1.5 %collective-permute-done.10 = f32[8,128]{1,0:T(8,128)S(1)} collective-permute-done((f32[8,128]{1,0:T(8,128)S(1)}, f32[8,128]{1,0:T(8,128)S(1)}, u32[]{:S(2)}, u32[]{:S(2)}) %collective-permute-start.10) | collective-permute-done | bytes 4128 | tf_op jit(solution)/shard_map/ppermute | solution.py:206
  27.0 0.0 collective-permute-done.9
  27.0 7.8 %collective-permute-start.14 = (f32[8,128]{1,0:T(8,128)S(1)}, f32[8,128]{1,0:T(8,128)S(1)}, u32[]{:S(2)}, u32[]{:S(2)}) collective-permute-start(f32[8,128]{1,0:T(8,128)S(1)} %add_add_fusion.refs_6_), channel_id=1, source_target_pairs={{0,24},{1,25},{2,26},{3,27},{4,28},{5,29},{6,30},{7,31},{8,16},{9,... | collective-permute-start | bytes 12296 | tf_op jit(solution)/shard_map/ppermute | solution.py:206
  34.7 0.0 collective-permute-start.13
  34.7 0.6 %collective-permute-start.12 = (f32[8,128]{1,0:T(8,128)S(1)}, f32[8,128]{1,0:T(8,128)S(1)}, u32[]{:S(2)}, u32[]{:S(2)}) collective-permute-start(f32[8,128]{1,0:T(8,128)S(1)} %add_add_fusion.refs_6_), channel_id=1, source_target_pairs={{0,8},{1,9},{2,10},{3,11},{4,12},{5,13},{6,14},{7,15},{8,0},{9,1},... | collective-permute-start | bytes 12296 | tf_op jit(solution)/shard_map/ppermute | solution.py:206
  35.4 0.9 %collective-permute-done.14.refs_9_ = f32[8,128]{1,0:T(8,128)S(1)} collective-permute-done((f32[8,128]{1,0:T(8,128)S(1)}, f32[8,128]{1,0:T(8,128)S(1)}, u32[]{:S(2)}, u32[]{:S(2)}) %collective-permute-start.14) | collective-permute-done | bytes 4128 | tf_op jit(solution)/shard_map/ppermute | solution.py:206
  36.3 2.9 %collective-permute-done.13.refs_8_ = f32[8,128]{1,0:T(8,128)S(1)} collective-permute-done((f32[8,128]{1,0:T(8,128)S(1)}, f32[8,128]{1,0:T(8,128)S(1)}, u32[]{:S(2)}, u32[]{:S(2)}) %collective-permute-start.13) | collective-permute-done | bytes 4128 | tf_op jit(solution)/shard_map/ppermute | solution.py:206
  39.2 0.0 collective-permute-done.12.refs_7_
  39.2 0.0 collective-permute-done.7.refs_5_
  39.3 0.9 %last_update.1 = (f32[1,64,128]{2,1,0:T(8,128)}, f32[1,64,128]{2,1,0:T(8,128)}) custom-call(f32[1,64,128]{2,1,0:T(8,128)S(1)} %copy-done, f32[1,64,128]{2,1,0:T(8,128)S(1)} %get-tuple-element.21.refs_1_, f32[1,64,128]{2,1,0:T(8,128)S(1)} %get-tuple-element.22.refs_2_, f32[2,64,128]{2,1,0:T(8,128)S(1)} %get-tuple-element.23.refs_3_, ...), custom_call_target="tpu_custom_call" | custom-call | tf_op jit(solution)/shard_map/last_update/pallas_call | solution.py:288
  (5 shorter events, 0.0 us)
Async XLA Ops:
  0.6 5.4 %collective-permute-start.2 = (f32[1,64,128]{2,1,0:T(8,128)}, f32[1,64,128]{2,1,0:T(8,128)S(1)}, u32[]{:S(2)}, u32[]{:S(2)}) collective-permute-start(f32[1,64,128]{2,1,0:T(8,128)} %refs_0_.1), channel_id=1, source_target_pairs={{0,3},{1,2},{2,1},{3,0},{4,7},{5,6},{6,5},{7,4},{8,11},{9,10},{10,... | collective-permute-start | bytes 98312 | tf_op jit(solution)/shard_map/ppermute | solution.py:206
  3.1 4.2 %collective-permute-start.1 = (f32[1,64,128]{2,1,0:T(8,128)}, f32[1,64,128]{2,1,0:T(8,128)S(1)}, u32[]{:S(2)}, u32[]{:S(2)}) collective-permute-start(f32[1,64,128]{2,1,0:T(8,128)} %refs_0_.1), channel_id=1, source_target_pairs={{0,2},{1,3},{2,0},{3,1},{4,6},{5,7},{6,4},{7,5},{8,10},{9,11},{10,... | collective-permute-start | bytes 98312 | tf_op jit(solution)/shard_map/ppermute | solution.py:206
  3.7 3.5 %collective-permute-start = (f32[1,64,128]{2,1,0:T(8,128)}, f32[1,64,128]{2,1,0:T(8,128)S(1)}, u32[]{:S(2)}, u32[]{:S(2)}) collective-permute-start(f32[1,64,128]{2,1,0:T(8,128)} %refs_0_.1), channel_id=1, source_target_pairs={{0,1},{1,0},{2,3},{3,2},{4,5},{5,4},{6,7},{7,6},{8,9},{9,8},{10,11... | collective-permute-start | bytes 98312 | tf_op jit(solution)/shard_map/ppermute | solution.py:206
  4.4 2.9 %copy-start = (f32[1,64,128]{2,1,0:T(8,128)S(1)}, f32[1,64,128]{2,1,0:T(8,128)}, u32[]{:S(2)}) copy-start(f32[1,64,128]{2,1,0:T(8,128)} %refs_0_.1) | copy-start | bytes 98308
  7.3 0.7 %copy-start.1 = (s32[1,1,96]{2,1,0:T(1,128)S(1)}, s32[1,1,96]{2,1,0:T(1,128)}, u32[]{:S(2)}) copy-start(s32[1,1,96]{2,1,0:T(1,128)} %param.10) | copy-start | bytes 1156
  7.3 0.7 %copy-start.2 = (s32[1,1,96]{2,1,0:T(1,128)S(1)}, s32[1,1,96]{2,1,0:T(1,128)}, u32[]{:S(2)}) copy-start(s32[1,1,96]{2,1,0:T(1,128)} %param.11) | copy-start | bytes 1156
  9.3 1.3 %collective-permute-start.3 = (f32[2,64,128]{2,1,0:T(8,128)S(1)}, f32[2,64,128]{2,1,0:T(8,128)S(1)}, u32[]{:S(2)}, u32[]{:S(2)}) collective-permute-start(f32[2,64,128]{2,1,0:T(8,128)S(1)} %get-tuple-element.20), channel_id=1, source_target_pairs={{0,1},{1,0},{2,3},{3,2},{4,5},{5,4},{6,7},{7,6},{8,9},{9,8},{10,11... | collective-permute-start | bytes 196616 | tf_op jit(solution)/shard_map/ppermute | solution.py:206
  10.6 4.3 %collective-permute-start.4 = (f32[2,64,128]{2,1,0:T(8,128)S(1)}, f32[2,64,128]{2,1,0:T(8,128)S(1)}, u32[]{:S(2)}, u32[]{:S(2)}) collective-permute-start(f32[2,64,128]{2,1,0:T(8,128)S(1)} %add.21), channel_id=1, source_target_pairs={{0,2},{1,3},{2,0},{3,1},{4,6},{5,7},{6,4},{7,5},{8,10},{9,11},{10,... | collective-permute-start | bytes 196616 | tf_op jit(solution)/shard_map/ppermute | solution.py:206
  14.9 1.3 %collective-permute-start.5 = (f32[2,64,128]{2,1,0:T(8,128)S(1)}, f32[2,64,128]{2,1,0:T(8,128)S(1)}, u32[]{:S(2)}, u32[]{:S(2)}) collective-permute-start(f32[2,64,128]{2,1,0:T(8,128)S(1)} %add.22.refs_12_), channel_id=1, source_target_pairs={{0,1},{1,0},{2,3},{3,2},{4,5},{5,4},{6,7},{7,6},{8,9},{9,8},{10,11... | collective-permute-start | bytes 196616 | tf_op jit(solution)/shard_map/ppermute | solution.py:206
  17.9 6.7 %collective-permute-start.6 = (f32[2,64,128]{2,1,0:T(8,128)S(1)}, f32[2,64,128]{2,1,0:T(8,128)S(1)}, u32[]{:S(2)}, u32[]{:S(2)}) collective-permute-start(f32[2,64,128]{2,1,0:T(8,128)S(1)} %get-tuple-element.24), channel_id=1, source_target_pairs={{0,1},{1,0},{2,3},{3,2},{4,5},{5,4},{6,7},{7,6},{8,9},{9,8},{10,11... | collective-permute-start | bytes 196616 | tf_op jit(solution)/shard_map/ppermute | solution.py:206
  18.1 1.2 %collective-permute-start.8 = (f32[8,128]{1,0:T(8,128)S(1)}, f32[8,128]{1,0:T(8,128)S(1)}, u32[]{:S(2)}, u32[]{:S(2)}) collective-permute-start(f32[8,128]{1,0:T(8,128)S(1)} %get-tuple-element.25), channel_id=1, source_target_pairs={{0,1},{1,0},{2,3},{3,2},{4,5},{5,4},{6,7},{7,6},{8,9},{9,8},{10,11... | collective-permute-start | bytes 12296 | tf_op jit(solution)/shard_map/ppermute | solution.py:206
  19.3 6.2 %collective-permute-start.11 = (f32[8,128]{1,0:T(8,128)S(1)}, f32[8,128]{1,0:T(8,128)S(1)}, u32[]{:S(2)}, u32[]{:S(2)}) collective-permute-start(f32[8,128]{1,0:T(8,128)S(1)} %add.24), channel_id=1, source_target_pairs={{0,6},{1,7},{2,4},{3,5},{4,2},{5,3},{6,0},{7,1},{8,14},{9,15},{10,... | collective-permute-start | bytes 12296 | tf_op jit(solution)/shard_map/ppermute | solution.py:206
  23.3 3.6 %collective-permute-start.10 = (f32[8,128]{1,0:T(8,128)S(1)}, f32[8,128]{1,0:T(8,128)S(1)}, u32[]{:S(2)}, u32[]{:S(2)}) collective-permute-start(f32[8,128]{1,0:T(8,128)S(1)} %add.24), channel_id=1, source_target_pairs={{0,4},{1,5},{2,6},{3,7},{4,0},{5,1},{6,2},{7,3},{8,12},{9,13},{10,... | collective-permute-start | bytes 12296 | tf_op jit(solution)/shard_map/ppermute | solution.py:206
  23.4 3.6 %collective-permute-start.9 = (f32[8,128]{1,0:T(8,128)S(1)}, f32[8,128]{1,0:T(8,128)S(1)}, u32[]{:S(2)}, u32[]{:S(2)}) collective-permute-start(f32[8,128]{1,0:T(8,128)S(1)} %add.24), channel_id=1, source_target_pairs={{0,2},{1,3},{2,0},{3,1},{4,6},{5,7},{6,4},{7,5},{8,10},{9,11},{10,... | collective-permute-start | bytes 12296 | tf_op jit(solution)/shard_map/ppermute | solution.py:206
  24.6 14.7 %collective-permute-start.7 = (f32[1,64,128]{2,1,0:T(8,128)S(1)}, f32[1,64,128]{2,1,0:T(8,128)S(1)}, u32[]{:S(2)}, u32[]{:S(2)}) collective-permute-start(f32[1,64,128]{2,1,0:T(8,128)S(1)} %slice_add_fusion), channel_id=1, source_target_pairs={{0,2},{1,3},{2,0},{3,1},{4,6},{5,7},{6,4},{7,5},{8,10},{9,11},{10,... | collective-permute-start | bytes 98312 | tf_op jit(solution)/shard_map/ppermute | solution.py:206
  27.0 9.4 %collective-permute-start.14 = (f32[8,128]{1,0:T(8,128)S(1)}, f32[8,128]{1,0:T(8,128)S(1)}, u32[]{:S(2)}, u32[]{:S(2)}) collective-permute-start(f32[8,128]{1,0:T(8,128)S(1)} %add_add_fusion.refs_6_), channel_id=1, source_target_pairs={{0,24},{1,25},{2,26},{3,27},{4,28},{5,29},{6,30},{7,31},{8,16},{9,... | collective-permute-start | bytes 12296 | tf_op jit(solution)/shard_map/ppermute | solution.py:206
  34.7 4.5 %collective-permute-start.13 = (f32[8,128]{1,0:T(8,128)S(1)}, f32[8,128]{1,0:T(8,128)S(1)}, u32[]{:S(2)}, u32[]{:S(2)}) collective-permute-start(f32[8,128]{1,0:T(8,128)S(1)} %add_add_fusion.refs_6_), channel_id=1, source_target_pairs={{0,16},{1,17},{2,18},{3,19},{4,20},{5,21},{6,22},{7,23},{8,24},{9,... | collective-permute-start | bytes 12296 | tf_op jit(solution)/shard_map/ppermute | solution.py:206
  34.7 4.5 %collective-permute-start.12 = (f32[8,128]{1,0:T(8,128)S(1)}, f32[8,128]{1,0:T(8,128)S(1)}, u32[]{:S(2)}, u32[]{:S(2)}) collective-permute-start(f32[8,128]{1,0:T(8,128)S(1)} %add_add_fusion.refs_6_), channel_id=1, source_target_pairs={{0,8},{1,9},{2,10},{3,11},{4,12},{5,13},{6,14},{7,15},{8,0},{9,1},... | collective-permute-start | bytes 12296 | tf_op jit(solution)/shard_map/ppermute | solution.py:206

commit v3 on v2

--- a/solution.py
+++ b/solution.py
@@ -9,7 +9,7 @@
 
 graph_weight = 0.01
 ridge_weight = 0.5
-unroll = 16
+unroll = 96
 f32 = jnp.float32
 bf16 = jnp.bfloat16
 
@@ -25,7 +25,8 @@
 def add_data(cell, shared, acc):
     users, items, count_ref, factors, words = cell
     count = count_ref[0, 0]
-    group = unroll if users.shape[0] % unroll == 0 else 1
+    slots = users.shape[0]
+    group = max(k for k in range(1, unroll + 1) if slots % k == 0)
     bit = jnp.left_shift(1, lax.broadcasted_iota(jnp.int32, (8, words.shape[2]), 0))
 
     def turn(index, carry):
@@ -41,7 +42,10 @@
             acc[user] += dot(left, tile, (1, 0))
         return carry
 
-    lax.fori_loop(0, (count + group - 1) // group, turn, 0)
+    if group == slots:
+        turn(0, 0)
+    else:
+        lax.fori_loop(0, (count + group - 1) // group, turn, 0)
 
 
 def add_graph(graph, shared, acc, first):
@@ -58,12 +62,21 @@
         acc[after] += graph_weight * there
 
 
-def prepare_kernel(cols, factors_in, words_in, self_in, next_in, factors, words, sym, edges, degrees, tiles, sems):
+def prepare_kernel(cols, *refs):
+    factors_in, words_in, users_in, items_in, self_in, next_in = refs[:6]
+    factors, words, users, items, sym, edges, degrees, tiles, sems = refs[6:]
     first = lax.axis_index("col") * self_in.shape[0]
     copies = [
         pltpu.make_async_copy(source, target, sems.at[k])
         for k, (source, target) in enumerate(
-            ((self_in, tiles.at[0]), (next_in, tiles.at[1]), (factors_in, factors), (words_in, words))
+            (
+                (self_in, tiles.at[0]),
+                (next_in, tiles.at[1]),
+                (factors_in, factors),
+                (words_in, words),
+                (users_in, users),
+                (items_in, items),
+            )
         )
     ]
     for copy in copies:
@@ -82,8 +95,8 @@
         ones = jnp.ones((8, both.shape[0]), bf16)
         degrees[j, 0:8] = jnp.sum(both, axis=0, keepdims=True) + dot(ones, edges_b, (1, 1))
         degrees[j, 8:16] = jnp.broadcast_to(jnp.sum(edge, axis=0, keepdims=True), (8, both.shape[1]))
-    copies[2].wait()
-    copies[3].wait()
+    for copy in copies[2:]:
+        copy.wait()
 
 
 def total(value):
@@ -231,23 +244,26 @@
     words = mask_words[0, 0]
     tile_shape = self_tiles.shape
 
-    factors, words, sym, edges, degrees = pl.pallas_call(
+    users, items = slot_users[0, 0], slot_items[0, 0]
+    factors, words, users, items, sym, edges, degrees = pl.pallas_call(
         functools.partial(prepare_kernel, cols),
         out_shape=[
             jax.ShapeDtypeStruct(item_factors.shape, bf16),
             jax.ShapeDtypeStruct(words.shape, words.dtype),
+            jax.ShapeDtypeStruct(users.shape, users.dtype),
+            jax.ShapeDtypeStruct(items.shape, items.dtype),
             jax.ShapeDtypeStruct(tile_shape, bf16),
             jax.ShapeDtypeStruct(tile_shape, bf16),
             jax.ShapeDtypeStruct((tile_shape[0], 16, tile_shape[2]), f32),
         ],
-        in_specs=[HBM] * 4,
-        out_specs=[VMEM] * 5,
-        scratch_shapes=[pltpu.VMEM((2,) + tile_shape, jnp.int32), pltpu.SemaphoreType.DMA((4,))],
+        in_specs=[HBM] * 6,
+        out_specs=[VMEM] * 2 + [SMEM] * 2 + [VMEM] * 3,
+        scratch_shapes=[pltpu.VMEM((2,) + tile_shape, jnp.int32), pltpu.SemaphoreType.DMA((6,))],
         compiler_params=params,
         cost_estimate=pl.CostEstimate(flops=10**6, bytes_accessed=4 * 10**6, transcendentals=0),
         name="prepare",
-    )(*(pltpu.with_memory_space_constraint(x, pltpu.HBM) for x in (item_factors, words, self_tiles, next_tiles)))
-    cell = (slot_users[0, 0], slot_items[0, 0], slot_counts, factors, words, sym, edges, degrees)
+    )(*(pltpu.with_memory_space_constraint(x, pltpu.HBM) for x in (item_factors, words, users, items, self_tiles, next_tiles)))
+    cell = (users, items, slot_counts, factors, words, sym, edges, degrees)
     cell_specs = [SMEM] * 3 + [VMEM] * 5
 
     keep, send = pl.pallas_call(

time: 40 us -> 36.5 us (0.912)
  starting transfers between devices: 20 us -> 14.2 us
  Pallas kernels: 5.35 us -> 8.52 us
  local copies, waits for them, and re-layouts: 0.67 us -> 0.01 us
    ppermute x15, starting transfers between devices: 20 us -> 14.2 us  [exchange(): return lax.ppermute(value, axes, [(i, i ^ offset) for i in range(size)])]
    pallas_call x1, Pallas kernels: 1.63 us -> 2.91 us  [per_device(): pl.pallas_call(functools.partial(second_kernel, cols, height), out_shape=...]
    pallas_call x1, Pallas kernels: 1.29 us -> 2.55 us  [per_device(): pl.pallas_call(functools.partial(first_kernel, cols), out_shape=[half, ha...]
    unnamed x6 -> x2, local copies, waits for them, and re-layouts: 0.67 us -> 0.01 us
    pallas_call x1, Pallas kernels: 1.57 us -> 2.2 us  [per_device(): pl.pallas_call(functools.partial(prepare_kernel, cols), out_shape=[jax.Sh...]
  transfers between devices with their start and end apart: 15 -> 15, of which waited for: 8 -> 9; matrix products, arithmetic and copies ran while one was open for 0% -> 0% of each run, Pallas kernels for 4% -> 6%
where the time goes in v3:
time: 36.5 us; the launch traced here: 36.4 us
  starting transfers between devices  14.2 us (39%)
  waiting for transfers between devices  12.3 us (34%)
  Pallas kernels  8.52 us (23%)
  between operations  1.37 us (4%)
    ppermute x15, starting transfers between devices, exchange(): return lax.ppermute(value, axes, [(i, i ^ offset) for i in range(size)])  14.2 us
    ppermute x15, waiting for transfers between devices, exchange(): return lax.ppermute(value, axes, [(i, i ^ offset) for i in range(size)])  12.3 us
    pallas_call x1, Pallas kernels, per_device(): pl.pallas_call(functools.partial(second_kernel, cols, height), out_shape=...  2.91 us
    pallas_call x1, Pallas kernels, per_device(): pl.pallas_call(functools.partial(first_kernel, cols), out_shape=[half, ha...  2.55 us
    pallas_call x1, Pallas kernels, per_device(): pl.pallas_call(functools.partial(prepare_kernel, cols), out_shape=[jax.Sh...  2.2 us
    pallas_call x1, Pallas kernels, per_device(): pl.pallas_call(functools.partial(last_kernel, len(images), len(tables)),...  0.86 us
  transfers between devices with their start and end apart: 15, of which 9 were waited for; matrix products, arithmetic and copies ran while one was open for 0% of the time, Pallas kernels for 6%

profile of v3, /device:TPU:0, one launch (start us, length us, event | category | flops | bytes accessed | tf_op | source)
XLA Modules:
  0.0 36.4 jit_solution(11224131875941136728)
XLA Ops:
  0.6 2.5 %collective-permute-start.2 = (f32[1,64,128]{2,1,0:T(8,128)}, f32[1,64,128]{2,1,0:T(8,128)S(1)}, u32[]{:S(2)}, u32[]{:S(2)}) collective-permute-start(f32[1,64,128]{2,1,0:T(8,128)} %refs_0_.3), channel_id=1, source_target_pairs={{0,3},{1,2},{2,1},{3,0},{4,7},{5,6},{6,5},{7,4},{8,11},{9,10},{10,... | collective-permute-start | bytes 98312 | tf_op jit(solution)/shard_map/ppermute | solution.py:219
  3.1 0.6 %collective-permute-start.1 = (f32[1,64,128]{2,1,0:T(8,128)}, f32[1,64,128]{2,1,0:T(8,128)S(1)}, u32[]{:S(2)}, u32[]{:S(2)}) collective-permute-start(f32[1,64,128]{2,1,0:T(8,128)} %refs_0_.3), channel_id=1, source_target_pairs={{0,2},{1,3},{2,0},{3,1},{4,6},{5,7},{6,4},{7,5},{8,10},{9,11},{10,... | collective-permute-start | bytes 98312 | tf_op jit(solution)/shard_map/ppermute | solution.py:219
  3.7 0.0 collective-permute-start
  4.4 0.0 copy-start
  4.4 2.2 %prepare.1 = (bf16[64,64,128]{2,1,0:T(8,128)(2,1)S(1)}, s32[96,16,128]{2,1,0:T(8,128)S(1)}, s32[96]{0:T(128)S(1)}, s32[96]{0:T(128)S(1)}, bf16[1,128,128]{2,1,0:...) custom-call(bf16[64,64,128]{2,1,0:T(8,128)(2,1)} %refs_0_.2, s32[96,16,128]{2,1,0:T(8,128)} %bitcast.3, ...), custom_call_target="tpu_custom_call" | custom-call | flops 1000000 | bytes 4000000 | tf_op jit(solution)/shard_map/prepare/pallas_call | solution.py:248
  6.7 0.0 collective-permute-done.2.refs_11_
  6.7 0.6 %collective-permute-done.1.refs_10_ = f32[1,64,128]{2,1,0:T(8,128)S(1)} collective-permute-done((f32[1,64,128]{2,1,0:T(8,128)}, f32[1,64,128]{2,1,0:T(8,128)S(1)}, u32[]{:S(2)}, u32[]{:S(2)}) %collective-permute-start.1) | collective-permute-done | bytes 32800 | tf_op jit(solution)/shard_map/ppermute | solution.py:219
  7.3 0.0 collective-permute-done.refs_9_
  7.3 0.0 copy-done
  7.3 2.5 %first_apply.1 = (f32[2,64,128]{2,1,0:T(8,128)S(1)}, f32[2,64,128]{2,1,0:T(8,128)S(1)}) custom-call(s32[96]{0:T(128)S(1)} %get-tuple-element.16.refs_0_, s32[96]{0:T(128)S(1)} %get-tuple-element.17.refs_1_, s32[1,1]{1,0:T(1,128)S(6)} %copy.10.refs_2_, bf16[64,64,128]{2,1,0:T(8,128)(2,1)S(1)} %get-tuple-element.18.refs_3_, ...), custom_call_target="tpu_custom_call" | custom-call | tf_op jit(solution)/shard_map/first_apply/pallas_call | solution.py:269
  9.9 0.1 collective-permute-start.3
  9.9 1.2 %collective-permute-done.3 = f32[2,64,128]{2,1,0:T(8,128)S(1)} collective-permute-done((f32[2,64,128]{2,1,0:T(8,128)S(1)}, f32[2,64,128]{2,1,0:T(8,128)S(1)}, u32[]{:S(2)}, u32[]{:S(2)}) %collective-permute-start.3) | collective-permute-done | bytes 65568 | tf_op jit(solution)/shard_map/ppermute | solution.py:219
  11.2 1.2 %collective-permute-start.4 = (f32[2,64,128]{2,1,0:T(8,128)S(1)}, f32[2,64,128]{2,1,0:T(8,128)S(1)}, u32[]{:S(2)}, u32[]{:S(2)}) collective-permute-start(f32[2,64,128]{2,1,0:T(8,128)S(1)} %add.21), channel_id=1, source_target_pairs={{0,2},{1,3},{2,0},{3,1},{4,6},{5,7},{6,4},{7,5},{8,10},{9,11},{10,... | collective-permute-start | bytes 196616 | tf_op jit(solution)/shard_map/ppermute | solution.py:219
  12.4 3.1 %collective-permute-done.4 = f32[2,64,128]{2,1,0:T(8,128)S(1)} collective-permute-done((f32[2,64,128]{2,1,0:T(8,128)S(1)}, f32[2,64,128]{2,1,0:T(8,128)S(1)}, u32[]{:S(2)}, u32[]{:S(2)}) %collective-permute-start.4) | collective-permute-done | bytes 65568 | tf_op jit(solution)/shard_map/ppermute | solution.py:219
  15.5 0.1 collective-permute-start.5
  15.6 1.2 %collective-permute-done.5.refs_13_ = f32[2,64,128]{2,1,0:T(8,128)S(1)} collective-permute-done((f32[2,64,128]{2,1,0:T(8,128)S(1)}, f32[2,64,128]{2,1,0:T(8,128)S(1)}, u32[]{:S(2)}, u32[]{:S(2)}) %collective-permute-start.5) | collective-permute-done | bytes 65568 | tf_op jit(solution)/shard_map/ppermute | solution.py:219
  16.8 2.9 %second_apply.1 = (f32[2,64,128]{2,1,0:T(8,128)S(1)}, f32[2,64,128]{2,1,0:T(8,128)S(1)}, f32[8,128]{1,0:T(8,128)S(1)}, f32[1,64,128]{2,1,0:T(8,128)S(1)}, f32[1,64,128]{2,1,0:T(8,128)S(1)}) custom-call(s32[96]{0:T(128)S(1)} %get-tuple-element.16.refs_0_, s32[96]{0:T(128)S(1)} %get-tuple-element.17.refs_1_, s32[1,1]{1,0:T(1,128)S(6)} %copy.10.refs_2_, ...), custom_call_target="tpu_custom_call" | custom-call | tf_op jit(solution)/shard_map/second_apply/pallas_call | solution.py:285
  19.8 0.2 collective-permute-start.6
  20.0 0.4 collective-permute-start.8
  20.3 0.8 %collective-permute-done.8 = f32[8,128]{1,0:T(8,128)S(1)} collective-permute-done((f32[8,128]{1,0:T(8,128)S(1)}, f32[8,128]{1,0:T(8,128)S(1)}, u32[]{:S(2)}, u32[]{:S(2)}) %collective-permute-start.8) | collective-permute-done | bytes 4128 | tf_op jit(solution)/shard_map/ppermute | solution.py:219
  21.2 2.1 %collective-permute-start.11 = (f32[8,128]{1,0:T(8,128)S(1)}, f32[8,128]{1,0:T(8,128)S(1)}, u32[]{:S(2)}, u32[]{:S(2)}) collective-permute-start(f32[8,128]{1,0:T(8,128)S(1)} %add.24), channel_id=1, source_target_pairs={{0,6},{1,7},{2,4},{3,5},{4,2},{5,3},{6,0},{7,1},{8,14},{9,15},{10,... | collective-permute-start | bytes 12296 | tf_op jit(solution)/shard_map/ppermute | solution.py:219
  23.2 0.5 %collective-permute-start.10 = (f32[8,128]{1,0:T(8,128)S(1)}, f32[8,128]{1,0:T(8,128)S(1)}, u32[]{:S(2)}, u32[]{:S(2)}) collective-permute-start(f32[8,128]{1,0:T(8,128)S(1)} %add.24), channel_id=1, source_target_pairs={{0,4},{1,5},{2,6},{3,7},{4,0},{5,1},{6,2},{7,3},{8,12},{9,13},{10,... | collective-permute-start | bytes 12296 | tf_op jit(solution)/shard_map/ppermute | solution.py:219
  23.8 0.9 %collective-permute-start.9 = (f32[8,128]{1,0:T(8,128)S(1)}, f32[8,128]{1,0:T(8,128)S(1)}, u32[]{:S(2)}, u32[]{:S(2)}) collective-permute-start(f32[8,128]{1,0:T(8,128)S(1)} %add.24), channel_id=1, source_target_pairs={{0,2},{1,3},{2,0},{3,1},{4,6},{5,7},{6,4},{7,5},{8,10},{9,11},{10,... | collective-permute-start | bytes 12296 | tf_op jit(solution)/shard_map/ppermute | solution.py:219
  24.7 0.0 collective-permute-done.6.refs_4_
  24.7 1.2 %collective-permute-start.7 = (f32[1,64,128]{2,1,0:T(8,128)S(1)}, f32[1,64,128]{2,1,0:T(8,128)S(1)}, u32[]{:S(2)}, u32[]{:S(2)}) collective-permute-start(f32[1,64,128]{2,1,0:T(8,128)S(1)} %slice_add_fusion), channel_id=1, source_target_pairs={{0,2},{1,3},{2,0},{3,1},{4,6},{5,7},{6,4},{7,5},{8,10},{9,11},{10,... | collective-permute-start | bytes 98312 | tf_op jit(solution)/shard_map/ppermute | solution.py:219
  25.9 0.0 collective-permute-done.11
  25.9 1.0 %collective-permute-done.10 = f32[8,128]{1,0:T(8,128)S(1)} collective-permute-done((f32[8,128]{1,0:T(8,128)S(1)}, f32[8,128]{1,0:T(8,128)S(1)}, u32[]{:S(2)}, u32[]{:S(2)}) %collective-permute-start.10) | collective-permute-done | bytes 4128 | tf_op jit(solution)/shard_map/ppermute | solution.py:219
  26.8 0.5 %collective-permute-done.9 = f32[8,128]{1,0:T(8,128)S(1)} collective-permute-done((f32[8,128]{1,0:T(8,128)S(1)}, f32[8,128]{1,0:T(8,128)S(1)}, u32[]{:S(2)}, u32[]{:S(2)}) %collective-permute-start.9) | collective-permute-done | bytes 4128 | tf_op jit(solution)/shard_map/ppermute | solution.py:219
  27.4 3.6 %collective-permute-start.14 = (f32[8,128]{1,0:T(8,128)S(1)}, f32[8,128]{1,0:T(8,128)S(1)}, u32[]{:S(2)}, u32[]{:S(2)}) collective-permute-start(f32[8,128]{1,0:T(8,128)S(1)} %add_add_fusion.refs_6_), channel_id=1, source_target_pairs={{0,24},{1,25},{2,26},{3,27},{4,28},{5,29},{6,30},{7,31},{8,16},{9,... | collective-permute-start | bytes 12296 | tf_op jit(solution)/shard_map/ppermute | solution.py:219
  31.0 0.0 collective-permute-start.13
  31.0 0.8 %collective-permute-start.12 = (f32[8,128]{1,0:T(8,128)S(1)}, f32[8,128]{1,0:T(8,128)S(1)}, u32[]{:S(2)}, u32[]{:S(2)}) collective-permute-start(f32[8,128]{1,0:T(8,128)S(1)} %add_add_fusion.refs_6_), channel_id=1, source_target_pairs={{0,8},{1,9},{2,10},{3,11},{4,12},{5,13},{6,14},{7,15},{8,0},{9,1},... | collective-permute-start | bytes 12296 | tf_op jit(solution)/shard_map/ppermute | solution.py:219
  31.8 1.0 %collective-permute-done.14.refs_9_ = f32[8,128]{1,0:T(8,128)S(1)} collective-permute-done((f32[8,128]{1,0:T(8,128)S(1)}, f32[8,128]{1,0:T(8,128)S(1)}, u32[]{:S(2)}, u32[]{:S(2)}) %collective-permute-start.14) | collective-permute-done | bytes 4128 | tf_op jit(solution)/shard_map/ppermute | solution.py:219
  32.8 2.7 %collective-permute-done.13.refs_8_ = f32[8,128]{1,0:T(8,128)S(1)} collective-permute-done((f32[8,128]{1,0:T(8,128)S(1)}, f32[8,128]{1,0:T(8,128)S(1)}, u32[]{:S(2)}, u32[]{:S(2)}) %collective-permute-start.13) | collective-permute-done | bytes 4128 | tf_op jit(solution)/shard_map/ppermute | solution.py:219
  35.5 0.0 collective-permute-done.12.refs_7_
  35.5 0.0 collective-permute-done.7.refs_5_
  35.5 0.9 %last_update.1 = (f32[1,64,128]{2,1,0:T(8,128)}, f32[1,64,128]{2,1,0:T(8,128)}) custom-call(f32[1,64,128]{2,1,0:T(8,128)S(1)} %copy-done, f32[1,64,128]{2,1,0:T(8,128)S(1)} %get-tuple-element.25.refs_1_, f32[1,64,128]{2,1,0:T(8,128)S(1)} %get-tuple-element.26.refs_2_, f32[2,64,128]{2,1,0:T(8,128)S(1)} %get-tuple-element.27.refs_3_, ...), custom_call_target="tpu_custom_call" | custom-call | tf_op jit(solution)/shard_map/last_update/pallas_call | solution.py:304
  (5 shorter events, 0.0 us)
Async XLA Ops:
  0.6 6.0 %collective-permute-start.2 = (f32[1,64,128]{2,1,0:T(8,128)}, f32[1,64,128]{2,1,0:T(8,128)S(1)}, u32[]{:S(2)}, u32[]{:S(2)}) collective-permute-start(f32[1,64,128]{2,1,0:T(8,128)} %refs_0_.3), channel_id=1, source_target_pairs={{0,3},{1,2},{2,1},{3,0},{4,7},{5,6},{6,5},{7,4},{8,11},{9,10},{10,... | collective-permute-start | bytes 98312 | tf_op jit(solution)/shard_map/ppermute | solution.py:219
  3.1 4.2 %collective-permute-start.1 = (f32[1,64,128]{2,1,0:T(8,128)}, f32[1,64,128]{2,1,0:T(8,128)S(1)}, u32[]{:S(2)}, u32[]{:S(2)}) collective-permute-start(f32[1,64,128]{2,1,0:T(8,128)} %refs_0_.3), channel_id=1, source_target_pairs={{0,2},{1,3},{2,0},{3,1},{4,6},{5,7},{6,4},{7,5},{8,10},{9,11},{10,... | collective-permute-start | bytes 98312 | tf_op jit(solution)/shard_map/ppermute | solution.py:219
  3.7 3.5 %collective-permute-start = (f32[1,64,128]{2,1,0:T(8,128)}, f32[1,64,128]{2,1,0:T(8,128)S(1)}, u32[]{:S(2)}, u32[]{:S(2)}) collective-permute-start(f32[1,64,128]{2,1,0:T(8,128)} %refs_0_.3), channel_id=1, source_target_pairs={{0,1},{1,0},{2,3},{3,2},{4,5},{5,4},{6,7},{7,6},{8,9},{9,8},{10,11... | collective-permute-start | bytes 98312 | tf_op jit(solution)/shard_map/ppermute | solution.py:219
  4.4 2.9 %copy-start = (f32[1,64,128]{2,1,0:T(8,128)S(1)}, f32[1,64,128]{2,1,0:T(8,128)}, u32[]{:S(2)}) copy-start(f32[1,64,128]{2,1,0:T(8,128)} %refs_0_.3) | copy-start | bytes 98308
  9.9 1.3 %collective-permute-start.3 = (f32[2,64,128]{2,1,0:T(8,128)S(1)}, f32[2,64,128]{2,1,0:T(8,128)S(1)}, u32[]{:S(2)}, u32[]{:S(2)}) collective-permute-start(f32[2,64,128]{2,1,0:T(8,128)S(1)} %get-tuple-element.24), channel_id=1, source_target_pairs={{0,1},{1,0},{2,3},{3,2},{4,5},{5,4},{6,7},{7,6},{8,9},{9,8},{10,11... | collective-permute-start | bytes 196616 | tf_op jit(solution)/shard_map/ppermute | solution.py:219
  11.2 4.3 %collective-permute-start.4 = (f32[2,64,128]{2,1,0:T(8,128)S(1)}, f32[2,64,128]{2,1,0:T(8,128)S(1)}, u32[]{:S(2)}, u32[]{:S(2)}) collective-permute-start(f32[2,64,128]{2,1,0:T(8,128)S(1)} %add.21), channel_id=1, source_target_pairs={{0,2},{1,3},{2,0},{3,1},{4,6},{5,7},{6,4},{7,5},{8,10},{9,11},{10,... | collective-permute-start | bytes 196616 | tf_op jit(solution)/shard_map/ppermute | solution.py:219
  15.5 1.3 %collective-permute-start.5 = (f32[2,64,128]{2,1,0:T(8,128)S(1)}, f32[2,64,128]{2,1,0:T(8,128)S(1)}, u32[]{:S(2)}, u32[]{:S(2)}) collective-permute-start(f32[2,64,128]{2,1,0:T(8,128)S(1)} %add.22.refs_12_), channel_id=1, source_target_pairs={{0,1},{1,0},{2,3},{3,2},{4,5},{5,4},{6,7},{7,6},{8,9},{9,8},{10,11... | collective-permute-start | bytes 196616 | tf_op jit(solution)/shard_map/ppermute | solution.py:219
  19.8 4.9 %collective-permute-start.6 = (f32[2,64,128]{2,1,0:T(8,128)S(1)}, f32[2,64,128]{2,1,0:T(8,128)S(1)}, u32[]{:S(2)}, u32[]{:S(2)}) collective-permute-start(f32[2,64,128]{2,1,0:T(8,128)S(1)} %get-tuple-element.28), channel_id=1, source_target_pairs={{0,1},{1,0},{2,3},{3,2},{4,5},{5,4},{6,7},{7,6},{8,9},{9,8},{10,11... | collective-permute-start | bytes 196616 | tf_op jit(solution)/shard_map/ppermute | solution.py:219
  20.0 1.2 %collective-permute-start.8 = (f32[8,128]{1,0:T(8,128)S(1)}, f32[8,128]{1,0:T(8,128)S(1)}, u32[]{:S(2)}, u32[]{:S(2)}) collective-permute-start(f32[8,128]{1,0:T(8,128)S(1)} %get-tuple-element.29), channel_id=1, source_target_pairs={{0,1},{1,0},{2,3},{3,2},{4,5},{5,4},{6,7},{7,6},{8,9},{9,8},{10,11... | collective-permute-start | bytes 12296 | tf_op jit(solution)/shard_map/ppermute | solution.py:219
  21.2 4.7 %collective-permute-start.11 = (f32[8,128]{1,0:T(8,128)S(1)}, f32[8,128]{1,0:T(8,128)S(1)}, u32[]{:S(2)}, u32[]{:S(2)}) collective-permute-start(f32[8,128]{1,0:T(8,128)S(1)} %add.24), channel_id=1, source_target_pairs={{0,6},{1,7},{2,4},{3,5},{4,2},{5,3},{6,0},{7,1},{8,14},{9,15},{10,... | collective-permute-start | bytes 12296 | tf_op jit(solution)/shard_map/ppermute | solution.py:219
  23.2 3.6 %collective-permute-start.10 = (f32[8,128]{1,0:T(8,128)S(1)}, f32[8,128]{1,0:T(8,128)S(1)}, u32[]{:S(2)}, u32[]{:S(2)}) collective-permute-start(f32[8,128]{1,0:T(8,128)S(1)} %add.24), channel_id=1, source_target_pairs={{0,4},{1,5},{2,6},{3,7},{4,0},{5,1},{6,2},{7,3},{8,12},{9,13},{10,... | collective-permute-start | bytes 12296 | tf_op jit(solution)/shard_map/ppermute | solution.py:219
  23.8 3.6 %collective-permute-start.9 = (f32[8,128]{1,0:T(8,128)S(1)}, f32[8,128]{1,0:T(8,128)S(1)}, u32[]{:S(2)}, u32[]{:S(2)}) collective-permute-start(f32[8,128]{1,0:T(8,128)S(1)} %add.24), channel_id=1, source_target_pairs={{0,2},{1,3},{2,0},{3,1},{4,6},{5,7},{6,4},{7,5},{8,10},{9,11},{10,... | collective-permute-start | bytes 12296 | tf_op jit(solution)/shard_map/ppermute | solution.py:219
  24.7 10.8 %collective-permute-start.7 = (f32[1,64,128]{2,1,0:T(8,128)S(1)}, f32[1,64,128]{2,1,0:T(8,128)S(1)}, u32[]{:S(2)}, u32[]{:S(2)}) collective-permute-start(f32[1,64,128]{2,1,0:T(8,128)S(1)} %slice_add_fusion), channel_id=1, source_target_pairs={{0,2},{1,3},{2,0},{3,1},{4,6},{5,7},{6,4},{7,5},{8,10},{9,11},{10,... | collective-permute-start | bytes 98312 | tf_op jit(solution)/shard_map/ppermute | solution.py:219
  27.4 5.4 %collective-permute-start.14 = (f32[8,128]{1,0:T(8,128)S(1)}, f32[8,128]{1,0:T(8,128)S(1)}, u32[]{:S(2)}, u32[]{:S(2)}) collective-permute-start(f32[8,128]{1,0:T(8,128)S(1)} %add_add_fusion.refs_6_), channel_id=1, source_target_pairs={{0,24},{1,25},{2,26},{3,27},{4,28},{5,29},{6,30},{7,31},{8,16},{9,... | collective-permute-start | bytes 12296 | tf_op jit(solution)/shard_map/ppermute | solution.py:219
  31.0 4.5 %collective-permute-start.13 = (f32[8,128]{1,0:T(8,128)S(1)}, f32[8,128]{1,0:T(8,128)S(1)}, u32[]{:S(2)}, u32[]{:S(2)}) collective-permute-start(f32[8,128]{1,0:T(8,128)S(1)} %add_add_fusion.refs_6_), channel_id=1, source_target_pairs={{0,16},{1,17},{2,18},{3,19},{4,20},{5,21},{6,22},{7,23},{8,24},{9,... | collective-permute-start | bytes 12296 | tf_op jit(solution)/shard_map/ppermute | solution.py:219
  31.0 4.5 %collective-permute-start.12 = (f32[8,128]{1,0:T(8,128)S(1)}, f32[8,128]{1,0:T(8,128)S(1)}, u32[]{:S(2)}, u32[]{:S(2)}) collective-permute-start(f32[8,128]{1,0:T(8,128)S(1)} %add_add_fusion.refs_6_), channel_id=1, source_target_pairs={{0,8},{1,9},{2,10},{3,11},{4,12},{5,13},{6,14},{7,15},{8,0},{9,1},... | collective-permute-start | bytes 12296 | tf_op jit(solution)/shard_map/ppermute | solution.py:219

commit v4 on v3

--- a/solution.py
+++ b/solution.py
@@ -25,7 +25,7 @@
 def add_data(cell, shared, acc):
     users, items, count_ref, factors, words = cell
     count = count_ref[0, 0]
-    slots = users.shape[0]
+    slots = users.shape[1]
     group = max(k for k in range(1, unroll + 1) if slots % k == 0)
     bit = jnp.left_shift(1, lax.broadcasted_iota(jnp.int32, (8, words.shape[2]), 0))
 
@@ -33,9 +33,10 @@
         start = index * group
         for step in range(group):
             slot = start + step
-            user, item = users[slot], items[slot]
+            user, item = users[0, slot], items[0, slot]
             left = factors[item]
-            scores = dot(left, shared[user], (0, 0))
+            pieces = shared.shape[1] // left.shape[0]
+            scores = dot(jnp.concatenate([left] * pieces), shared[user], (0, 0))
             used = jnp.where(slot < count, bit, 0)
             mask = (words[slot][:, None, :] & used[None]) != 0
             tile = jnp.where(mask.reshape(scores.shape), scores, 0.0).astype(bf16)
@@ -58,6 +59,9 @@
         degree, column_degree = degrees[j, 0:1], degrees[j, 8:9]
         here = degree * own.astype(f32) - dot(own, sym[j], (1, 0)) - dot(following, edges[j], (1, 1))
         there = column_degree * following.astype(f32) - dot(own, edges[j], (1, 0))
+        rank = acc.shape[1]
+        here = sum(here[k : k + rank] for k in range(0, here.shape[0], rank))
+        there = sum(there[k : k + rank] for k in range(0, there.shape[0], rank))
         acc[local] += graph_weight * here
         acc[after] += graph_weight * there
 
@@ -99,6 +103,10 @@
         copy.wait()
 
 
+def even_masks(cols):
+    return [mask for mask in range(cols) if bin(mask).count("1") % 2 == 0]
+
+
 def total(value):
     return jnp.sum(jnp.sum(value, axis=tuple(range(value.ndim - 2))), keepdims=True)
 
@@ -106,7 +114,7 @@
 def first_kernel(parts, *refs):
     users, items, count, factors, words, sym, edges, degrees = refs[:8]
     pieces = refs[8 : 8 + parts]
-    keep, send, shared, acc = refs[8 + parts :]
+    acc, shared = refs[8 + parts :]
     me = lax.axis_index("col")
     share = pieces[0].shape[0]
     for offset in range(parts):
@@ -115,39 +123,29 @@
     acc[...] = jnp.zeros_like(acc)
     add_graph((sym, edges, degrees), shared, acc, me * share)
     add_data((users, items, count, factors, words), shared, acc)
-    split(acc, keep, send, me, share)
-
-
-def split(acc, keep, send, me, share):
-    odd = me & 1
-    for j in range(keep.shape[0] // share):
-        keep[pl.ds(j * share, share)] = acc[pl.ds((2 * j + odd) * share, share)]
-        send[pl.ds(j * share, share)] = acc[pl.ds((2 * j + (odd ^ 1)) * share, share)]
-
-
-def second_kernel(parts, height, *refs):
+
+
+def second_kernel(parts, count_sums, height, *refs):
     users, items, count, factors, words, sym, edges, degrees = refs[:8]
     pieces = refs[8 : 8 + parts]
-    mine, theirs = refs[8 + parts : 10 + parts]
-    keep, send, scalars, own_z, own_w, shared, acc, start, image, move = refs[10 + parts :]
+    sums = refs[8 + parts : 8 + parts + count_sums]
+    keep, send, scalars, own_z, own_w, shared, acc, start, image, move = refs[8 + parts + count_sums :]
     me, row = lax.axis_index("col"), lax.axis_index("row")
     share = pieces[0].shape[0]
     for offset in range(parts):
         block = (me ^ offset) * share
         start[pl.ds(block, share)] = pieces[offset][...]
-    odd = me & 1
-    for j in range(parts // 2):
-        image[pl.ds((2 * j + odd) * share, share)] = mine[pl.ds(j * share, share)]
-        image[pl.ds((2 * j + (odd ^ 1)) * share, share)] = theirs[pl.ds(j * share, share)]
     rhs = start[...]
-    w = image[...] + ridge_weight * rhs
+    w = sum(ref[...].astype(f32) for ref in sums) + ridge_weight * rhs
     a, b = total(rhs * rhs), total(rhs * w)
     step = jnp.where(b > 0.0, a / jnp.where(b > 0.0, b, 1.0), 1.0)
     step = jnp.where(step > 0.0, step, 1.0)
     z = rhs - step * w
     image[...] = w
     move[...] = z
-    shared[...] = z.astype(bf16)
+    high = z.astype(bf16)
+    shared[:, : z.shape[1]] = high
+    shared[:, z.shape[1] :] = (z - high.astype(f32)).astype(bf16)
     rz, zz, zw = total(rhs * z), total(z * z), total(z * w)
     acc[...] = jnp.zeros_like(acc)
     add_graph((sym, edges, degrees), shared, acc, me * share)
@@ -158,7 +156,7 @@
     values = (
         a * part,
         b * part,
-        step * part,
+        step,
         rz * part,
         zz * part,
         zw * part,
@@ -170,10 +168,10 @@
     packed = jnp.zeros((height, 128), f32)
     for index, value in enumerate(values):
         packed = jnp.where(lane == index, value, packed)
-    scalars[...] = jnp.where(sublane == row, packed, 0.0)
-    for j in range(parts // 2):
-        keep[pl.ds(j * share, share)] = acc[pl.ds((me ^ (2 * j)) * share, share)]
-        send[pl.ds(j * share, share)] = acc[pl.ds((me ^ (2 * j + 1)) * share, share)]
+    scalars[...] = packed
+    for j, mask in enumerate(even_masks(parts)):
+        keep[pl.ds(j * share, share)] = acc[pl.ds((me ^ mask) * share, share)]
+        send[pl.ds(j * share, share)] = acc[pl.ds((me ^ mask ^ 1) * share, share)]
     own_z[...] = move[pl.ds(me * share, share)]
     own_w[...] = image[pl.ds(me * share, share)]
 
@@ -203,7 +201,7 @@
     curve = whole(p * p * b + p * rho * (zw + rh) + rho * rho * zh)
     alpha_next = norm_next / curve
     sublane = lax.broadcasted_iota(jnp.int32, (height, 1), 0)
-    mine = jnp.where(sublane == row, rho, 0.0)
+    mine = jnp.where(sublane == row * lax.axis_size("col"), rho, 0.0)
     rho = whole(mine)
     rest = 1.0 - rho
     p = rest + beta
@@ -244,7 +242,7 @@
     words = mask_words[0, 0]
     tile_shape = self_tiles.shape
 
-    users, items = slot_users[0, 0], slot_items[0, 0]
+    users, items = slot_users[0], slot_items[0]
     factors, words, users, items, sym, edges, degrees = pl.pallas_call(
         functools.partial(prepare_kernel, cols),
         out_shape=[
@@ -257,7 +255,7 @@
             jax.ShapeDtypeStruct((tile_shape[0], 16, tile_shape[2]), f32),
         ],
         in_specs=[HBM] * 6,
-        out_specs=[VMEM] * 2 + [SMEM] * 2 + [VMEM] * 3,
+        out_specs=[VMEM] * 7,
         scratch_shapes=[pltpu.VMEM((2,) + tile_shape, jnp.int32), pltpu.SemaphoreType.DMA((6,))],
         compiler_params=params,
         cost_estimate=pl.CostEstimate(flops=10**6, bytes_accessed=4 * 10**6, transcendentals=0),
@@ -266,40 +264,35 @@
     cell = (users, items, slot_counts, factors, words, sym, edges, degrees)
     cell_specs = [SMEM] * 3 + [VMEM] * 5
 
-    keep, send = pl.pallas_call(
+    value = pl.pallas_call(
         functools.partial(first_kernel, cols),
-        out_shape=[half, half],
+        out_shape=jax.ShapeDtypeStruct(row_shape, f32),
         in_specs=cell_specs + [VMEM] * cols,
-        out_specs=[VMEM] * 2,
-        scratch_shapes=[pltpu.VMEM(row_shape, bf16), pltpu.VMEM(row_shape, f32)],
+        out_specs=VMEM,
+        scratch_shapes=[pltpu.VMEM(row_shape, bf16)],
         compiler_params=params,
         name="first_apply",
     )(*cell, *pieces)
-    keep = keep + exchange(send, "col", cols, 1)
-    bits = [1 << k for k in range(1, cols.bit_length() - 1)]
-    for bit in bits:
-        keep = keep + exchange(keep, "col", cols, bit)
-    theirs = exchange(keep, "col", cols, 1)
-
-    height = -(-rows // 8) * 8
+    sums = [(value + exchange(value, "col", cols, 1)).astype(bf16)]
+    for mask in even_masks(cols)[1:]:
+        sums.append(exchange(sums[0], "col", cols, mask))
+
+    height = rows * cols
     keep, send, table, own_z, own_w = pl.pallas_call(
-        functools.partial(second_kernel, cols, height),
+        functools.partial(second_kernel, cols, len(sums), height),
         out_shape=[half, half, jax.ShapeDtypeStruct((height, 128), f32), piece, piece],
-        in_specs=cell_specs + [VMEM] * (cols + 2),
+        in_specs=cell_specs + [VMEM] * (cols + len(sums)),
         out_specs=[VMEM] * 5,
-        scratch_shapes=[pltpu.VMEM(row_shape, bf16)] + [pltpu.VMEM(row_shape, f32)] * 4,
+        scratch_shapes=[pltpu.VMEM((cols * share, 2 * rank, width), bf16)] + [pltpu.VMEM(row_shape, f32)] * 4,
         compiler_params=params,
         name="second_apply",
-    )(*cell, *pieces, keep, theirs)
+    )(*cell, *pieces, *sums)
     pair = exchange(send, "col", cols, 1)
     images = [keep, pair]
-    for j in range(1, cols // 2):
+    for j, mask in list(enumerate(even_masks(cols)))[1:]:
         block = slice(j * share, (j + 1) * share)
-        images.append(exchange(keep[block] + pair[block], "col", cols, 2 * j))
-    tables = [table]
-    for group in bit_groups(rows * cols):
-        table = functools.reduce(jnp.add, tables)
-        tables = [table] + [exchange(table, ("row", "col"), rows * cols, o) for o in spans(group)]
+        images.append(exchange(keep[block] + pair[block], "col", cols, mask))
+    tables = [lax.all_to_all(table, ("row", "col"), 0, 0, tiled=True)]
 
     return pl.pallas_call(
         functools.partial(last_kernel, len(images), len(tables)),

time: 36.5 us -> 33.7 us (0.923)
  blocking collectives: 0 us -> 12.3 us
  starting transfers between devices: 14.2 us -> 4.98 us
  waiting for transfers between devices: 12.3 us -> 7.01 us
  Pallas kernels: 8.52 us -> 7.81 us
    all_to_all x0 -> x1, blocking collectives: none -> 12.3 us  [per_device(): tables = [lax.all_to_all(table, ('row', 'col'), 0, 0, tiled=True)]]
    ppermute x15 -> x7, starting transfers between devices: 14.2 us -> 4.98 us  [exchange(): return lax.ppermute(value, axes, [(i, i ^ offset) for i in range(size)])]
    ppermute x15 -> x7, waiting for transfers between devices: 12.3 us -> 7.01 us  [exchange(): return lax.ppermute(value, axes, [(i, i ^ offset) for i in range(size)])]
    pallas_call x1, Pallas kernels: 2.2 us -> 1.59 us  [per_device(): pl.pallas_call(functools.partial(prepare_kernel, cols), out_shape=[jax.Sh...]
  transfers between devices with their start and end apart: 15 -> 7, of which waited for: 9 -> 4; matrix products, arithmetic and copies ran while one was open for 0% -> 0% of each run, Pallas kernels for 6% -> 5%
where the time goes in v4:
time: 33.7 us; the launch traced here: 33.5 us
  blocking collectives  12.3 us (36%)
  Pallas kernels  7.81 us (23%)
  waiting for transfers between devices  7.01 us (21%)
  starting transfers between devices  4.98 us (15%)
  between operations  1.34 us (4%)
    all_to_all x1, blocking collectives, per_device(): tables = [lax.all_to_all(table, ('row', 'col'), 0, 0, tiled=True)]  12.3 us
    ppermute x7, waiting for transfers between devices, exchange(): return lax.ppermute(value, axes, [(i, i ^ offset) for i in range(size)])  7.01 us
    ppermute x7, starting transfers between devices, exchange(): return lax.ppermute(value, axes, [(i, i ^ offset) for i in range(size)])  4.98 us
    pallas_call x1, Pallas kernels, per_device(): pl.pallas_call(functools.partial(second_kernel, cols, len(sums), height),...  2.87 us
    pallas_call x1, Pallas kernels, per_device(): pl.pallas_call(functools.partial(first_kernel, cols), out_shape=jax.Shape...  2.48 us
    pallas_call x1, Pallas kernels, per_device(): pl.pallas_call(functools.partial(prepare_kernel, cols), out_shape=[jax.Sh...  1.59 us
    pallas_call x1, Pallas kernels, per_device(): pl.pallas_call(functools.partial(last_kernel, len(images), len(tables)),...  0.86 us
  transfers between devices with their start and end apart: 7, of which 4 were waited for; matrix products, arithmetic and copies ran while one was open for 0% of the time, Pallas kernels for 5%

profile of v4, /device:TPU:0, one launch (start us, length us, event | category | flops | bytes accessed | tf_op | source)
XLA Modules:
  0.0 33.5 jit_solution(13966628237338598059)
XLA Ops:
  0.6 2.5 %collective-permute-start.2 = (f32[1,64,128]{2,1,0:T(8,128)}, f32[1,64,128]{2,1,0:T(8,128)S(1)}, u32[]{:S(2)}, u32[]{:S(2)}) collective-permute-start(f32[1,64,128]{2,1,0:T(8,128)} %refs_0_.3), channel_id=1, source_target_pairs={{0,3},{1,2},{2,1},{3,0},{4,7},{5,6},{6,5},{7,4},{8,11},{9,10},{10,... | collective-permute-start | bytes 98312 | tf_op jit(solution)/shard_map/ppermute | solution.py:217
  3.1 0.6 %collective-permute-start.1 = (f32[1,64,128]{2,1,0:T(8,128)}, f32[1,64,128]{2,1,0:T(8,128)S(1)}, u32[]{:S(2)}, u32[]{:S(2)}) collective-permute-start(f32[1,64,128]{2,1,0:T(8,128)} %refs_0_.3), channel_id=1, source_target_pairs={{0,2},{1,3},{2,0},{3,1},{4,6},{5,7},{6,4},{7,5},{8,10},{9,11},{10,... | collective-permute-start | bytes 98312 | tf_op jit(solution)/shard_map/ppermute | solution.py:217
  3.7 0.0 collective-permute-start
  4.4 0.0 copy-start
  4.4 1.6 %prepare.1 = (bf16[64,64,128]{2,1,0:T(8,128)(2,1)S(1)}, s32[96,16,128]{2,1,0:T(8,128)S(1)}, s32[1,96]{1,0:T(1,128)S(1)}, s32[1,96]{1,0:T(1,128)S(1)}, bf16[1,128...) custom-call(bf16[64,64,128]{2,1,0:T(8,128)(2,1)} %refs_0_.2, ...), custom_call_target="tpu_custom_call" | custom-call | flops 1000000 | bytes 4000000 | tf_op jit(solution)/shard_map/prepare/pallas_call | solution.py:246
  6.0 0.0 collective-permute-done.2.refs_11_
  6.1 1.2 %collective-permute-done.1.refs_10_ = f32[1,64,128]{2,1,0:T(8,128)S(1)} collective-permute-done((f32[1,64,128]{2,1,0:T(8,128)}, f32[1,64,128]{2,1,0:T(8,128)S(1)}, u32[]{:S(2)}, u32[]{:S(2)}) %collective-permute-start.1) | collective-permute-done | bytes 32800 | tf_op jit(solution)/shard_map/ppermute | solution.py:217
  7.3 0.0 collective-permute-done.refs_9_
  7.3 0.0 copy-done
  7.3 2.5 %first_apply.1 = f32[4,64,128]{2,1,0:T(8,128)S(1)} custom-call(s32[1,96]{1,0:T(1,128)S(1)} %get-tuple-element.14.refs_0_, s32[1,96]{1,0:T(1,128)S(1)} %get-tuple-element.15.refs_1_, s32[1,1]{1,0:T(1,128)S(6)} %copy.11.refs_2_, bf16[64,64,128]{2,1,0:T(8,128)(2,1)S(1)} %get-tuple-element.16.refs_3_, s32[96,16,128]{2,1,0:T(8,128)S(1)} %get-tuple-element.17.refs_4_, ...), custom_call_target="tpu_custom_call" | custom-call | tf_op jit(solution)/shard_map/first_apply/pallas_call | solution.py:267
  9.8 0.1 collective-permute-start.3
  9.9 1.3 %collective-permute-done.3 = f32[4,64,128]{2,1,0:T(8,128)S(1)} collective-permute-done((f32[4,64,128]{2,1,0:T(8,128)S(1)}, f32[4,64,128]{2,1,0:T(8,128)S(1)}, u32[]{:S(2)}, u32[]{:S(2)}) %collective-permute-start.3) | collective-permute-done | bytes 131104 | tf_op jit(solution)/shard_map/ppermute | solution.py:217
  11.2 0.8 %collective-permute-start.4 = (bf16[4,64,128]{2,1,0:T(8,128)(2,1)S(1)}, bf16[4,64,128]{2,1,0:T(8,128)(2,1)S(1)}, u32[]{:S(2)}, u32[]{:S(2)}) collective-permute-start(bf16[4,64,128]{2,1,0:T(8,128)(2,1)S(1)} %add_convert_fusion.refs_12_), channel_id=1, source_target_pairs={{0,3},{1,2},{2,1},{3,0},{4,7},{5,6},{6,5},{7,4},{8,11},{9,10},{10,... | collective-permute-start | bytes 196616 | tf_op jit(solution)/shard_map/ppermute | solution.py:217
  12.0 3.3 %collective-permute-done.4.refs_13_ = bf16[4,64,128]{2,1,0:T(8,128)(2,1)S(1)} collective-permute-done((bf16[4,64,128]{2,1,0:T(8,128)(2,1)S(1)}, bf16[4,64,128]{2,1,0:T(8,128)(2,1)S(1)}, u32[]{:S(2)}, u32[]{:S(2)}) %collective-permute-start.4) | collective-permute-done | bytes 65568 | tf_op jit(solution)/shard_map/ppermute | solution.py:217
  15.3 2.9 %second_apply.1 = (f32[2,64,128]{2,1,0:T(8,128)S(1)}, f32[2,64,128]{2,1,0:T(8,128)S(1)}, f32[32,128]{1,0:T(8,128)S(1)}, f32[1,64,128]{2,1,0:T(8,128)S(1)}, f32[1,64,128]{2,1,0:T(8,128)S(1)}) custom-call(s32[1,96]{1,0:T(1,128)S(1)} %get-tuple-element.14.refs_0_, s32[1,96]{1,0:T(1,128)S(1)} %get-tuple-element.15.refs_1_, s32[1,1]{1,0:T(1,128)S(6)} %copy.11.refs_2_, ...), custom_call_target="tpu_custom_call" | custom-call | tf_op jit(solution)/shard_map/second_apply/pallas_call | solution.py:281
  18.2 0.2 collective-permute-start.5
  18.4 1.1 %collective-permute-done.5.refs_4_ = f32[2,64,128]{2,1,0:T(8,128)S(1)} collective-permute-done((f32[2,64,128]{2,1,0:T(8,128)S(1)}, f32[2,64,128]{2,1,0:T(8,128)S(1)}, u32[]{:S(2)}, u32[]{:S(2)}) %collective-permute-start.5) | collective-permute-done | bytes 65568 | tf_op jit(solution)/shard_map/ppermute | solution.py:217
  19.5 0.7 %collective-permute-start.6 = (f32[1,64,128]{2,1,0:T(8,128)S(1)}, f32[1,64,128]{2,1,0:T(8,128)S(1)}, u32[]{:S(2)}, u32[]{:S(2)}) collective-permute-start(f32[1,64,128]{2,1,0:T(8,128)S(1)} %slice_add_fusion), channel_id=1, source_target_pairs={{0,3},{1,2},{2,1},{3,0},{4,7},{5,6},{6,5},{7,4},{8,11},{9,10},{10,... | collective-permute-start | bytes 98312 | tf_op jit(solution)/shard_map/ppermute | solution.py:217
  20.3 12.3 %all_to_all.11 = f32[32,1,128]{2,1,0:T(1,128)S(1)} all-to-all(f32[32,1,128]{2,1,0:T(1,128)S(1)} %bitcast.8), channel_id=1, replica_groups=mesh['row'=8,'col'=4] {'row','col'}, dimensions={0} | all-to-all | bytes 32768 | tf_op jit(solution)/shard_map/all_to_all | solution.py:295
  32.6 0.0 collective-permute-done.6.refs_5_
  32.6 0.9 %last_update.1 = (f32[1,64,128]{2,1,0:T(8,128)}, f32[1,64,128]{2,1,0:T(8,128)}) custom-call(f32[1,64,128]{2,1,0:T(8,128)S(1)} %copy-done, f32[1,64,128]{2,1,0:T(8,128)S(1)} %get-tuple-element.21.refs_1_, f32[1,64,128]{2,1,0:T(8,128)S(1)} %get-tuple-element.22.refs_2_, f32[2,64,128]{2,1,0:T(8,128)S(1)} %get-tuple-element.23.refs_3_, ...), custom_call_target="tpu_custom_call" | custom-call | tf_op jit(solution)/shard_map/last_update/pallas_call | solution.py:297
  (2 shorter events, 0.0 us)
Async XLA Ops:
  0.6 5.4 %collective-permute-start.2 = (f32[1,64,128]{2,1,0:T(8,128)}, f32[1,64,128]{2,1,0:T(8,128)S(1)}, u32[]{:S(2)}, u32[]{:S(2)}) collective-permute-start(f32[1,64,128]{2,1,0:T(8,128)} %refs_0_.3), channel_id=1, source_target_pairs={{0,3},{1,2},{2,1},{3,0},{4,7},{5,6},{6,5},{7,4},{8,11},{9,10},{10,... | collective-permute-start | bytes 98312 | tf_op jit(solution)/shard_map/ppermute | solution.py:217
  3.1 4.2 %collective-permute-start.1 = (f32[1,64,128]{2,1,0:T(8,128)}, f32[1,64,128]{2,1,0:T(8,128)S(1)}, u32[]{:S(2)}, u32[]{:S(2)}) collective-permute-start(f32[1,64,128]{2,1,0:T(8,128)} %refs_0_.3), channel_id=1, source_target_pairs={{0,2},{1,3},{2,0},{3,1},{4,6},{5,7},{6,4},{7,5},{8,10},{9,11},{10,... | collective-permute-start | bytes 98312 | tf_op jit(solution)/shard_map/ppermute | solution.py:217
  3.7 3.5 %collective-permute-start = (f32[1,64,128]{2,1,0:T(8,128)}, f32[1,64,128]{2,1,0:T(8,128)S(1)}, u32[]{:S(2)}, u32[]{:S(2)}) collective-permute-start(f32[1,64,128]{2,1,0:T(8,128)} %refs_0_.3), channel_id=1, source_target_pairs={{0,1},{1,0},{2,3},{3,2},{4,5},{5,4},{6,7},{7,6},{8,9},{9,8},{10,11... | collective-permute-start | bytes 98312 | tf_op jit(solution)/shard_map/ppermute | solution.py:217
  4.4 2.9 %copy-start = (f32[1,64,128]{2,1,0:T(8,128)S(1)}, f32[1,64,128]{2,1,0:T(8,128)}, u32[]{:S(2)}) copy-start(f32[1,64,128]{2,1,0:T(8,128)} %refs_0_.3) | copy-start | bytes 98308
  9.8 1.4 %collective-permute-start.3 = (f32[4,64,128]{2,1,0:T(8,128)S(1)}, f32[4,64,128]{2,1,0:T(8,128)S(1)}, u32[]{:S(2)}, u32[]{:S(2)}) collective-permute-start(f32[4,64,128]{2,1,0:T(8,128)S(1)} %first_apply.1), channel_id=1, source_target_pairs={{0,1},{1,0},{2,3},{3,2},{4,5},{5,4},{6,7},{7,6},{8,9},{9,8},{10,11... | collective-permute-start | bytes 393224 | tf_op jit(solution)/shard_map/ppermute | solution.py:217
  11.2 4.1 %collective-permute-start.4 = (bf16[4,64,128]{2,1,0:T(8,128)(2,1)S(1)}, bf16[4,64,128]{2,1,0:T(8,128)(2,1)S(1)}, u32[]{:S(2)}, u32[]{:S(2)}) collective-permute-start(bf16[4,64,128]{2,1,0:T(8,128)(2,1)S(1)} %add_convert_fusion.refs_12_), channel_id=1, source_target_pairs={{0,3},{1,2},{2,1},{3,0},{4,7},{5,6},{6,5},{7,4},{8,11},{9,10},{10,... | collective-permute-start | bytes 196616 | tf_op jit(solution)/shard_map/ppermute | solution.py:217
  18.2 1.3 %collective-permute-start.5 = (f32[2,64,128]{2,1,0:T(8,128)S(1)}, f32[2,64,128]{2,1,0:T(8,128)S(1)}, u32[]{:S(2)}, u32[]{:S(2)}) collective-permute-start(f32[2,64,128]{2,1,0:T(8,128)S(1)} %get-tuple-element.24), channel_id=1, source_target_pairs={{0,1},{1,0},{2,3},{3,2},{4,5},{5,4},{6,7},{7,6},{8,9},{9,8},{10,11... | collective-permute-start | bytes 196616 | tf_op jit(solution)/shard_map/ppermute | solution.py:217
  19.5 13.1 %collective-permute-start.6 = (f32[1,64,128]{2,1,0:T(8,128)S(1)}, f32[1,64,128]{2,1,0:T(8,128)S(1)}, u32[]{:S(2)}, u32[]{:S(2)}) collective-permute-start(f32[1,64,128]{2,1,0:T(8,128)S(1)} %slice_add_fusion), channel_id=1, source_target_pairs={{0,3},{1,2},{2,1},{3,0},{4,7},{5,6},{6,5},{7,4},{8,11},{9,10},{10,... | collective-permute-start | bytes 98312 | tf_op jit(solution)/shard_map/ppermute | solution.py:217

commit v5 on v4

--- a/solution.py
+++ b/solution.py
@@ -156,7 +156,7 @@
     values = (
         a * part,
         b * part,
-        step,
+        step * part,
         rz * part,
         zz * part,
         zw * part,
@@ -168,10 +168,16 @@
     packed = jnp.zeros((height, 128), f32)
     for index, value in enumerate(values):
         packed = jnp.where(lane == index, value, packed)
+    packed = jnp.where(sublane == row, packed, 0.0)
     scalars[...] = packed
+    block = keep.shape[0] // (parts // 2)
+    rank = block // share
     for j, mask in enumerate(even_masks(parts)):
-        keep[pl.ds(j * share, share)] = acc[pl.ds((me ^ mask) * share, share)]
-        send[pl.ds(j * share, share)] = acc[pl.ds((me ^ mask ^ 1) * share, share)]
+        for i in range(share):
+            rows = pl.ds(j * block + i * rank, rank)
+            keep[rows] = acc[(me ^ mask) * share + i]
+            send[rows] = acc[(me ^ mask ^ 1) * share + i]
+    send[pl.ds(keep.shape[0], height)] = packed
     own_z[...] = move[pl.ds(me * share, share)]
     own_w[...] = image[pl.ds(me * share, share)]
 
@@ -201,14 +207,14 @@
     curve = whole(p * p * b + p * rho * (zw + rh) + rho * rho * zh)
     alpha_next = norm_next / curve
     sublane = lax.broadcasted_iota(jnp.int32, (height, 1), 0)
-    mine = jnp.where(sublane == row * lax.axis_size("col"), rho, 0.0)
+    mine = jnp.where(sublane == row, rho, 0.0)
     rho = whole(mine)
     rest = 1.0 - rho
     p = rest + beta
     r, z, w = own_r[...], own_z[...], own_w[...]
     hz = ridge_weight * z
     for ref in images:
-        hz = hz + ref[: z.shape[0]]
+        hz = hz + ref[: z.shape[0] * z.shape[1]].reshape(z.shape)
     solution_ref[...] = (alpha + alpha_next * p) * r + (alpha_next * rho) * z
     residual_ref[...] = rest * r + rho * z - alpha_next * (p * w + rho * hz)
 
@@ -217,17 +223,12 @@
     return lax.ppermute(value, axes, [(i, i ^ offset) for i in range(size)])
 
 
-def bit_groups(size):
-    bits = [1 << k for k in range(size.bit_length() - 1)]
-    groups = [bits[:1]] + [bits[k : k + 2] for k in range(1, len(bits), 2)]
-    return [group for group in groups if group]
-
-
-def spans(group):
-    offsets = [0]
-    for bit in group:
-        offsets = offsets + [offset ^ bit for offset in offsets]
-    return offsets[1:]
+def stages(rows, cols):
+    first = even_masks(cols)[1:]
+    if rows > 1:
+        first = first + [(mask ^ cols) | 1 for mask in even_masks(cols)]
+    bits = [cols << k for k in range(1, rows.bit_length() - 1)]
+    return [first] + [[bit | 1] for bit in bits]
 
 
 def per_device(
@@ -248,14 +249,14 @@
         out_shape=[
             jax.ShapeDtypeStruct(item_factors.shape, bf16),
             jax.ShapeDtypeStruct(words.shape, words.dtype),
-            jax.ShapeDtypeStruct(users.shape, users.dtype),
-            jax.ShapeDtypeStruct(items.shape, items.dtype),
+            pltpu.SMEM(users.shape, users.dtype),
+            pltpu.SMEM(items.shape, items.dtype),
             jax.ShapeDtypeStruct(tile_shape, bf16),
             jax.ShapeDtypeStruct(tile_shape, bf16),
             jax.ShapeDtypeStruct((tile_shape[0], 16, tile_shape[2]), f32),
         ],
         in_specs=[HBM] * 6,
-        out_specs=[VMEM] * 7,
+        out_specs=[VMEM] * 2 + [SMEM] * 2 + [VMEM] * 3,
         scratch_shapes=[pltpu.VMEM((2,) + tile_shape, jnp.int32), pltpu.SemaphoreType.DMA((6,))],
         compiler_params=params,
         cost_estimate=pl.CostEstimate(flops=10**6, bytes_accessed=4 * 10**6, transcendentals=0),
@@ -277,10 +278,13 @@
     for mask in even_masks(cols)[1:]:
         sums.append(exchange(sums[0], "col", cols, mask))
 
-    height = rows * cols
+    height = -(-rows // 8) * 8
+    block = share * rank
+    flat = jax.ShapeDtypeStruct((cols // 2 * block, width), f32)
+    tall = jax.ShapeDtypeStruct((cols // 2 * block + height, width), f32)
     keep, send, table, own_z, own_w = pl.pallas_call(
         functools.partial(second_kernel, cols, len(sums), height),
-        out_shape=[half, half, jax.ShapeDtypeStruct((height, 128), f32), piece, piece],
+        out_shape=[flat, tall, jax.ShapeDtypeStruct((height, 128), f32), piece, piece],
         in_specs=cell_specs + [VMEM] * (cols + len(sums)),
         out_specs=[VMEM] * 5,
         scratch_shapes=[pltpu.VMEM((cols * share, 2 * rank, width), bf16)] + [pltpu.VMEM(row_shape, f32)] * 4,
@@ -288,11 +292,19 @@
         name="second_apply",
     )(*cell, *pieces, *sums)
     pair = exchange(send, "col", cols, 1)
+    tables = [table, pair[-height:]]
     images = [keep, pair]
-    for j, mask in list(enumerate(even_masks(cols)))[1:]:
-        block = slice(j * share, (j + 1) * share)
-        images.append(exchange(keep[block] + pair[block], "col", cols, mask))
-    tables = [lax.all_to_all(table, ("row", "col"), 0, 0, tiled=True)]
+    for group in stages(rows, cols):
+        table = functools.reduce(jnp.add, tables)
+        tables = [table]
+        for mask in group:
+            if mask < cols:
+                j = even_masks(cols).index(mask)
+                part = slice(j * block, (j + 1) * block)
+                images.append(exchange(jnp.concatenate([keep[part] + pair[part], table]), "col", cols, mask))
+                tables.append(images[-1][-height:])
+            else:
+                tables.append(exchange(table, ("row", "col"), rows * cols, mask))
 
     return pl.pallas_call(
         functools.partial(last_kernel, len(images), len(tables)),

time: 33.7 us -> 32.3 us (0.958)
  blocking collectives: 12.3 us -> 0 us
  starting transfers between devices: 4.98 us -> 11 us
  waiting for transfers between devices: 7.01 us -> 13 us
  Pallas kernels: 7.81 us -> 6.73 us
    all_to_all x1 -> x0, blocking collectives: 12.3 us -> none  [per_device(): tables = [lax.all_to_all(table, ('row', 'col'), 0, 0, tiled=True)]]
    ppermute x7 -> x11, starting transfers between devices: 4.98 us -> 11 us  [exchange(): return lax.ppermute(value, axes, [(i, i ^ offset) for i in range(size)])]
    ppermute x7 -> x11, waiting for transfers between devices: 7.01 us -> 13 us  [exchange(): return lax.ppermute(value, axes, [(i, i ^ offset) for i in range(size)])]
    pallas_call x1, Pallas kernels: 2.87 us -> 2.31 us  [per_device(): pl.pallas_call(functools.partial(second_kernel, cols, len(sums), height),...]
    pallas_call x1, Pallas kernels: 2.48 us -> 1.97 us  [per_device(): pl.pallas_call(functools.partial(first_kernel, cols), out_shape=jax.Shape...]
  transfers between devices with their start and end apart: 7 -> 11, of which waited for: 4 -> 8; matrix products, arithmetic and copies ran while one was open for 0% -> 0% of each run, Pallas kernels for 5% -> 5%
where the time goes in v5:
time: 32.3 us; the launch traced here: 32.2 us
  waiting for transfers between devices  13 us (40%)
  starting transfers between devices  11 us (34%)
  Pallas kernels  6.73 us (21%)
  between operations  1.35 us (4%)
    ppermute x11, waiting for transfers between devices, exchange(): return lax.ppermute(value, axes, [(i, i ^ offset) for i in range(size)])  13 us
    ppermute x11, starting transfers between devices, exchange(): return lax.ppermute(value, axes, [(i, i ^ offset) for i in range(size)])  11 us
    pallas_call x1, Pallas kernels, per_device(): pl.pallas_call(functools.partial(second_kernel, cols, len(sums), height),...  2.31 us
    pallas_call x1, Pallas kernels, per_device(): pl.pallas_call(functools.partial(first_kernel, cols), out_shape=jax.Shape...  1.97 us
    pallas_call x1, Pallas kernels, per_device(): pl.pallas_call(functools.partial(prepare_kernel, cols), out_shape=[jax.Sh...  1.6 us
    pallas_call x1, Pallas kernels, per_device(): pl.pallas_call(functools.partial(last_kernel, len(images), len(tables)),...  0.85 us
  transfers between devices with their start and end apart: 11, of which 8 were waited for; matrix products, arithmetic and copies ran while one was open for 0% of the time, Pallas kernels for 5%

profile of v5, /device:TPU:0, one launch (start us, length us, event | category | flops | bytes accessed | tf_op | source)
XLA Modules:
  0.0 32.2 jit_solution(6146719301564354725)
XLA Ops:
  0.6 2.5 %collective-permute-start.2 = (f32[1,64,128]{2,1,0:T(8,128)}, f32[1,64,128]{2,1,0:T(8,128)S(1)}, u32[]{:S(2)}, u32[]{:S(2)}) collective-permute-start(f32[1,64,128]{2,1,0:T(8,128)} %refs_0_.3), channel_id=1, source_target_pairs={{0,3},{1,2},{2,1},{3,0},{4,7},{5,6},{6,5},{7,4},{8,11},{9,10},{10,... | collective-permute-start | bytes 98312 | tf_op jit(solution)/shard_map/ppermute | solution.py:223
  3.1 0.6 %collective-permute-start.1 = (f32[1,64,128]{2,1,0:T(8,128)}, f32[1,64,128]{2,1,0:T(8,128)S(1)}, u32[]{:S(2)}, u32[]{:S(2)}) collective-permute-start(f32[1,64,128]{2,1,0:T(8,128)} %refs_0_.3), channel_id=1, source_target_pairs={{0,2},{1,3},{2,0},{3,1},{4,6},{5,7},{6,4},{7,5},{8,10},{9,11},{10,... | collective-permute-start | bytes 98312 | tf_op jit(solution)/shard_map/ppermute | solution.py:223
  3.7 0.0 collective-permute-start
  4.4 0.0 copy-start
  4.4 1.6 %prepare.1 = (bf16[64,64,128]{2,1,0:T(8,128)(2,1)S(1)}, s32[96,16,128]{2,1,0:T(8,128)S(1)}, s32[1,96]{1,0:T(1,128)S(4)}, s32[1,96]{1,0:T(1,128)S(4)}, bf16[1,128...) custom-call(bf16[64,64,128]{2,1,0:T(8,128)(2,1)} %refs_0_.2, ...), custom_call_target="tpu_custom_call" | custom-call | flops 1000000 | bytes 4000000 | tf_op jit(solution)/shard_map/prepare/pallas_call | solution.py:247
  6.1 0.0 collective-permute-done.2.refs_11_
  6.1 1.2 %collective-permute-done.1.refs_10_ = f32[1,64,128]{2,1,0:T(8,128)S(1)} collective-permute-done((f32[1,64,128]{2,1,0:T(8,128)}, f32[1,64,128]{2,1,0:T(8,128)S(1)}, u32[]{:S(2)}, u32[]{:S(2)}) %collective-permute-start.1) | collective-permute-done | bytes 32800 | tf_op jit(solution)/shard_map/ppermute | solution.py:223
  7.3 0.0 collective-permute-done.refs_9_
  7.3 0.0 copy-done
  7.3 2.0 %first_apply.1 = f32[4,64,128]{2,1,0:T(8,128)S(1)} custom-call(s32[1,96]{1,0:T(1,128)S(4)} %get-tuple-element.14.refs_0_, s32[1,96]{1,0:T(1,128)S(4)} %get-tuple-element.15.refs_1_, s32[1,1]{1,0:T(1,128)S(6)} %copy.10.refs_2_, bf16[64,64,128]{2,1,0:T(8,128)(2,1)S(1)} %get-tuple-element.16.refs_3_, s32[96,16,128]{2,1,0:T(8,128)S(1)} %get-tuple-element.17.refs_4_, ...), custom_call_target="tpu_custom_call" | custom-call | tf_op jit(solution)/shard_map/first_apply/pallas_call | solution.py:268
  9.3 0.1 collective-permute-start.3
  9.3 1.3 %collective-permute-done.3 = f32[4,64,128]{2,1,0:T(8,128)S(1)} collective-permute-done((f32[4,64,128]{2,1,0:T(8,128)S(1)}, f32[4,64,128]{2,1,0:T(8,128)S(1)}, u32[]{:S(2)}, u32[]{:S(2)}) %collective-permute-start.3) | collective-permute-done | bytes 131104 | tf_op jit(solution)/shard_map/ppermute | solution.py:223
  10.7 0.8 %collective-permute-start.4 = (bf16[4,64,128]{2,1,0:T(8,128)(2,1)S(1)}, bf16[4,64,128]{2,1,0:T(8,128)(2,1)S(1)}, u32[]{:S(2)}, u32[]{:S(2)}) collective-permute-start(bf16[4,64,128]{2,1,0:T(8,128)(2,1)S(1)} %add_convert_fusion.refs_12_), channel_id=1, source_target_pairs={{0,3},{1,2},{2,1},{3,0},{4,7},{5,6},{6,5},{7,4},{8,11},{9,10},{10,... | collective-permute-start | bytes 196616 | tf_op jit(solution)/shard_map/ppermute | solution.py:223
  11.5 3.3 %collective-permute-done.4.refs_13_ = bf16[4,64,128]{2,1,0:T(8,128)(2,1)S(1)} collective-permute-done((bf16[4,64,128]{2,1,0:T(8,128)(2,1)S(1)}, bf16[4,64,128]{2,1,0:T(8,128)(2,1)S(1)}, u32[]{:S(2)}, u32[]{:S(2)}) %collective-permute-start.4) | collective-permute-done | bytes 65568 | tf_op jit(solution)/shard_map/ppermute | solution.py:223
  14.8 2.3 %second_apply.1 = (f32[128,128]{1,0:T(8,128)S(1)}, f32[136,128]{1,0:T(8,128)S(1)}, f32[8,128]{1,0:T(8,128)S(1)}, f32[1,64,128]{2,1,0:T(8,128)S(1)}, f32[1,64,128]{2,1,0:T(8,128)S(1)}) custom-call(s32[1,96]{1,0:T(1,128)S(4)} %get-tuple-element.14.refs_0_, s32[1,96]{1,0:T(1,128)S(4)} %get-tuple-element.15.refs_1_, s32[1,1]{1,0:T(1,128)S(6)} %copy.10.refs_2_, ...), custom_call_target="tpu_custom_call" | custom-call | tf_op jit(solution)/shard_map/second_apply/pallas_call | solution.py:285
  17.1 0.2 collective-permute-start.5
  17.4 1.1 %collective-permute-done.5.refs_4_ = f32[136,128]{1,0:T(8,128)S(1)} collective-permute-done((f32[136,128]{1,0:T(8,128)S(1)}, f32[136,128]{1,0:T(8,128)S(1)}, u32[]{:S(2)}, u32[]{:S(2)}) %collective-permute-start.5) | collective-permute-done | bytes 69664 | tf_op jit(solution)/shard_map/ppermute | solution.py:223
  18.5 0.8 %collective-permute-start.6 = (f32[72,128]{1,0:T(8,128)S(1)}, f32[72,128]{1,0:T(8,128)S(1)}, u32[]{:S(2)}, u32[]{:S(2)}) collective-permute-start(f32[72,128]{1,0:T(8,128)S(1)} %pad_maximum_fusion), channel_id=1, source_target_pairs={{0,3},{1,2},{2,1},{3,0},{4,7},{5,6},{6,5},{7,4},{8,11},{9,10},{10,... | collective-permute-start | bytes 110600 | tf_op jit(solution)/shard_map/ppermute | solution.py:223
  19.3 1.9 %collective-permute-start.8 = (f32[8,128]{1,0:T(8,128)S(1)}, f32[8,128]{1,0:T(8,128)S(1)}, u32[]{:S(2)}, u32[]{:S(2)}) collective-permute-start(f32[8,128]{1,0:T(8,128)S(1)} %slice_add_fusion.2), channel_id=1, source_target_pairs={{0,7},{1,6},{2,5},{3,4},{4,3},{5,2},{6,1},{7,0},{8,15},{9,14},{10,... | collective-permute-start | bytes 12296 | tf_op jit(solution)/shard_map/ppermute | solution.py:223
  21.2 0.3 collective-permute-start.7
  21.5 1.7 %collective-permute-done.8 = f32[8,128]{1,0:T(8,128)S(1)} collective-permute-done((f32[8,128]{1,0:T(8,128)S(1)}, f32[8,128]{1,0:T(8,128)S(1)}, u32[]{:S(2)}, u32[]{:S(2)}) %collective-permute-start.8) | collective-permute-done | bytes 4128 | tf_op jit(solution)/shard_map/ppermute | solution.py:223
  23.2 1.0 %collective-permute-done.7 = f32[8,128]{1,0:T(8,128)S(1)} collective-permute-done((f32[8,128]{1,0:T(8,128)S(1)}, f32[8,128]{1,0:T(8,128)S(1)}, u32[]{:S(2)}, u32[]{:S(2)}) %collective-permute-start.7) | collective-permute-done | bytes 4128 | tf_op jit(solution)/shard_map/ppermute | solution.py:223
  24.3 0.0 collective-permute-done.6.refs_5_
  24.3 1.4 %collective-permute-start.9 = (f32[8,128]{1,0:T(8,128)S(1)}, f32[8,128]{1,0:T(8,128)S(1)}, u32[]{:S(2)}, u32[]{:S(2)}) collective-permute-start(f32[8,128]{1,0:T(8,128)S(1)} %fusion.1), channel_id=1, source_target_pairs={{0,9},{1,8},{2,11},{3,10},{4,13},{5,12},{6,15},{7,14},{8,1},{9,0},... | collective-permute-start | bytes 12296 | tf_op jit(solution)/shard_map/ppermute | solution.py:223
  25.7 1.7 %collective-permute-done.9 = f32[8,128]{1,0:T(8,128)S(1)} collective-permute-done((f32[8,128]{1,0:T(8,128)S(1)}, f32[8,128]{1,0:T(8,128)S(1)}, u32[]{:S(2)}, u32[]{:S(2)}) %collective-permute-start.9) | collective-permute-done | bytes 4128 | tf_op jit(solution)/shard_map/ppermute | solution.py:223
  27.4 2.4 %collective-permute-start.10 = (f32[8,128]{1,0:T(8,128)S(1)}, f32[8,128]{1,0:T(8,128)S(1)}, u32[]{:S(2)}, u32[]{:S(2)}) collective-permute-start(f32[8,128]{1,0:T(8,128)S(1)} %add.27.refs_6_), channel_id=1, source_target_pairs={{0,17},{1,16},{2,19},{3,18},{4,21},{5,20},{6,23},{7,22},{8,25},{9,... | collective-permute-start | bytes 12296 | tf_op jit(solution)/shard_map/ppermute | solution.py:223
  29.7 1.6 %collective-permute-done.10.refs_7_ = f32[8,128]{1,0:T(8,128)S(1)} collective-permute-done((f32[8,128]{1,0:T(8,128)S(1)}, f32[8,128]{1,0:T(8,128)S(1)}, u32[]{:S(2)}, u32[]{:S(2)}) %collective-permute-start.10) | collective-permute-done | bytes 4128 | tf_op jit(solution)/shard_map/ppermute | solution.py:223
  31.3 0.9 %last_update.1 = (f32[1,64,128]{2,1,0:T(8,128)}, f32[1,64,128]{2,1,0:T(8,128)}) custom-call(f32[1,64,128]{2,1,0:T(8,128)S(1)} %copy-done, f32[1,64,128]{2,1,0:T(8,128)S(1)} %get-tuple-element.21.refs_1_, f32[1,64,128]{2,1,0:T(8,128)S(1)} %get-tuple-element.22.refs_2_, f32[128,128]{1,0:T(8,128)S(1)} %get-tuple-element.23.refs_3_, ...), custom_call_target="tpu_custom_call" | custom-call | tf_op jit(solution)/shard_map/last_update/pallas_call | solution.py:309
  (6 shorter events, 0.0 us)
Async XLA Ops:
  0.6 5.4 %collective-permute-start.2 = (f32[1,64,128]{2,1,0:T(8,128)}, f32[1,64,128]{2,1,0:T(8,128)S(1)}, u32[]{:S(2)}, u32[]{:S(2)}) collective-permute-start(f32[1,64,128]{2,1,0:T(8,128)} %refs_0_.3), channel_id=1, source_target_pairs={{0,3},{1,2},{2,1},{3,0},{4,7},{5,6},{6,5},{7,4},{8,11},{9,10},{10,... | collective-permute-start | bytes 98312 | tf_op jit(solution)/shard_map/ppermute | solution.py:223
  3.1 4.2 %collective-permute-start.1 = (f32[1,64,128]{2,1,0:T(8,128)}, f32[1,64,128]{2,1,0:T(8,128)S(1)}, u32[]{:S(2)}, u32[]{:S(2)}) collective-permute-start(f32[1,64,128]{2,1,0:T(8,128)} %refs_0_.3), channel_id=1, source_target_pairs={{0,2},{1,3},{2,0},{3,1},{4,6},{5,7},{6,4},{7,5},{8,10},{9,11},{10,... | collective-permute-start | bytes 98312 | tf_op jit(solution)/shard_map/ppermute | solution.py:223
  3.7 3.5 %collective-permute-start = (f32[1,64,128]{2,1,0:T(8,128)}, f32[1,64,128]{2,1,0:T(8,128)S(1)}, u32[]{:S(2)}, u32[]{:S(2)}) collective-permute-start(f32[1,64,128]{2,1,0:T(8,128)} %refs_0_.3), channel_id=1, source_target_pairs={{0,1},{1,0},{2,3},{3,2},{4,5},{5,4},{6,7},{7,6},{8,9},{9,8},{10,11... | collective-permute-start | bytes 98312 | tf_op jit(solution)/shard_map/ppermute | solution.py:223
  4.4 2.9 %copy-start = (f32[1,64,128]{2,1,0:T(8,128)S(1)}, f32[1,64,128]{2,1,0:T(8,128)}, u32[]{:S(2)}) copy-start(f32[1,64,128]{2,1,0:T(8,128)} %refs_0_.3) | copy-start | bytes 98308
  9.3 1.4 %collective-permute-start.3 = (f32[4,64,128]{2,1,0:T(8,128)S(1)}, f32[4,64,128]{2,1,0:T(8,128)S(1)}, u32[]{:S(2)}, u32[]{:S(2)}) collective-permute-start(f32[4,64,128]{2,1,0:T(8,128)S(1)} %first_apply.1), channel_id=1, source_target_pairs={{0,1},{1,0},{2,3},{3,2},{4,5},{5,4},{6,7},{7,6},{8,9},{9,8},{10,11... | collective-permute-start | bytes 393224 | tf_op jit(solution)/shard_map/ppermute | solution.py:223
  10.7 4.1 %collective-permute-start.4 = (bf16[4,64,128]{2,1,0:T(8,128)(2,1)S(1)}, bf16[4,64,128]{2,1,0:T(8,128)(2,1)S(1)}, u32[]{:S(2)}, u32[]{:S(2)}) collective-permute-start(bf16[4,64,128]{2,1,0:T(8,128)(2,1)S(1)} %add_convert_fusion.refs_12_), channel_id=1, source_target_pairs={{0,3},{1,2},{2,1},{3,0},{4,7},{5,6},{6,5},{7,4},{8,11},{9,10},{10,... | collective-permute-start | bytes 196616 | tf_op jit(solution)/shard_map/ppermute | solution.py:223
  17.1 1.3 %collective-permute-start.5 = (f32[136,128]{1,0:T(8,128)S(1)}, f32[136,128]{1,0:T(8,128)S(1)}, u32[]{:S(2)}, u32[]{:S(2)}) collective-permute-start(f32[136,128]{1,0:T(8,128)S(1)} %get-tuple-element.24), channel_id=1, source_target_pairs={{0,1},{1,0},{2,3},{3,2},{4,5},{5,4},{6,7},{7,6},{8,9},{9,8},{10,11... | collective-permute-start | bytes 208904 | tf_op jit(solution)/shard_map/ppermute | solution.py:223
  18.5 5.8 %collective-permute-start.6 = (f32[72,128]{1,0:T(8,128)S(1)}, f32[72,128]{1,0:T(8,128)S(1)}, u32[]{:S(2)}, u32[]{:S(2)}) collective-permute-start(f32[72,128]{1,0:T(8,128)S(1)} %pad_maximum_fusion), channel_id=1, source_target_pairs={{0,3},{1,2},{2,1},{3,0},{4,7},{5,6},{6,5},{7,4},{8,11},{9,10},{10,... | collective-permute-start | bytes 110600 | tf_op jit(solution)/shard_map/ppermute | solution.py:223
  19.3 3.9 %collective-permute-start.8 = (f32[8,128]{1,0:T(8,128)S(1)}, f32[8,128]{1,0:T(8,128)S(1)}, u32[]{:S(2)}, u32[]{:S(2)}) collective-permute-start(f32[8,128]{1,0:T(8,128)S(1)} %slice_add_fusion.2), channel_id=1, source_target_pairs={{0,7},{1,6},{2,5},{3,4},{4,3},{5,2},{6,1},{7,0},{8,15},{9,14},{10,... | collective-permute-start | bytes 12296 | tf_op jit(solution)/shard_map/ppermute | solution.py:223
  21.2 3.0 %collective-permute-start.7 = (f32[8,128]{1,0:T(8,128)S(1)}, f32[8,128]{1,0:T(8,128)S(1)}, u32[]{:S(2)}, u32[]{:S(2)}) collective-permute-start(f32[8,128]{1,0:T(8,128)S(1)} %slice_add_fusion.2), channel_id=1, source_target_pairs={{0,5},{1,4},{2,7},{3,6},{4,1},{5,0},{6,3},{7,2},{8,13},{9,12},{10,... | collective-permute-start | bytes 12296 | tf_op jit(solution)/shard_map/ppermute | solution.py:223
  24.3 3.1 %collective-permute-start.9 = (f32[8,128]{1,0:T(8,128)S(1)}, f32[8,128]{1,0:T(8,128)S(1)}, u32[]{:S(2)}, u32[]{:S(2)}) collective-permute-start(f32[8,128]{1,0:T(8,128)S(1)} %fusion.1), channel_id=1, source_target_pairs={{0,9},{1,8},{2,11},{3,10},{4,13},{5,12},{6,15},{7,14},{8,1},{9,0},... | collective-permute-start | bytes 12296 | tf_op jit(solution)/shard_map/ppermute | solution.py:223
  27.4 3.9 %collective-permute-start.10 = (f32[8,128]{1,0:T(8,128)S(1)}, f32[8,128]{1,0:T(8,128)S(1)}, u32[]{:S(2)}, u32[]{:S(2)}) collective-permute-start(f32[8,128]{1,0:T(8,128)S(1)} %add.27.refs_6_), channel_id=1, source_target_pairs={{0,17},{1,16},{2,19},{3,18},{4,21},{5,20},{6,23},{7,22},{8,25},{9,... | collective-permute-start | bytes 12296 | tf_op jit(solution)/shard_map/ppermute | solution.py:223

commit v6 on v5

--- a/solution.py
+++ b/solution.py
@@ -114,12 +114,14 @@
 def first_kernel(parts, *refs):
     users, items, count, factors, words, sym, edges, degrees = refs[:8]
     pieces = refs[8 : 8 + parts]
-    acc, shared = refs[8 + parts :]
+    acc, start, shared = refs[8 + parts :]
     me = lax.axis_index("col")
     share = pieces[0].shape[0]
     for offset in range(parts):
         block = (me ^ offset) * share
-        shared[pl.ds(block, share)] = pieces[offset][...].astype(bf16)
+        piece = pieces[offset][...]
+        start[pl.ds(block, share)] = piece
+        shared[pl.ds(block, share)] = piece.astype(bf16)
     acc[...] = jnp.zeros_like(acc)
     add_graph((sym, edges, degrees), shared, acc, me * share)
     add_data((users, items, count, factors, words), shared, acc)
@@ -127,14 +129,11 @@
 
 def second_kernel(parts, count_sums, height, *refs):
     users, items, count, factors, words, sym, edges, degrees = refs[:8]
-    pieces = refs[8 : 8 + parts]
-    sums = refs[8 + parts : 8 + parts + count_sums]
-    keep, send, scalars, own_z, own_w, shared, acc, start, image, move = refs[8 + parts + count_sums :]
+    start = refs[8]
+    sums = refs[9 : 9 + count_sums]
+    keep, send, scalars, own_z, own_w, shared, acc, image, move = refs[9 + count_sums :]
     me, row = lax.axis_index("col"), lax.axis_index("row")
-    share = pieces[0].shape[0]
-    for offset in range(parts):
-        block = (me ^ offset) * share
-        start[pl.ds(block, share)] = pieces[offset][...]
+    share = start.shape[0] // parts
     rhs = start[...]
     w = sum(ref[...].astype(f32) for ref in sums) + ridge_weight * rhs
     a, b = total(rhs * rhs), total(rhs * w)
@@ -265,11 +264,12 @@
     cell = (users, items, slot_counts, factors, words, sym, edges, degrees)
     cell_specs = [SMEM] * 3 + [VMEM] * 5
 
-    value = pl.pallas_call(
+    whole = jax.ShapeDtypeStruct(row_shape, f32)
+    value, start = pl.pallas_call(
         functools.partial(first_kernel, cols),
-        out_shape=jax.ShapeDtypeStruct(row_shape, f32),
+        out_shape=[whole, whole],
         in_specs=cell_specs + [VMEM] * cols,
-        out_specs=VMEM,
+        out_specs=[VMEM] * 2,
         scratch_shapes=[pltpu.VMEM(row_shape, bf16)],
         compiler_params=params,
         name="first_apply",
@@ -285,12 +285,12 @@
     keep, send, table, own_z, own_w = pl.pallas_call(
         functools.partial(second_kernel, cols, len(sums), height),
         out_shape=[flat, tall, jax.ShapeDtypeStruct((height, 128), f32), piece, piece],
-        in_specs=cell_specs + [VMEM] * (cols + len(sums)),
+        in_specs=cell_specs + [VMEM] * (1 + len(sums)),
         out_specs=[VMEM] * 5,
-        scratch_shapes=[pltpu.VMEM((cols * share, 2 * rank, width), bf16)] + [pltpu.VMEM(row_shape, f32)] * 4,
+        scratch_shapes=[pltpu.VMEM((cols * share, 2 * rank, width), bf16)] + [pltpu.VMEM(row_shape, f32)] * 3,
         compiler_params=params,
         name="second_apply",
-    )(*cell, *pieces, *sums)
+    )(*cell, start, *sums)
     pair = exchange(send, "col", cols, 1)
     tables = [table, pair[-height:]]
     images = [keep, pair]

time: 32.3 us -> 32.3 us (level)
  no operation moved by 1% of the time
where the time goes in v6:
time: 32.3 us; the launch traced here: 32.1 us
  waiting for transfers between devices  13 us (40%)
  starting transfers between devices  11 us (34%)
  Pallas kernels  6.7 us (21%)
  between operations  1.35 us (4%)
    ppermute x11, waiting for transfers between devices, exchange(): return lax.ppermute(value, axes, [(i, i ^ offset) for i in range(size)])  13 us
    ppermute x11, starting transfers between devices, exchange(): return lax.ppermute(value, axes, [(i, i ^ offset) for i in range(size)])  11 us
    pallas_call x1, Pallas kernels, per_device(): pl.pallas_call(functools.partial(second_kernel, cols, len(sums), height),...  2.29 us
    pallas_call x1, Pallas kernels, per_device(): pl.pallas_call(functools.partial(first_kernel, cols), out_shape=[whole, w...  1.95 us
    pallas_call x1, Pallas kernels, per_device(): pl.pallas_call(functools.partial(prepare_kernel, cols), out_shape=[jax.Sh...  1.6 us
    pallas_call x1, Pallas kernels, per_device(): pl.pallas_call(functools.partial(last_kernel, len(images), len(tables)),...  0.85 us
  transfers between devices with their start and end apart: 11, of which 8 were waited for; matrix products, arithmetic and copies ran while one was open for 0% of the time, Pallas kernels for 5%

profile of v6, /device:TPU:0, one launch (start us, length us, event | category | flops | bytes accessed | tf_op | source)
XLA Modules:
  0.0 32.1 jit_solution(17447913132136407598)
XLA Ops:
  0.6 2.5 %collective-permute-start.2 = (f32[1,64,128]{2,1,0:T(8,128)}, f32[1,64,128]{2,1,0:T(8,128)S(1)}, u32[]{:S(2)}, u32[]{:S(2)}) collective-permute-start(f32[1,64,128]{2,1,0:T(8,128)} %refs_0_.3), channel_id=1, source_target_pairs={{0,3},{1,2},{2,1},{3,0},{4,7},{5,6},{6,5},{7,4},{8,11},{9,10},{10,... | collective-permute-start | bytes 98312 | tf_op jit(solution)/shard_map/ppermute | solution.py:222
  3.1 0.6 %collective-permute-start.1 = (f32[1,64,128]{2,1,0:T(8,128)}, f32[1,64,128]{2,1,0:T(8,128)S(1)}, u32[]{:S(2)}, u32[]{:S(2)}) collective-permute-start(f32[1,64,128]{2,1,0:T(8,128)} %refs_0_.3), channel_id=1, source_target_pairs={{0,2},{1,3},{2,0},{3,1},{4,6},{5,7},{6,4},{7,5},{8,10},{9,11},{10,... | collective-permute-start | bytes 98312 | tf_op jit(solution)/shard_map/ppermute | solution.py:222
  3.7 0.0 collective-permute-start
  4.4 0.0 copy-start
  4.4 1.6 %prepare.1 = (bf16[64,64,128]{2,1,0:T(8,128)(2,1)S(1)}, s32[96,16,128]{2,1,0:T(8,128)S(1)}, s32[1,96]{1,0:T(1,128)S(4)}, s32[1,96]{1,0:T(1,128)S(4)}, bf16[1,128...) custom-call(bf16[64,64,128]{2,1,0:T(8,128)(2,1)} %refs_0_.2, ...), custom_call_target="tpu_custom_call" | custom-call | flops 1000000 | bytes 4000000 | tf_op jit(solution)/shard_map/prepare/pallas_call | solution.py:246
  6.1 0.0 collective-permute-done.2.refs_11_
  6.1 1.2 %collective-permute-done.1.refs_10_ = f32[1,64,128]{2,1,0:T(8,128)S(1)} collective-permute-done((f32[1,64,128]{2,1,0:T(8,128)}, f32[1,64,128]{2,1,0:T(8,128)S(1)}, u32[]{:S(2)}, u32[]{:S(2)}) %collective-permute-start.1) | collective-permute-done | bytes 32800 | tf_op jit(solution)/shard_map/ppermute | solution.py:222
  7.3 0.0 collective-permute-done.refs_9_
  7.3 0.0 copy-done
  7.3 2.0 %first_apply.1 = (f32[4,64,128]{2,1,0:T(8,128)S(1)}, f32[4,64,128]{2,1,0:T(8,128)S(1)}) custom-call(s32[1,96]{1,0:T(1,128)S(4)} %get-tuple-element.16.refs_0_, s32[1,96]{1,0:T(1,128)S(4)} %get-tuple-element.17.refs_1_, s32[1,1]{1,0:T(1,128)S(6)} %copy.10.refs_2_, bf16[64,64,128]{2,1,0:T(8,128)(2,1)S(1)} %get-tuple-element.18.refs_3_, ...), custom_call_target="tpu_custom_call" | custom-call | tf_op jit(solution)/shard_map/first_apply/pallas_call | solution.py:268
  9.2 0.1 collective-permute-start.3
  9.3 1.3 %collective-permute-done.3 = f32[4,64,128]{2,1,0:T(8,128)S(1)} collective-permute-done((f32[4,64,128]{2,1,0:T(8,128)S(1)}, f32[4,64,128]{2,1,0:T(8,128)S(1)}, u32[]{:S(2)}, u32[]{:S(2)}) %collective-permute-start.3) | collective-permute-done | bytes 131104 | tf_op jit(solution)/shard_map/ppermute | solution.py:222
  10.7 0.8 %collective-permute-start.4 = (bf16[4,64,128]{2,1,0:T(8,128)(2,1)S(1)}, bf16[4,64,128]{2,1,0:T(8,128)(2,1)S(1)}, u32[]{:S(2)}, u32[]{:S(2)}) collective-permute-start(bf16[4,64,128]{2,1,0:T(8,128)(2,1)S(1)} %add_convert_fusion.refs_9_), channel_id=1, source_target_pairs={{0,3},{1,2},{2,1},{3,0},{4,7},{5,6},{6,5},{7,4},{8,11},{9,10},{10,... | collective-permute-start | bytes 196616 | tf_op jit(solution)/shard_map/ppermute | solution.py:222
  11.5 3.3 %collective-permute-done.4.refs_10_ = bf16[4,64,128]{2,1,0:T(8,128)(2,1)S(1)} collective-permute-done((bf16[4,64,128]{2,1,0:T(8,128)(2,1)S(1)}, bf16[4,64,128]{2,1,0:T(8,128)(2,1)S(1)}, u32[]{:S(2)}, u32[]{:S(2)}) %collective-permute-start.4) | collective-permute-done | bytes 65568 | tf_op jit(solution)/shard_map/ppermute | solution.py:222
  14.8 2.3 %second_apply.1 = (f32[128,128]{1,0:T(8,128)S(1)}, f32[136,128]{1,0:T(8,128)S(1)}, f32[8,128]{1,0:T(8,128)S(1)}, f32[1,64,128]{2,1,0:T(8,128)S(1)}, f32[1,64,128]{2,1,0:T(8,128)S(1)}) custom-call(s32[1,96]{1,0:T(1,128)S(4)} %get-tuple-element.16.refs_0_, s32[1,96]{1,0:T(1,128)S(4)} %get-tuple-element.17.refs_1_, s32[1,1]{1,0:T(1,128)S(6)} %copy.10.refs_2_, ...), custom_call_target="tpu_custom_call" | custom-call | tf_op jit(solution)/shard_map/second_apply/pallas_call | solution.py:285
  17.1 0.2 collective-permute-start.5
  17.3 1.1 %collective-permute-done.5.refs_4_ = f32[136,128]{1,0:T(8,128)S(1)} collective-permute-done((f32[136,128]{1,0:T(8,128)S(1)}, f32[136,128]{1,0:T(8,128)S(1)}, u32[]{:S(2)}, u32[]{:S(2)}) %collective-permute-start.5) | collective-permute-done | bytes 69664 | tf_op jit(solution)/shard_map/ppermute | solution.py:222
  18.5 0.8 %collective-permute-start.6 = (f32[72,128]{1,0:T(8,128)S(1)}, f32[72,128]{1,0:T(8,128)S(1)}, u32[]{:S(2)}, u32[]{:S(2)}) collective-permute-start(f32[72,128]{1,0:T(8,128)S(1)} %pad_maximum_fusion), channel_id=1, source_target_pairs={{0,3},{1,2},{2,1},{3,0},{4,7},{5,6},{6,5},{7,4},{8,11},{9,10},{10,... | collective-permute-start | bytes 110600 | tf_op jit(solution)/shard_map/ppermute | solution.py:222
  19.3 1.9 %collective-permute-start.8 = (f32[8,128]{1,0:T(8,128)S(1)}, f32[8,128]{1,0:T(8,128)S(1)}, u32[]{:S(2)}, u32[]{:S(2)}) collective-permute-start(f32[8,128]{1,0:T(8,128)S(1)} %slice_add_fusion.2), channel_id=1, source_target_pairs={{0,7},{1,6},{2,5},{3,4},{4,3},{5,2},{6,1},{7,0},{8,15},{9,14},{10,... | collective-permute-start | bytes 12296 | tf_op jit(solution)/shard_map/ppermute | solution.py:222
  21.2 0.3 collective-permute-start.7
  21.5 1.7 %collective-permute-done.8 = f32[8,128]{1,0:T(8,128)S(1)} collective-permute-done((f32[8,128]{1,0:T(8,128)S(1)}, f32[8,128]{1,0:T(8,128)S(1)}, u32[]{:S(2)}, u32[]{:S(2)}) %collective-permute-start.8) | collective-permute-done | bytes 4128 | tf_op jit(solution)/shard_map/ppermute | solution.py:222
  23.2 1.0 %collective-permute-done.7 = f32[8,128]{1,0:T(8,128)S(1)} collective-permute-done((f32[8,128]{1,0:T(8,128)S(1)}, f32[8,128]{1,0:T(8,128)S(1)}, u32[]{:S(2)}, u32[]{:S(2)}) %collective-permute-start.7) | collective-permute-done | bytes 4128 | tf_op jit(solution)/shard_map/ppermute | solution.py:222
  24.2 0.0 collective-permute-done.6.refs_5_
  24.2 1.4 %collective-permute-start.9 = (f32[8,128]{1,0:T(8,128)S(1)}, f32[8,128]{1,0:T(8,128)S(1)}, u32[]{:S(2)}, u32[]{:S(2)}) collective-permute-start(f32[8,128]{1,0:T(8,128)S(1)} %fusion.1), channel_id=1, source_target_pairs={{0,9},{1,8},{2,11},{3,10},{4,13},{5,12},{6,15},{7,14},{8,1},{9,0},... | collective-permute-start | bytes 12296 | tf_op jit(solution)/shard_map/ppermute | solution.py:222
  25.6 1.7 %collective-permute-done.9 = f32[8,128]{1,0:T(8,128)S(1)} collective-permute-done((f32[8,128]{1,0:T(8,128)S(1)}, f32[8,128]{1,0:T(8,128)S(1)}, u32[]{:S(2)}, u32[]{:S(2)}) %collective-permute-start.9) | collective-permute-done | bytes 4128 | tf_op jit(solution)/shard_map/ppermute | solution.py:222
  27.3 2.4 %collective-permute-start.10 = (f32[8,128]{1,0:T(8,128)S(1)}, f32[8,128]{1,0:T(8,128)S(1)}, u32[]{:S(2)}, u32[]{:S(2)}) collective-permute-start(f32[8,128]{1,0:T(8,128)S(1)} %add.27.refs_6_), channel_id=1, source_target_pairs={{0,17},{1,16},{2,19},{3,18},{4,21},{5,20},{6,23},{7,22},{8,25},{9,... | collective-permute-start | bytes 12296 | tf_op jit(solution)/shard_map/ppermute | solution.py:222
  29.7 1.6 %collective-permute-done.10.refs_7_ = f32[8,128]{1,0:T(8,128)S(1)} collective-permute-done((f32[8,128]{1,0:T(8,128)S(1)}, f32[8,128]{1,0:T(8,128)S(1)}, u32[]{:S(2)}, u32[]{:S(2)}) %collective-permute-start.10) | collective-permute-done | bytes 4128 | tf_op jit(solution)/shard_map/ppermute | solution.py:222
  31.3 0.9 %last_update.1 = (f32[1,64,128]{2,1,0:T(8,128)}, f32[1,64,128]{2,1,0:T(8,128)}) custom-call(f32[1,64,128]{2,1,0:T(8,128)S(1)} %copy-done, f32[1,64,128]{2,1,0:T(8,128)S(1)} %get-tuple-element.25.refs_1_, f32[1,64,128]{2,1,0:T(8,128)S(1)} %get-tuple-element.26.refs_2_, f32[128,128]{1,0:T(8,128)S(1)} %get-tuple-element.27.refs_3_, ...), custom_call_target="tpu_custom_call" | custom-call | tf_op jit(solution)/shard_map/last_update/pallas_call | solution.py:309
  (6 shorter events, 0.0 us)
Async XLA Ops:
  0.6 5.4 %collective-permute-start.2 = (f32[1,64,128]{2,1,0:T(8,128)}, f32[1,64,128]{2,1,0:T(8,128)S(1)}, u32[]{:S(2)}, u32[]{:S(2)}) collective-permute-start(f32[1,64,128]{2,1,0:T(8,128)} %refs_0_.3), channel_id=1, source_target_pairs={{0,3},{1,2},{2,1},{3,0},{4,7},{5,6},{6,5},{7,4},{8,11},{9,10},{10,... | collective-permute-start | bytes 98312 | tf_op jit(solution)/shard_map/ppermute | solution.py:222
  3.1 4.2 %collective-permute-start.1 = (f32[1,64,128]{2,1,0:T(8,128)}, f32[1,64,128]{2,1,0:T(8,128)S(1)}, u32[]{:S(2)}, u32[]{:S(2)}) collective-permute-start(f32[1,64,128]{2,1,0:T(8,128)} %refs_0_.3), channel_id=1, source_target_pairs={{0,2},{1,3},{2,0},{3,1},{4,6},{5,7},{6,4},{7,5},{8,10},{9,11},{10,... | collective-permute-start | bytes 98312 | tf_op jit(solution)/shard_map/ppermute | solution.py:222
  3.7 3.5 %collective-permute-start = (f32[1,64,128]{2,1,0:T(8,128)}, f32[1,64,128]{2,1,0:T(8,128)S(1)}, u32[]{:S(2)}, u32[]{:S(2)}) collective-permute-start(f32[1,64,128]{2,1,0:T(8,128)} %refs_0_.3), channel_id=1, source_target_pairs={{0,1},{1,0},{2,3},{3,2},{4,5},{5,4},{6,7},{7,6},{8,9},{9,8},{10,11... | collective-permute-start | bytes 98312 | tf_op jit(solution)/shard_map/ppermute | solution.py:222
  4.4 2.9 %copy-start = (f32[1,64,128]{2,1,0:T(8,128)S(1)}, f32[1,64,128]{2,1,0:T(8,128)}, u32[]{:S(2)}) copy-start(f32[1,64,128]{2,1,0:T(8,128)} %refs_0_.3) | copy-start | bytes 98308
  9.2 1.4 %collective-permute-start.3 = (f32[4,64,128]{2,1,0:T(8,128)S(1)}, f32[4,64,128]{2,1,0:T(8,128)S(1)}, u32[]{:S(2)}, u32[]{:S(2)}) collective-permute-start(f32[4,64,128]{2,1,0:T(8,128)S(1)} %get-tuple-element.24), channel_id=1, source_target_pairs={{0,1},{1,0},{2,3},{3,2},{4,5},{5,4},{6,7},{7,6},{8,9},{9,8},{10,11... | collective-permute-start | bytes 393224 | tf_op jit(solution)/shard_map/ppermute | solution.py:222
  10.7 4.1 %collective-permute-start.4 = (bf16[4,64,128]{2,1,0:T(8,128)(2,1)S(1)}, bf16[4,64,128]{2,1,0:T(8,128)(2,1)S(1)}, u32[]{:S(2)}, u32[]{:S(2)}) collective-permute-start(bf16[4,64,128]{2,1,0:T(8,128)(2,1)S(1)} %add_convert_fusion.refs_9_), channel_id=1, source_target_pairs={{0,3},{1,2},{2,1},{3,0},{4,7},{5,6},{6,5},{7,4},{8,11},{9,10},{10,... | collective-permute-start | bytes 196616 | tf_op jit(solution)/shard_map/ppermute | solution.py:222
  17.1 1.3 %collective-permute-start.5 = (f32[136,128]{1,0:T(8,128)S(1)}, f32[136,128]{1,0:T(8,128)S(1)}, u32[]{:S(2)}, u32[]{:S(2)}) collective-permute-start(f32[136,128]{1,0:T(8,128)S(1)} %get-tuple-element.28), channel_id=1, source_target_pairs={{0,1},{1,0},{2,3},{3,2},{4,5},{5,4},{6,7},{7,6},{8,9},{9,8},{10,11... | collective-permute-start | bytes 208904 | tf_op jit(solution)/shard_map/ppermute | solution.py:222
  18.5 5.8 %collective-permute-start.6 = (f32[72,128]{1,0:T(8,128)S(1)}, f32[72,128]{1,0:T(8,128)S(1)}, u32[]{:S(2)}, u32[]{:S(2)}) collective-permute-start(f32[72,128]{1,0:T(8,128)S(1)} %pad_maximum_fusion), channel_id=1, source_target_pairs={{0,3},{1,2},{2,1},{3,0},{4,7},{5,6},{6,5},{7,4},{8,11},{9,10},{10,... | collective-permute-start | bytes 110600 | tf_op jit(solution)/shard_map/ppermute | solution.py:222
  19.3 3.9 %collective-permute-start.8 = (f32[8,128]{1,0:T(8,128)S(1)}, f32[8,128]{1,0:T(8,128)S(1)}, u32[]{:S(2)}, u32[]{:S(2)}) collective-permute-start(f32[8,128]{1,0:T(8,128)S(1)} %slice_add_fusion.2), channel_id=1, source_target_pairs={{0,7},{1,6},{2,5},{3,4},{4,3},{5,2},{6,1},{7,0},{8,15},{9,14},{10,... | collective-permute-start | bytes 12296 | tf_op jit(solution)/shard_map/ppermute | solution.py:222
  21.2 3.0 %collective-permute-start.7 = (f32[8,128]{1,0:T(8,128)S(1)}, f32[8,128]{1,0:T(8,128)S(1)}, u32[]{:S(2)}, u32[]{:S(2)}) collective-permute-start(f32[8,128]{1,0:T(8,128)S(1)} %slice_add_fusion.2), channel_id=1, source_target_pairs={{0,5},{1,4},{2,7},{3,6},{4,1},{5,0},{6,3},{7,2},{8,13},{9,12},{10,... | collective-permute-start | bytes 12296 | tf_op jit(solution)/shard_map/ppermute | solution.py:222
  24.2 3.1 %collective-permute-start.9 = (f32[8,128]{1,0:T(8,128)S(1)}, f32[8,128]{1,0:T(8,128)S(1)}, u32[]{:S(2)}, u32[]{:S(2)}) collective-permute-start(f32[8,128]{1,0:T(8,128)S(1)} %fusion.1), channel_id=1, source_target_pairs={{0,9},{1,8},{2,11},{3,10},{4,13},{5,12},{6,15},{7,14},{8,1},{9,0},... | collective-permute-start | bytes 12296 | tf_op jit(solution)/shard_map/ppermute | solution.py:222
  27.3 3.9 %collective-permute-start.10 = (f32[8,128]{1,0:T(8,128)S(1)}, f32[8,128]{1,0:T(8,128)S(1)}, u32[]{:S(2)}, u32[]{:S(2)}) collective-permute-start(f32[8,128]{1,0:T(8,128)S(1)} %add.27.refs_6_), channel_id=1, source_target_pairs={{0,17},{1,16},{2,19},{3,18},{4,21},{5,20},{6,23},{7,22},{8,25},{9,... | collective-permute-start | bytes 12296 | tf_op jit(solution)/shard_map/ppermute | solution.py:222

commit v7 on v6

--- a/solution.py
+++ b/solution.py
@@ -114,7 +114,7 @@
 def first_kernel(parts, *refs):
     users, items, count, factors, words, sym, edges, degrees = refs[:8]
     pieces = refs[8 : 8 + parts]
-    acc, start, shared = refs[8 + parts :]
+    value, start, shared, acc = refs[8 + parts :]
     me = lax.axis_index("col")
     share = pieces[0].shape[0]
     for offset in range(parts):
@@ -125,6 +125,7 @@
     acc[...] = jnp.zeros_like(acc)
     add_graph((sym, edges, degrees), shared, acc, me * share)
     add_data((users, items, count, factors, words), shared, acc)
+    value[...] = acc[...].astype(bf16)
 
 
 def second_kernel(parts, count_sums, height, *refs):
@@ -135,7 +136,8 @@
     me, row = lax.axis_index("col"), lax.axis_index("row")
     share = start.shape[0] // parts
     rhs = start[...]
-    w = sum(ref[...].astype(f32) for ref in sums) + ridge_weight * rhs
+    pairs = [near[...].astype(f32) + far[...].astype(f32) for near, far in zip(sums[::2], sums[1::2])]
+    w = sum(pairs) + ridge_weight * rhs
     a, b = total(rhs * rhs), total(rhs * w)
     step = jnp.where(b > 0.0, a / jnp.where(b > 0.0, b, 1.0), 1.0)
     step = jnp.where(step > 0.0, step, 1.0)
@@ -267,16 +269,17 @@
     whole = jax.ShapeDtypeStruct(row_shape, f32)
     value, start = pl.pallas_call(
         functools.partial(first_kernel, cols),
-        out_shape=[whole, whole],
+        out_shape=[jax.ShapeDtypeStruct(row_shape, bf16), whole],
         in_specs=cell_specs + [VMEM] * cols,
         out_specs=[VMEM] * 2,
-        scratch_shapes=[pltpu.VMEM(row_shape, bf16)],
+        scratch_shapes=[pltpu.VMEM(row_shape, bf16), pltpu.VMEM(row_shape, f32)],
         compiler_params=params,
         name="first_apply",
     )(*cell, *pieces)
-    sums = [(value + exchange(value, "col", cols, 1)).astype(bf16)]
-    for mask in even_masks(cols)[1:]:
-        sums.append(exchange(sums[0], "col", cols, mask))
+    sums = []
+    for mask in even_masks(cols):
+        near = exchange(value, "col", cols, mask) if mask else value
+        sums += [near, exchange(near, "col", cols, 1)]
 
     height = -(-rows // 8) * 8
     block = share * rank

time: 32.3 us -> 32.5 us (level)
  starting transfers between devices: 11 us -> 11.4 us
    ppermute x11 -> x12, starting transfers between devices: 11 us -> 11.4 us  [exchange(): return lax.ppermute(value, axes, [(i, i ^ offset) for i in range(size)])]
    ppermute x11 -> x12, waiting for transfers between devices: 13 us -> 12.8 us  [exchange(): return lax.ppermute(value, axes, [(i, i ^ offset) for i in range(size)])]
  transfers between devices with their start and end apart: 11 -> 12, of which waited for: 8 -> 8; matrix products, arithmetic and copies ran while one was open for 0% -> 0% of each run, Pallas kernels for 5% -> 5%
where the time goes in v7:
time: 32.5 us; the launch traced here: 32.3 us
  waiting for transfers between devices  12.8 us (39%)
  starting transfers between devices  11.4 us (35%)
  Pallas kernels  6.73 us (21%)
  between operations  1.35 us (4%)
    ppermute x12, waiting for transfers between devices, exchange(): return lax.ppermute(value, axes, [(i, i ^ offset) for i in range(size)])  12.8 us
    ppermute x12, starting transfers between devices, exchange(): return lax.ppermute(value, axes, [(i, i ^ offset) for i in range(size)])  11.4 us
    pallas_call x1, Pallas kernels, per_device(): pl.pallas_call(functools.partial(second_kernel, cols, len(sums), height),...  2.31 us
    pallas_call x1, Pallas kernels, per_device(): pl.pallas_call(functools.partial(first_kernel, cols), out_shape=[jax.Shap...  1.96 us
    pallas_call x1, Pallas kernels, per_device(): pl.pallas_call(functools.partial(prepare_kernel, cols), out_shape=[jax.Sh...  1.6 us
    pallas_call x1, Pallas kernels, per_device(): pl.pallas_call(functools.partial(last_kernel, len(images), len(tables)),...  0.85 us
  transfers between devices with their start and end apart: 12, of which 8 were waited for; matrix products, arithmetic and copies ran while one was open for 0% of the time, Pallas kernels for 5%

profile of v7, /device:TPU:0, one launch (start us, length us, event | category | flops | bytes accessed | tf_op | source)
XLA Modules:
  0.0 32.3 jit_solution(5990790225029065531)
XLA Ops:
  0.6 2.5 %collective-permute-start.2 = (f32[1,64,128]{2,1,0:T(8,128)}, f32[1,64,128]{2,1,0:T(8,128)S(1)}, u32[]{:S(2)}, u32[]{:S(2)}) collective-permute-start(f32[1,64,128]{2,1,0:T(8,128)} %refs_0_.3), channel_id=1, source_target_pairs={{0,3},{1,2},{2,1},{3,0},{4,7},{5,6},{6,5},{7,4},{8,11},{9,10},{10,... | collective-permute-start | bytes 98312 | tf_op jit(solution)/shard_map/ppermute | solution.py:224
  3.1 0.6 %collective-permute-start.1 = (f32[1,64,128]{2,1,0:T(8,128)}, f32[1,64,128]{2,1,0:T(8,128)S(1)}, u32[]{:S(2)}, u32[]{:S(2)}) collective-permute-start(f32[1,64,128]{2,1,0:T(8,128)} %refs_0_.3), channel_id=1, source_target_pairs={{0,2},{1,3},{2,0},{3,1},{4,6},{5,7},{6,4},{7,5},{8,10},{9,11},{10,... | collective-permute-start | bytes 98312 | tf_op jit(solution)/shard_map/ppermute | solution.py:224
  3.7 0.0 collective-permute-start
  4.4 0.0 copy-start
  4.4 1.6 %prepare.1 = (bf16[64,64,128]{2,1,0:T(8,128)(2,1)S(1)}, s32[96,16,128]{2,1,0:T(8,128)S(1)}, s32[1,96]{1,0:T(1,128)S(4)}, s32[1,96]{1,0:T(1,128)S(4)}, bf16[1,128...) custom-call(bf16[64,64,128]{2,1,0:T(8,128)(2,1)} %refs_0_.2, ...), custom_call_target="tpu_custom_call" | custom-call | flops 1000000 | bytes 4000000 | tf_op jit(solution)/shard_map/prepare/pallas_call | solution.py:248
  6.1 0.0 collective-permute-done.2.refs_11_
  6.1 1.2 %collective-permute-done.1.refs_10_ = f32[1,64,128]{2,1,0:T(8,128)S(1)} collective-permute-done((f32[1,64,128]{2,1,0:T(8,128)}, f32[1,64,128]{2,1,0:T(8,128)S(1)}, u32[]{:S(2)}, u32[]{:S(2)}) %collective-permute-start.1) | collective-permute-done | bytes 32800 | tf_op jit(solution)/shard_map/ppermute | solution.py:224
  7.3 0.0 collective-permute-done.refs_9_
  7.3 0.0 copy-done
  7.3 2.0 %first_apply.1 = (bf16[4,64,128]{2,1,0:T(8,128)(2,1)S(1)}, f32[4,64,128]{2,1,0:T(8,128)S(1)}) custom-call(s32[1,96]{1,0:T(1,128)S(4)} %get-tuple-element.16.refs_0_, s32[1,96]{1,0:T(1,128)S(4)} %get-tuple-element.17.refs_1_, s32[1,1]{1,0:T(1,128)S(6)} %copy.10.refs_2_, bf16[64,64,128]{2,1,0:T(8,128)(2,1)S(1)} %get-tuple-element.18.refs_3_, ...), custom_call_target="tpu_custom_call" | custom-call | tf_op jit(solution)/shard_map/first_apply/pallas_call | solution.py:270
  9.3 0.8 %collective-permute-start.4 = (bf16[4,64,128]{2,1,0:T(8,128)(2,1)S(1)}, bf16[4,64,128]{2,1,0:T(8,128)(2,1)S(1)}, u32[]{:S(2)}, u32[]{:S(2)}) collective-permute-start(bf16[4,64,128]{2,1,0:T(8,128)(2,1)S(1)} %get-tuple-element.24.refs_9_), channel_id=1, source_target_pairs={{0,3},{1,2},{2,1},{3,0},{4,7},{5,6},{6,5},{7,4},{8,11},{9,10},{10,... | collective-permute-start | bytes 196616 | tf_op jit(solution)/shard_map/ppermute | solution.py:224
  10.0 0.4 %collective-permute-start.3 = (bf16[4,64,128]{2,1,0:T(8,128)(2,1)S(1)}, bf16[4,64,128]{2,1,0:T(8,128)(2,1)S(1)}, u32[]{:S(2)}, u32[]{:S(2)}) collective-permute-start(bf16[4,64,128]{2,1,0:T(8,128)(2,1)S(1)} %get-tuple-element.24.refs_9_), channel_id=1, source_target_pairs={{0,1},{1,0},{2,3},{3,2},{4,5},{5,4},{6,7},{7,6},{8,9},{9,8},{10,11... | collective-permute-start | bytes 196616 | tf_op jit(solution)/shard_map/ppermute | solution.py:224
  10.4 3.3 %collective-permute-done.4.refs_11_ = bf16[4,64,128]{2,1,0:T(8,128)(2,1)S(1)} collective-permute-done((bf16[4,64,128]{2,1,0:T(8,128)(2,1)S(1)}, bf16[4,64,128]{2,1,0:T(8,128)(2,1)S(1)}, u32[]{:S(2)}, u32[]{:S(2)}) %collective-permute-start.4) | collective-permute-done | bytes 65568 | tf_op jit(solution)/shard_map/ppermute | solution.py:224
  13.7 0.1 collective-permute-start.5
  13.8 0.0 collective-permute-done.3.refs_10_
  13.8 1.1 %collective-permute-done.5.refs_12_ = bf16[4,64,128]{2,1,0:T(8,128)(2,1)S(1)} collective-permute-done((bf16[4,64,128]{2,1,0:T(8,128)(2,1)S(1)}, bf16[4,64,128]{2,1,0:T(8,128)(2,1)S(1)}, u32[]{:S(2)}, u32[]{:S(2)}) %collective-permute-start.5) | collective-permute-done | bytes 65568 | tf_op jit(solution)/shard_map/ppermute | solution.py:224
  15.0 2.3 %second_apply.1 = (f32[128,128]{1,0:T(8,128)S(1)}, f32[136,128]{1,0:T(8,128)S(1)}, f32[8,128]{1,0:T(8,128)S(1)}, f32[1,64,128]{2,1,0:T(8,128)S(1)}, f32[1,64,128]{2,1,0:T(8,128)S(1)}) custom-call(s32[1,96]{1,0:T(1,128)S(4)} %get-tuple-element.16.refs_0_, s32[1,96]{1,0:T(1,128)S(4)} %get-tuple-element.17.refs_1_, s32[1,1]{1,0:T(1,128)S(6)} %copy.10.refs_2_, ...), custom_call_target="tpu_custom_call" | custom-call | tf_op jit(solution)/shard_map/second_apply/pallas_call | solution.py:288
  17.3 0.2 collective-permute-start.6
  17.5 1.1 %collective-permute-done.6.refs_4_ = f32[136,128]{1,0:T(8,128)S(1)} collective-permute-done((f32[136,128]{1,0:T(8,128)S(1)}, f32[136,128]{1,0:T(8,128)S(1)}, u32[]{:S(2)}, u32[]{:S(2)}) %collective-permute-start.6) | collective-permute-done | bytes 69664 | tf_op jit(solution)/shard_map/ppermute | solution.py:224
  18.6 0.5 %collective-permute-start.7 = (f32[72,128]{1,0:T(8,128)S(1)}, f32[72,128]{1,0:T(8,128)S(1)}, u32[]{:S(2)}, u32[]{:S(2)}) collective-permute-start(f32[72,128]{1,0:T(8,128)S(1)} %pad_maximum_fusion), channel_id=1, source_target_pairs={{0,3},{1,2},{2,1},{3,0},{4,7},{5,6},{6,5},{7,4},{8,11},{9,10},{10,... | collective-permute-start | bytes 110600 | tf_op jit(solution)/shard_map/ppermute | solution.py:224
  19.2 2.2 %collective-permute-start.9 = (f32[8,128]{1,0:T(8,128)S(1)}, f32[8,128]{1,0:T(8,128)S(1)}, u32[]{:S(2)}, u32[]{:S(2)}) collective-permute-start(f32[8,128]{1,0:T(8,128)S(1)} %slice_add_fusion.2), channel_id=1, source_target_pairs={{0,7},{1,6},{2,5},{3,4},{4,3},{5,2},{6,1},{7,0},{8,15},{9,14},{10,... | collective-permute-start | bytes 12296 | tf_op jit(solution)/shard_map/ppermute | solution.py:224
  21.4 0.3 collective-permute-start.8
  21.7 1.4 %collective-permute-done.9 = f32[8,128]{1,0:T(8,128)S(1)} collective-permute-done((f32[8,128]{1,0:T(8,128)S(1)}, f32[8,128]{1,0:T(8,128)S(1)}, u32[]{:S(2)}, u32[]{:S(2)}) %collective-permute-start.9) | collective-permute-done | bytes 4128 | tf_op jit(solution)/shard_map/ppermute | solution.py:224
  23.1 1.3 %collective-permute-done.8 = f32[8,128]{1,0:T(8,128)S(1)} collective-permute-done((f32[8,128]{1,0:T(8,128)S(1)}, f32[8,128]{1,0:T(8,128)S(1)}, u32[]{:S(2)}, u32[]{:S(2)}) %collective-permute-start.8) | collective-permute-done | bytes 4128 | tf_op jit(solution)/shard_map/ppermute | solution.py:224
  24.4 0.0 collective-permute-done.7.refs_5_
  24.4 1.4 %collective-permute-start.10 = (f32[8,128]{1,0:T(8,128)S(1)}, f32[8,128]{1,0:T(8,128)S(1)}, u32[]{:S(2)}, u32[]{:S(2)}) collective-permute-start(f32[8,128]{1,0:T(8,128)S(1)} %fusion.1), channel_id=1, source_target_pairs={{0,9},{1,8},{2,11},{3,10},{4,13},{5,12},{6,15},{7,14},{8,1},{9,0},... | collective-permute-start | bytes 12296 | tf_op jit(solution)/shard_map/ppermute | solution.py:224
  25.8 1.7 %collective-permute-done.10 = f32[8,128]{1,0:T(8,128)S(1)} collective-permute-done((f32[8,128]{1,0:T(8,128)S(1)}, f32[8,128]{1,0:T(8,128)S(1)}, u32[]{:S(2)}, u32[]{:S(2)}) %collective-permute-start.10) | collective-permute-done | bytes 4128 | tf_op jit(solution)/shard_map/ppermute | solution.py:224
  27.5 2.4 %collective-permute-start.11 = (f32[8,128]{1,0:T(8,128)S(1)}, f32[8,128]{1,0:T(8,128)S(1)}, u32[]{:S(2)}, u32[]{:S(2)}) collective-permute-start(f32[8,128]{1,0:T(8,128)S(1)} %add.23.refs_6_), channel_id=1, source_target_pairs={{0,17},{1,16},{2,19},{3,18},{4,21},{5,20},{6,23},{7,22},{8,25},{9,... | collective-permute-start | bytes 12296 | tf_op jit(solution)/shard_map/ppermute | solution.py:224
  29.9 1.6 %collective-permute-done.11.refs_7_ = f32[8,128]{1,0:T(8,128)S(1)} collective-permute-done((f32[8,128]{1,0:T(8,128)S(1)}, f32[8,128]{1,0:T(8,128)S(1)}, u32[]{:S(2)}, u32[]{:S(2)}) %collective-permute-start.11) | collective-permute-done | bytes 4128 | tf_op jit(solution)/shard_map/ppermute | solution.py:224
  31.5 0.9 %last_update.1 = (f32[1,64,128]{2,1,0:T(8,128)}, f32[1,64,128]{2,1,0:T(8,128)}) custom-call(f32[1,64,128]{2,1,0:T(8,128)S(1)} %copy-done, f32[1,64,128]{2,1,0:T(8,128)S(1)} %get-tuple-element.25.refs_1_, f32[1,64,128]{2,1,0:T(8,128)S(1)} %get-tuple-element.26.refs_2_, f32[128,128]{1,0:T(8,128)S(1)} %get-tuple-element.27.refs_3_, ...), custom_call_target="tpu_custom_call" | custom-call | tf_op jit(solution)/shard_map/last_update/pallas_call | solution.py:312
  (5 shorter events, 0.0 us)
Async XLA Ops:
  0.6 5.4 %collective-permute-start.2 = (f32[1,64,128]{2,1,0:T(8,128)}, f32[1,64,128]{2,1,0:T(8,128)S(1)}, u32[]{:S(2)}, u32[]{:S(2)}) collective-permute-start(f32[1,64,128]{2,1,0:T(8,128)} %refs_0_.3), channel_id=1, source_target_pairs={{0,3},{1,2},{2,1},{3,0},{4,7},{5,6},{6,5},{7,4},{8,11},{9,10},{10,... | collective-permute-start | bytes 98312 | tf_op jit(solution)/shard_map/ppermute | solution.py:224
  3.1 4.2 %collective-permute-start.1 = (f32[1,64,128]{2,1,0:T(8,128)}, f32[1,64,128]{2,1,0:T(8,128)S(1)}, u32[]{:S(2)}, u32[]{:S(2)}) collective-permute-start(f32[1,64,128]{2,1,0:T(8,128)} %refs_0_.3), channel_id=1, source_target_pairs={{0,2},{1,3},{2,0},{3,1},{4,6},{5,7},{6,4},{7,5},{8,10},{9,11},{10,... | collective-permute-start | bytes 98312 | tf_op jit(solution)/shard_map/ppermute | solution.py:224
  3.7 3.5 %collective-permute-start = (f32[1,64,128]{2,1,0:T(8,128)}, f32[1,64,128]{2,1,0:T(8,128)S(1)}, u32[]{:S(2)}, u32[]{:S(2)}) collective-permute-start(f32[1,64,128]{2,1,0:T(8,128)} %refs_0_.3), channel_id=1, source_target_pairs={{0,1},{1,0},{2,3},{3,2},{4,5},{5,4},{6,7},{7,6},{8,9},{9,8},{10,11... | collective-permute-start | bytes 98312 | tf_op jit(solution)/shard_map/ppermute | solution.py:224
  4.4 2.9 %copy-start = (f32[1,64,128]{2,1,0:T(8,128)S(1)}, f32[1,64,128]{2,1,0:T(8,128)}, u32[]{:S(2)}) copy-start(f32[1,64,128]{2,1,0:T(8,128)} %refs_0_.3) | copy-start | bytes 98308
  9.3 4.5 %collective-permute-start.4 = (bf16[4,64,128]{2,1,0:T(8,128)(2,1)S(1)}, bf16[4,64,128]{2,1,0:T(8,128)(2,1)S(1)}, u32[]{:S(2)}, u32[]{:S(2)}) collective-permute-start(bf16[4,64,128]{2,1,0:T(8,128)(2,1)S(1)} %get-tuple-element.24.refs_9_), channel_id=1, source_target_pairs={{0,3},{1,2},{2,1},{3,0},{4,7},{5,6},{6,5},{7,4},{8,11},{9,10},{10,... | collective-permute-start | bytes 196616 | tf_op jit(solution)/shard_map/ppermute | solution.py:224
  10.0 3.8 %collective-permute-start.3 = (bf16[4,64,128]{2,1,0:T(8,128)(2,1)S(1)}, bf16[4,64,128]{2,1,0:T(8,128)(2,1)S(1)}, u32[]{:S(2)}, u32[]{:S(2)}) collective-permute-start(bf16[4,64,128]{2,1,0:T(8,128)(2,1)S(1)} %get-tuple-element.24.refs_9_), channel_id=1, source_target_pairs={{0,1},{1,0},{2,3},{3,2},{4,5},{5,4},{6,7},{7,6},{8,9},{9,8},{10,11... | collective-permute-start | bytes 196616 | tf_op jit(solution)/shard_map/ppermute | solution.py:224
  13.7 1.3 %collective-permute-start.5 = (bf16[4,64,128]{2,1,0:T(8,128)(2,1)S(1)}, bf16[4,64,128]{2,1,0:T(8,128)(2,1)S(1)}, u32[]{:S(2)}, u32[]{:S(2)}) collective-permute-start(bf16[4,64,128]{2,1,0:T(8,128)(2,1)S(1)} %collective-permute-done.4.refs_11_), channel_id=1, source_target_pairs={{0,1},{1,0},{2,3},{3,2},{4,5},{5,4},{6,7},{7,6},{8,9},{9,8},{10,11... | collective-permute-start | bytes 196616 | tf_op jit(solution)/shard_map/ppermute | solution.py:224
  17.3 1.3 %collective-permute-start.6 = (f32[136,128]{1,0:T(8,128)S(1)}, f32[136,128]{1,0:T(8,128)S(1)}, u32[]{:S(2)}, u32[]{:S(2)}) collective-permute-start(f32[136,128]{1,0:T(8,128)S(1)} %get-tuple-element.28), channel_id=1, source_target_pairs={{0,1},{1,0},{2,3},{3,2},{4,5},{5,4},{6,7},{7,6},{8,9},{9,8},{10,11... | collective-permute-start | bytes 208904 | tf_op jit(solution)/shard_map/ppermute | solution.py:224
  18.6 5.8 %collective-permute-start.7 = (f32[72,128]{1,0:T(8,128)S(1)}, f32[72,128]{1,0:T(8,128)S(1)}, u32[]{:S(2)}, u32[]{:S(2)}) collective-permute-start(f32[72,128]{1,0:T(8,128)S(1)} %pad_maximum_fusion), channel_id=1, source_target_pairs={{0,3},{1,2},{2,1},{3,0},{4,7},{5,6},{6,5},{7,4},{8,11},{9,10},{10,... | collective-permute-start | bytes 110600 | tf_op jit(solution)/shard_map/ppermute | solution.py:224
  19.2 3.9 %collective-permute-start.9 = (f32[8,128]{1,0:T(8,128)S(1)}, f32[8,128]{1,0:T(8,128)S(1)}, u32[]{:S(2)}, u32[]{:S(2)}) collective-permute-start(f32[8,128]{1,0:T(8,128)S(1)} %slice_add_fusion.2), channel_id=1, source_target_pairs={{0,7},{1,6},{2,5},{3,4},{4,3},{5,2},{6,1},{7,0},{8,15},{9,14},{10,... | collective-permute-start | bytes 12296 | tf_op jit(solution)/shard_map/ppermute | solution.py:224
  21.4 3.0 %collective-permute-start.8 = (f32[8,128]{1,0:T(8,128)S(1)}, f32[8,128]{1,0:T(8,128)S(1)}, u32[]{:S(2)}, u32[]{:S(2)}) collective-permute-start(f32[8,128]{1,0:T(8,128)S(1)} %slice_add_fusion.2), channel_id=1, source_target_pairs={{0,5},{1,4},{2,7},{3,6},{4,1},{5,0},{6,3},{7,2},{8,13},{9,12},{10,... | collective-permute-start | bytes 12296 | tf_op jit(solution)/shard_map/ppermute | solution.py:224
  24.4 3.1 %collective-permute-start.10 = (f32[8,128]{1,0:T(8,128)S(1)}, f32[8,128]{1,0:T(8,128)S(1)}, u32[]{:S(2)}, u32[]{:S(2)}) collective-permute-start(f32[8,128]{1,0:T(8,128)S(1)} %fusion.1), channel_id=1, source_target_pairs={{0,9},{1,8},{2,11},{3,10},{4,13},{5,12},{6,15},{7,14},{8,1},{9,0},... | collective-permute-start | bytes 12296 | tf_op jit(solution)/shard_map/ppermute | solution.py:224
  27.5 3.9 %collective-permute-start.11 = (f32[8,128]{1,0:T(8,128)S(1)}, f32[8,128]{1,0:T(8,128)S(1)}, u32[]{:S(2)}, u32[]{:S(2)}) collective-permute-start(f32[8,128]{1,0:T(8,128)S(1)} %add.23.refs_6_), channel_id=1, source_target_pairs={{0,17},{1,16},{2,19},{3,18},{4,21},{5,20},{6,23},{7,22},{8,25},{9,... | collective-permute-start | bytes 12296 | tf_op jit(solution)/shard_map/ppermute | solution.py:224
